TPU v7x, 512 devices: a whole 4x8x8 slice. The times are simulated.
512 devices in a mesh: rep: 32 (over z_hi, y, core), shard: 16 (over z_lo, x).
Axes of the slice: x: 4, y: 8, z: 8 (z_hi: 2, z_lo: 4; z = z_hi * 4 + z_lo), core: 2. Of those that a mesh axis runs over, the one named last changes fastest.
Arguments:
- queries: bfloat16 [65536, 4096], P(('rep', 'shard')), may hold values from -120 to 120
- keys: bfloat16 [65536, 512], P(('rep', 'shard')), may hold values from -5.5 to 5.5
- grad_out: bfloat16 [65536, 4096], P(('rep', 'shard')), may hold values from -0.75 to 0.75
- inputs: bfloat16 [65536, 8192], P(('rep', 'shard')), may hold values from -6 to 6
- old_owner: int32 [64], replicated, may hold values from 0 to 11, as said below
- new_owner: int32 [64], replicated, may hold values from 0 to 15, as said below
- param_old: float32 [128, 96, 512], P('rep', 'shard'), may hold values from -0.75 to 0.75
- first_old: float32 [128, 96, 512], P('rep', 'shard'), may hold values from -6 to 6
- second_old: float32 [128, 96, 512], P('rep', 'shard'), may hold values from 0.5 to 20
Outputs:
- param_new: float32 [128, 64, 512], P('rep', 'shard')
- first_new: float32 [128, 64, 512], P('rep', 'shard')
- second_new: float32 [128, 64, 512], P('rep', 'shard')
- weights: bfloat16 [128, 64, 512], P('rep')
Inputs may be any that keep to these rules, and one draw needn't show every extreme that they name: `old_owner`: each old owner holds at most 6 blocks, and some hold exactly 6. `new_owner`: each new owner holds exactly 4 blocks.
All inputs are finite; a program needn't handle non-finite values.
Results may differ from a plain program's by a relative error of at most 0.0034.
Values may be sent and summed in bfloat16 or wider, within the bound.
No kernel may reach another device: no remote copies, remote signals or barrier semaphores. Data moves between devices by JAX's collectives and lax.ppermute only.
A program may use at most 128 MiB of HBM per device.

v0:
```python
import jax
import jax.numpy as jnp
from jax import lax
from jax.sharding import PartitionSpec as P

KV = 4
HD = 128
GRP = 8
STEP = 1000


beta_first = 0.9
beta_second = 0.95
learning_rate = 0.02
decay_rate = 0.1
epsilon = 1e-08


def laid_out(parts, dim):
    shape = list(parts.shape[1:])
    shape[dim] *= parts.shape[0]
    return jnp.moveaxis(parts, 0, dim).reshape(shape)


def from_everyone(x, axis):
    copies = jnp.broadcast_to(x, (lax.axis_size(axis), *x.shape))
    return lax.all_to_all(copies, axis, split_axis=0, concat_axis=0, tiled=True)


def collect(x, axis, dim):
    return laid_out(from_everyone(x, axis), dim)


def split_up(x, dim, devices):
    shape = x.shape
    parts = x.reshape(*shape[:dim], devices, shape[dim] // devices, *shape[dim + 1 :])
    return jnp.moveaxis(parts, dim, 0)


def sent_and_summed(x, axis, dim):
    parts = split_up(x, dim, lax.axis_size(axis))
    arrived = lax.all_to_all(parts, axis, split_axis=0, concat_axis=0, tiled=True)
    return arrived.sum(axis=0)


def owner_ranks(owner, owners):
    onehot = (owner[:, None] == jnp.arange(owners, dtype=jnp.int32)[None, :]).astype(jnp.int32)
    running = jnp.cumsum(onehot, axis=0)
    return jnp.sum(running * onehot, axis=1) - 1


def slot_table(owner, owners, capacity):
    blocks = owner.shape[0]
    position = owner * capacity + owner_ranks(owner, owners)
    match = position[None, :] == jnp.arange(owners * capacity, dtype=jnp.int32)[:, None]
    chosen = jnp.sum(jnp.where(match, jnp.arange(blocks, dtype=jnp.int32)[None, :], 0), axis=1)
    return (chosen, jnp.any(match, axis=1))


def adamw(param, first, second, gradient):
    first = beta_first * first + (1.0 - beta_first) * gradient
    second = beta_second * second + (1.0 - beta_second) * gradient * gradient
    first_hat = first / (1.0 - beta_first**STEP)
    second_hat = second / (1.0 - beta_second**STEP)
    param = param - learning_rate * (
        first_hat / (jnp.sqrt(second_hat) + epsilon) + decay_rate * param
    )
    return (param, first, second)


def value_terms(queries, keys_all, grad_out, offset):
    rows_here = queries.shape[0]
    length = keys_all.shape[0]
    query_groups = queries.reshape(rows_here, KV, GRP, HD).transpose(1, 2, 0, 3)
    cotangent_groups = grad_out.reshape(rows_here, KV, GRP, HD).transpose(1, 2, 0, 3)
    key_groups = keys_all.reshape(length, KV, HD).transpose(1, 0, 2)
    allowed = jnp.arange(length)[None, :] <= (offset + jnp.arange(rows_here))[:, None]

    def one_group(triple):
        query_block, key_block, cotangent = triple
        scores = jnp.einsum(
            "htd,ud->htu", query_block, key_block, preferred_element_type=jnp.float32
        ) * HD ** (-0.5)
        scores = jnp.where(allowed[None], scores, -jnp.inf)
        highest = jnp.max(scores, axis=-1, keepdims=True)
        weights = jnp.exp(scores - highest)
        probs = (weights / jnp.sum(weights, axis=-1, keepdims=True)).astype(jnp.bfloat16)
        return jnp.einsum("htu,htd->ud", probs, cotangent, preferred_element_type=jnp.float32)

    return lax.map(one_group, (query_groups, key_groups, cotangent_groups))


def local(queries, keys, grad_out, inputs, old_owner, new_owner, param_old, first_old, second_old):
    shards = lax.axis_size("shard")
    replicas = lax.axis_size("rep")
    shard_index = lax.axis_index("shard")
    rows_here = queries.shape[0]
    blocks = old_owner.shape[0]
    block_rows = inputs.shape[1] // blocks
    new_capacity = blocks // shards
    columns = KV * HD
    keys_all = collect(keys, "shard", 0)
    value_part = value_terms(queries, keys_all, grad_out, shard_index * rows_here)
    values = lax.psum(value_part, "shard").astype(jnp.bfloat16)
    slot_block, slot_valid = slot_table(new_owner, shards, new_capacity)
    pieces = inputs.reshape(rows_here, blocks, block_rows)
    outgoing = jnp.where(
        slot_valid[None, :, None], jnp.take(pieces, slot_block, axis=1), jnp.zeros((), jnp.bfloat16)
    )
    arrived = lax.all_to_all(outgoing, "shard", split_axis=1, concat_axis=0, tiled=True)
    product = jnp.einsum("tsk,gtd->ksgd", arrived, values, preferred_element_type=jnp.float32)
    gradient = sent_and_summed(
        product.reshape(block_rows // replicas * lax.axis_size("rep"), new_capacity, columns),
        "rep",
        0,
    )
    new_block, unused_valid = slot_table(new_owner, shards, new_capacity)
    old_rank = owner_ranks(old_owner, shards)
    source_slot = jnp.take(old_rank, new_block)
    keeping = jnp.take(old_owner, new_block) == shard_index
    sent_param = jnp.where(keeping[None, :, None], jnp.take(param_old, source_slot, axis=1), 0.0)
    sent_first = jnp.where(keeping[None, :, None], jnp.take(first_old, source_slot, axis=1), 0.0)
    sent_second = jnp.where(keeping[None, :, None], jnp.take(second_old, source_slot, axis=1), 0.0)
    received = (
        lax.all_to_all(sent_param, "shard", split_axis=1, concat_axis=0, tiled=True),
        lax.all_to_all(sent_first, "shard", split_axis=1, concat_axis=0, tiled=True),
        lax.all_to_all(sent_second, "shard", split_axis=1, concat_axis=0, tiled=True),
    )
    moved = tuple(
        (jnp.sum(state.reshape(shards, -1, new_capacity, columns), axis=0) for state in received)
    )
    param_new, first_new, second_new = adamw(moved[0], moved[1], moved[2], gradient)
    working = param_new.astype(jnp.bfloat16)
    every_shard = collect(working, "shard", 1)
    new_slot = new_owner * new_capacity + owner_ranks(new_owner, shards)
    weights = jnp.take(every_shard, new_slot, axis=1)
    return (param_new, first_new, second_new, weights)


def solution(mesh):
    placed = (
        P(("rep", "shard"), None),
        P(("rep", "shard"), None),
        P(("rep", "shard"), None),
        P(("rep", "shard"), None),
        P(),
        P(),
        P("rep", "shard", None),
        P("rep", "shard", None),
        P("rep", "shard", None),
    )
    return jax.shard_map(
        local,
        mesh=mesh,
        in_specs=placed,
        out_specs=(
            P("rep", "shard", None),
            P("rep", "shard", None),
            P("rep", "shard", None),
            P("rep", None, None),
        ),
        check_vma=False,
    )
```

profile of v0, /device:TPU:1, one launch (start us, length us, event | category | flops | bytes accessed | tf_op | source)
XLA Modules:
  0.0 356.6 jit_solution(8832650210763158937)
XLA Ops:
  3.9 1.4 gather_fusion.2
  9.7 1.6 bitcast_select_fusion.1
  11.4 10.4 %all-to-all-start = ((f32[4,64,512]{2,0,1:T(4,128)}), f32[4,64,512]{2,0,1:T(4,128)S(1)}, u32[]{:S(2)}, u32[]{:S(2)}) async-start(f32[4,64,512]{2,0,1:T(4,128)} %get-tuple-element.130), calls=%async_computation | async-start | bytes 1048576 | tf_op jit(solution)/shard_map/all_to_all | solution.py:125
  21.9 13.6 %all-to-all-done = f32[4,64,512]{2,0,1:T(4,128)S(1)} async-done(((f32[4,64,512]{2,0,1:T(4,128)}), f32[4,64,512]{2,0,1:T(4,128)S(1)}, u32[]{:S(2)}, u32[]{:S(2)}) %all-to-all-start) | async-done | bytes 524320 | tf_op jit(solution)/shard_map/all_to_all | solution.py:125
  36.0 52.6 %all_to_all.69 = bf16[16,128,512]{1,2,0:T(8,128)(2,1)} all-to-all(bf16[16,128,512]{1,2,0:T(8,128)(2,1)S(1)} %broadcast_in_dim.138), channel_id=1, replica_groups=mesh['rep'=32,'shard'=16] {'shard'}, dimensions={0} | all-to-all | bytes 4194304 | tf_op jit(solution)/shard_map/all_to_all | solution.py:27
  88.6 5.0 %all-to-all-start.1 = ((f32[4,64,512]{2,0,1:T(4,128)}), f32[4,64,512]{2,0,1:T(4,128)S(1)}, u32[]{:S(2)}, u32[]{:S(2)}) async-start(f32[4,64,512]{2,0,1:T(4,128)} %get-tuple-element.128), calls=%async_computation.1 | async-start | bytes 1048576 | tf_op jit(solution)/shard_map/all_to_all | solution.py:126
  93.6 3.2 copy.87
  96.8 2.9 copy.88
  99.7 2.4 copy.79
  102.1 1.3 copy.82
  103.5 2.5 gather_fusion
  106.1 1.7 select_bitcast_fusion
  108.4 1.4 copy.81
  109.8 2.3 reshape_reshape.6
  112.1 6.9 %all-to-all-start.3 = ((bf16[128,64,128]{2,0,1:T(8,128)(2,1)}), bf16[128,64,128]{2,0,1:T(8,128)(2,1)S(1)}, u32[]{:S(2)}, u32[]{:S(2)}) async-start(bf16[128,64,128]{2,0,1:T(8,128)(2,1)} %select_bitcast_fusion), calls=%async_computation.3 | async-start | bytes 4194304 | tf_op jit(solution)/shard_map/all_to_all | solution.py:110
  119.1 51.1 %while.11 = (s32[]{:T(128)}, f32[4,2048,128]{1,2,0:T(8,128)}, bf16[4,8,128,128]{2,3,1,0:T(8,128)(2,1)}, bf16[4,2048,128]{1,2,0:T(8,128)(2,1)}, bf16[4,8,128,128]...) while((s32[]{:T(128)}, f32[4,2048,128]{1,2,0:T(8,128)}, bf16[4,8,128,128]{2,3,1,0:T(8,128)(2,1)}, ...), condition=%wide.region_10.13_spmd.clone, body=%wide.region_7.12_spmd.clone.sunk | while | flops 1086588928 | bytes 19409484 | solution.py:90
  119.3 7.3 %fusion.71 = (f32[8,128]{1,0:T(8,128)S(1)}, f32[8,128,2048]{2,1,0:T(8,128)}) fusion(pred[128,2048]{1,0:T(8,128)(4,1)S(1)} %iota_compare_fusion.5, bf16[4,2048,128]{1,2,0:T(8,128)(2,1)} %get-tuple-element.189, s32[]{:T(128)} %get-tuple-element.179, bf16[4,8,128,128]{2,3,1,0:T(8,128)(2,1)} %get-tuple-element.188), kind=kOutput, calls=%fused_computation.76.clone.1 | convolution fusion | flops 545261568 | bytes 9442304 | tf_op jit(solution)/shard_map/while/body/eval_jaxpr/sub | solution.py:86
  126.6 5.4 %fusion.72 = f32[4,2048,128]{1,2,0:T(8,128)} fusion(f32[4,2048,128]{1,2,0:T(8,128)} %get-tuple-element.180, s32[]{:T(128)} %get-tuple-element.179, f32[8,128,2048]{2,1,0:T(8,128)} %get-tuple-element.170, f32[8,128]{1,0:T(8,128)S(1)} %get-tuple-element.171, bf16[4,8,128,128]{2,3,1,0:T(8,128)(2,1)} %get-tuple-element.190), kind=kOutput, calls=%fused_computation.18.clone.1 | convolution fusion | flops 541065216 | bytes 9704448 | tf_op jit(solution)/shard_map/while/body/eval_jaxpr/htu,htd->ud/dot_general | solution.py:88
  132.2 7.3 %fusion.71 = (f32[8,128]{1,0:T(8,128)S(1)}, f32[8,128,2048]{2,1,0:T(8,128)}) fusion(pred[128,2048]{1,0:T(8,128)(4,1)S(1)} %iota_compare_fusion.5, bf16[4,2048,128]{1,2,0:T(8,128)(2,1)} %get-tuple-element.189, s32[]{:T(128)} %get-tuple-element.179, bf16[4,8,128,128]{2,3,1,0:T(8,128)(2,1)} %get-tuple-element.188), kind=kOutput, calls=%fused_computation.76.clone.1 | convolution fusion | flops 545261568 | bytes 9442304 | tf_op jit(solution)/shard_map/while/body/eval_jaxpr/sub | solution.py:86
  139.4 5.3 %fusion.72 = f32[4,2048,128]{1,2,0:T(8,128)} fusion(f32[4,2048,128]{1,2,0:T(8,128)} %get-tuple-element.180, s32[]{:T(128)} %get-tuple-element.179, f32[8,128,2048]{2,1,0:T(8,128)} %get-tuple-element.170, f32[8,128]{1,0:T(8,128)S(1)} %get-tuple-element.171, bf16[4,8,128,128]{2,3,1,0:T(8,128)(2,1)} %get-tuple-element.190), kind=kOutput, calls=%fused_computation.18.clone.1 | convolution fusion | flops 541065216 | bytes 9704448 | tf_op jit(solution)/shard_map/while/body/eval_jaxpr/htu,htd->ud/dot_general | solution.py:88
  144.9 7.3 %fusion.71 = (f32[8,128]{1,0:T(8,128)S(1)}, f32[8,128,2048]{2,1,0:T(8,128)}) fusion(pred[128,2048]{1,0:T(8,128)(4,1)S(1)} %iota_compare_fusion.5, bf16[4,2048,128]{1,2,0:T(8,128)(2,1)} %get-tuple-element.189, s32[]{:T(128)} %get-tuple-element.179, bf16[4,8,128,128]{2,3,1,0:T(8,128)(2,1)} %get-tuple-element.188), kind=kOutput, calls=%fused_computation.76.clone.1 | convolution fusion | flops 545261568 | bytes 9442304 | tf_op jit(solution)/shard_map/while/body/eval_jaxpr/sub | solution.py:86
  152.2 5.3 %fusion.72 = f32[4,2048,128]{1,2,0:T(8,128)} fusion(f32[4,2048,128]{1,2,0:T(8,128)} %get-tuple-element.180, s32[]{:T(128)} %get-tuple-element.179, f32[8,128,2048]{2,1,0:T(8,128)} %get-tuple-element.170, f32[8,128]{1,0:T(8,128)S(1)} %get-tuple-element.171, bf16[4,8,128,128]{2,3,1,0:T(8,128)(2,1)} %get-tuple-element.190), kind=kOutput, calls=%fused_computation.18.clone.1 | convolution fusion | flops 541065216 | bytes 9704448 | tf_op jit(solution)/shard_map/while/body/eval_jaxpr/htu,htd->ud/dot_general | solution.py:88
  157.7 7.3 %fusion.71 = (f32[8,128]{1,0:T(8,128)S(1)}, f32[8,128,2048]{2,1,0:T(8,128)}) fusion(pred[128,2048]{1,0:T(8,128)(4,1)S(1)} %iota_compare_fusion.5, bf16[4,2048,128]{1,2,0:T(8,128)(2,1)} %get-tuple-element.189, s32[]{:T(128)} %get-tuple-element.179, bf16[4,8,128,128]{2,3,1,0:T(8,128)(2,1)} %get-tuple-element.188), kind=kOutput, calls=%fused_computation.76.clone.1 | convolution fusion | flops 545261568 | bytes 9442304 | tf_op jit(solution)/shard_map/while/body/eval_jaxpr/sub | solution.py:86
  164.9 5.3 %fusion.72 = f32[4,2048,128]{1,2,0:T(8,128)} fusion(f32[4,2048,128]{1,2,0:T(8,128)} %get-tuple-element.180, s32[]{:T(128)} %get-tuple-element.179, f32[8,128,2048]{2,1,0:T(8,128)} %get-tuple-element.170, f32[8,128]{1,0:T(8,128)S(1)} %get-tuple-element.171, bf16[4,8,128,128]{2,3,1,0:T(8,128)(2,1)} %get-tuple-element.190), kind=kOutput, calls=%fused_computation.18.clone.1 | convolution fusion | flops 541065216 | bytes 9704448 | tf_op jit(solution)/shard_map/while/body/eval_jaxpr/htu,htd->ud/dot_general | solution.py:88
  170.2 7.0 %all-to-all-start.5 = ((f32[4,64,512]{2,0,1:T(4,128)}), f32[4,64,512]{2,0,1:T(4,128)}, u32[]{:S(2)}, u32[]{:S(2)}) async-start(f32[4,64,512]{2,0,1:T(4,128)} %get-tuple-element.129), calls=%async_computation.5 | async-start | bytes 1048576 | tf_op jit(solution)/shard_map/all_to_all | solution.py:127
  177.2 101.7 %all-reduce.1 = bf16[4,2048,128]{1,2,0:T(8,128)(2,1)} all-reduce(f32[4,2048,128]{1,2,0:T(8,128)} %get-tuple-element.38), channel_id=1, replica_groups=mesh['rep'=32,'shard'=16] {'shard'}, use_global_device_ids=true, to_apply=%region_11.14 | all-reduce | flops 1048576 | bytes 6291456 | tf_op jit(solution)/shard_map/psum | solution.py:104
  279.0 1.4 copy-done.4
  282.3 1.6 reshape_reshape.7
  283.9 26.3 %all-to-all-start.4 = ((f32[32,4,4,512]{3,2,1,0:T(4,128)}), f32[32,4,4,512]{3,2,1,0:T(4,128)S(1)}, u32[]{:S(2)}, u32[]{:S(2)}) async-start(f32[32,4,4,512]{3,2,1,0:T(4,128)} %reshape_reshape.7), calls=%async_computation.4 | async-start | bytes 2097152 | tf_op jit(solution)/shard_map/all_to_all | solution.py:42
  311.5 28.8 %all-to-all-done.4 = f32[32,4,4,512]{3,2,1,0:T(4,128)S(1)} async-done(((f32[32,4,4,512]{3,2,1,0:T(4,128)}), f32[32,4,4,512]{3,2,1,0:T(4,128)S(1)}, u32[]{:S(2)}, u32[]{:S(2)}) %all-to-all-start.4) | async-done | bytes 1048608 | tf_op jit(solution)/shard_map/all_to_all | solution.py:42
  341.4 4.5 %all-to-all-start.6 = ((bf16[16,4,4,512]{3,1,2,0:T(4,128)(2,1)}), bf16[16,4,4,512]{3,1,2,0:T(4,128)(2,1)S(1)}, u32[]{:S(2)}, u32[]{:S(2)}) async-start(bf16[16,4,4,512]{3,1,2,0:T(4,128)(2,1)} %broadcast_in_dim.144), calls=%async_computation.6 | async-start | bytes 524288 | tf_op jit(solution)/shard_map/all_to_all | solution.py:27
  347.8 7.0 %all-to-all-done.6 = bf16[16,4,4,512]{3,1,2,0:T(4,128)(2,1)S(1)} async-done(((bf16[16,4,4,512]{3,1,2,0:T(4,128)(2,1)}), bf16[16,4,4,512]{3,1,2,0:T(4,128)(2,1)S(1)}, u32[]{:S(2)}, u32[]{:S(2)}) %all-to-all-start.6) | async-done | bytes 262176 | tf_op jit(solution)/shard_map/all_to_all | solution.py:27
  (62 shorter events, 17.7 us)
Async XLA Ops:
  0.6 6.5 %copy-start = (f32[4,6,512]{2,0,1:T(4,128)S(1)}, f32[4,6,512]{2,0,1:T(4,128)}, u32[]{:S(2)}) copy-start(f32[4,6,512]{2,0,1:T(4,128)} %param.22) | copy-start | bytes 147460
  0.6 7.3 %copy-start.2 = (f32[4,6,512]{2,0,1:T(4,128)S(1)}, f32[4,6,512]{2,0,1:T(4,128)}, u32[]{:S(2)}) copy-start(f32[4,6,512]{2,0,1:T(4,128)} %param.23) | copy-start | bytes 147460
  0.7 8.2 %copy-start.3 = (f32[4,6,512]{2,0,1:T(4,128)S(1)}, f32[4,6,512]{2,0,1:T(4,128)}, u32[]{:S(2)}) copy-start(f32[4,6,512]{2,0,1:T(4,128)} %param.21) | copy-start | bytes 147460
  9.7 12.0 %copy-start.6 = (bf16[128,512]{1,0:T(8,128)(2,1)S(1)}, bf16[128,512]{1,0:T(8,128)(2,1)}, u32[]{:S(2)}) copy-start(bf16[128,512]{1,0:T(8,128)(2,1)} %param.16) | copy-start | bytes 393220
  11.4 24.2 %all-to-all-start = ((f32[4,64,512]{2,0,1:T(4,128)}), f32[4,64,512]{2,0,1:T(4,128)S(1)}, u32[]{:S(2)}, u32[]{:S(2)}) async-start(f32[4,64,512]{2,0,1:T(4,128)} %get-tuple-element.130), calls=%async_computation | async-start | bytes 1048576 | tf_op jit(solution)/shard_map/all_to_all | solution.py:125
  88.6 23.5 %all-to-all-start.1 = ((f32[4,64,512]{2,0,1:T(4,128)}), f32[4,64,512]{2,0,1:T(4,128)S(1)}, u32[]{:S(2)}, u32[]{:S(2)}) async-start(f32[4,64,512]{2,0,1:T(4,128)} %get-tuple-element.128), calls=%async_computation.1 | async-start | bytes 1048576 | tf_op jit(solution)/shard_map/all_to_all | solution.py:126
  99.7 2.4 copy-start.5
  106.1 2.3 copy-start.1
  112.1 58.1 %all-to-all-start.3 = ((bf16[128,64,128]{2,0,1:T(8,128)(2,1)}), bf16[128,64,128]{2,0,1:T(8,128)(2,1)S(1)}, u32[]{:S(2)}, u32[]{:S(2)}) async-start(bf16[128,64,128]{2,0,1:T(8,128)(2,1)} %select_bitcast_fusion), calls=%async_computation.3 | async-start | bytes 4194304 | tf_op jit(solution)/shard_map/all_to_all | solution.py:110
  170.2 113.7 %all-to-all-start.5 = ((f32[4,64,512]{2,0,1:T(4,128)}), f32[4,64,512]{2,0,1:T(4,128)}, u32[]{:S(2)}, u32[]{:S(2)}) async-start(f32[4,64,512]{2,0,1:T(4,128)} %get-tuple-element.129), calls=%async_computation.5 | async-start | bytes 1048576 | tf_op jit(solution)/shard_map/all_to_all | solution.py:127
  278.9 1.6 copy-start.4
  283.9 56.4 %all-to-all-start.4 = ((f32[32,4,4,512]{3,2,1,0:T(4,128)}), f32[32,4,4,512]{3,2,1,0:T(4,128)S(1)}, u32[]{:S(2)}, u32[]{:S(2)}) async-start(f32[32,4,4,512]{3,2,1,0:T(4,128)} %reshape_reshape.7), calls=%async_computation.4 | async-start | bytes 2097152 | tf_op jit(solution)/shard_map/all_to_all | solution.py:42
  341.4 13.4 %all-to-all-start.6 = ((bf16[16,4,4,512]{3,1,2,0:T(4,128)(2,1)}), bf16[16,4,4,512]{3,1,2,0:T(4,128)(2,1)S(1)}, u32[]{:S(2)}, u32[]{:S(2)}) async-start(bf16[16,4,4,512]{3,1,2,0:T(4,128)(2,1)} %broadcast_in_dim.144), calls=%async_computation.6 | async-start | bytes 524288 | tf_op jit(solution)/shard_map/all_to_all | solution.py:27
where the time goes:
time: 361 us; the launch traced here: 357 us
  blocking collectives  154 us (43%)
  starting transfers between devices  60.1 us (17%)
  matrix products  51.5 us (14%)
  waiting for transfers between devices  49.5 us (14%)
  local copies, waits for them, and re-layouts  30 us (8%)
  other arithmetic  10.2 us (3%)
    psum x1, blocking collectives, local(): values = lax.psum(value_part, 'shard').astype(jnp.bfloat16)  102 us
    all_to_all x1, blocking collectives, from_everyone(): return lax.all_to_all(copies, axis, split_axis=0, concat_axis=0, tiled=True)  52.6 us
    sub x4, matrix products, one_group(): weights = jnp.exp(scores - highest)  29.1 us
    all_to_all x1, waiting for transfers between devices, sent_and_summed(): lax.all_to_all(parts, axis, split_axis=0, concat_axis=0, tiled=True)  28.8 us
    all_to_all x1, starting transfers between devices, sent_and_summed(): lax.all_to_all(parts, axis, split_axis=0, concat_axis=0, tiled=True)  26.3 us
    dot_general x4, matrix products, one_group(): jnp.einsum('htu,htd->ud', probs, cotangent, preferred_element_type=jnp.fl...  21.1 us
    all_to_all x1, waiting for transfers between devices, local(): lax.all_to_all(sent_param, 'shard', split_axis=1, concat_axis=0, tiled=True)  13.6 us
    unnamed x22, local copies, waits for them, and re-layouts  11.8 us
  transfers between devices with their start and end apart: 6, of which 3 were waited for; matrix products, arithmetic and copies ran while one was open for 21% of the time, Pallas kernels for 0%

commit v1 on v0

v1 whole, which is shorter than its diff:
```python
import jax
import jax.numpy as jnp
from jax import lax
from jax.experimental import pallas as pl
from jax.experimental.pallas import tpu as pltpu
from jax.sharding import Mesh, PartitionSpec as P

KV = 4
HD = 128
GRP = 8
STEP = 1000
LOG2E = 1.4426950408889634
MIB = 1 << 20

beta_first = 0.9
beta_second = 0.95
learning_rate = 0.02
decay_rate = 0.1
epsilon = 1e-08

PLANE = 512
CHUNK = 256
WHOLE = pl.BlockSpec(memory_space=pltpu.VMEM)
SCALARS = pl.BlockSpec(memory_space=pltpu.SMEM)
NT = (((1,), (1,)), ((), ()))
TN = (((0,), (0,)), ((), ()))


def swapped(x, axes):
    return lax.all_to_all(x, axes, split_axis=0, concat_axis=0, tiled=True)


def from_everyone(x, axes):
    return swapped(jnp.broadcast_to(x, (lax.axis_size(axes), *x.shape)), axes)


def value_kernel(place, q_ref, k_ref, d_ref, out_ref, own_ref, s_a, s_b, total):
    plane = place[0]
    factor = HD**-0.5 * LOG2E

    def scores(h, last, s_ref):
        q = q_ref[:, pl.ds(pl.multiple_of(h * HD, HD), HD)]
        top = jnp.full((8, PLANE), -jnp.inf, jnp.float32)
        for at in range(0, (last + 1) * PLANE, CHUNK):
            s = lax.dot_general(k_ref[at : at + CHUNK, :], q, NT, preferred_element_type=jnp.float32)
            if at >= last * PLANE:
                key = lax.broadcasted_iota(jnp.int32, s.shape, 0) + (at - last * PLANE)
                s = jnp.where(key <= lax.broadcasted_iota(jnp.int32, s.shape, 1), s, -jnp.inf)
            s_ref[at : at + CHUNK, :] = s
            top = jnp.maximum(top, jnp.max(s.reshape(CHUNK // 8, 8, PLANE), axis=0))
        return jnp.max(top, axis=0, keepdims=True)

    def add_terms(h, last, s_ref, top):
        d = d_ref[:, pl.ds(pl.multiple_of(h * HD, HD), HD)]
        size = jnp.zeros((8, PLANE), jnp.float32)
        for at in range(0, (last + 1) * PLANE, CHUNK):
            w = jnp.exp2((s_ref[at : at + CHUNK, :] - top) * factor)
            s_ref[at : at + CHUNK, :] = w
            size = size + jnp.sum(w.reshape(CHUNK // 8, 8, PLANE), axis=0)
        inverse = 1.0 / jnp.sum(size, axis=0, keepdims=True)
        for at in range(0, (last + 1) * PLANE, CHUNK):
            p = (s_ref[at : at + CHUNK, :] * inverse).astype(jnp.bfloat16)
            total[at : at + CHUNK, :] += jnp.dot(p, d, preferred_element_type=jnp.float32)

    for last in range(4):

        @pl.when(plane == last)
        def _(last=last):
            total[...] = jnp.zeros_like(total)

            @pl.loop(0, GRP // 2)
            def _(pair):
                top_a = scores(2 * pair, last, s_a)
                top_b = scores(2 * pair + 1, last, s_b)
                add_terms(2 * pair, last, s_a, top_a)
                add_terms(2 * pair + 1, last, s_b, top_b)

            own_ref[...] = total[last * PLANE : (last + 1) * PLANE, :]
            for k in range(4):
                out_ref[k] = total[k * PLANE : (k + 1) * PLANE, :].astype(jnp.bfloat16)


def value_terms(place, q, k, d):
    return pl.pallas_call(
        value_kernel,
        out_shape=(
            jax.ShapeDtypeStruct((4, PLANE, HD), jnp.bfloat16),
            jax.ShapeDtypeStruct((PLANE, HD), jnp.float32),
        ),
        in_specs=[SCALARS, WHOLE, WHOLE, WHOLE],
        out_specs=(WHOLE, WHOLE),
        scratch_shapes=[
            pltpu.VMEM((4 * PLANE, PLANE), jnp.float32),
            pltpu.VMEM((4 * PLANE, PLANE), jnp.float32),
            pltpu.VMEM((4 * PLANE, HD), jnp.float32),
        ],
        compiler_params=pltpu.CompilerParams(vmem_limit_bytes=40 * MIB),
        cost_estimate=pl.CostEstimate(flops=12 * 10**9, bytes_accessed=4 * MIB, transcendentals=8 * 10**6),
        name="values",
    )(place, q, k, d)


def gradient_kernel(place, in_ref, v_ref, out_ref, own_ref, values, rows):
    y = place[0]
    for c in range(2):
        for g in range(KV):
            values[c * PLANE : (c + 1) * PLANE, g * HD : (g + 1) * HD] = v_ref[c * KV + g]

    @pl.loop(0, 8)
    def _(b):
        lhs = in_ref[:, pl.ds(pl.multiple_of(b * 128, 128), 128)]
        rows[...] = lax.dot_general(lhs, values[...], TN, preferred_element_type=jnp.float32)
        for to in range(8):
            part = jnp.concatenate([rows[8 * to : 8 * to + 8, :], rows[64 + 8 * to : 72 + 8 * to, :]], axis=0)
            out_ref[to, b] = part.astype(jnp.bfloat16)
        mine = pl.multiple_of(8 * y, 8)
        own_ref[b, 0:8, :] = rows[pl.ds(mine, 8), :]
        own_ref[b, 8:16, :] = rows[pl.ds(mine + 64, 8), :]


def gradient_terms(place, pieces, values):
    return pl.pallas_call(
        gradient_kernel,
        out_shape=(
            jax.ShapeDtypeStruct((8, 8, 16, KV * HD), jnp.bfloat16),
            jax.ShapeDtypeStruct((8, 16, KV * HD), jnp.float32),
        ),
        in_specs=[SCALARS, WHOLE, WHOLE],
        out_specs=(WHOLE, WHOLE),
        scratch_shapes=[
            pltpu.VMEM((2 * PLANE, KV * HD), jnp.bfloat16),
            pltpu.VMEM((128, KV * HD), jnp.float32),
        ],
        compiler_params=pltpu.CompilerParams(vmem_limit_bytes=32 * MIB),
        cost_estimate=pl.CostEstimate(flops=2 * 10**9, bytes_accessed=4 * MIB, transcendentals=0),
        name="gradient",
    )(place, pieces, values)


def update_kernel(
    place, old_owner, new_owner, g_ref, st_ref, p_out, f_out, s_out, w_out, w_rows, old_count, new_count
):
    me = place[0]
    for i in range(16):
        old_count[i] = 0
        new_count[i] = 0

    @pl.loop(0, 64)
    def _(b):
        old = old_owner[b]
        slot = old_count[old]
        old_count[old] = slot + 1
        new = new_owner[b]
        to = new_count[new]
        new_count[new] = to + 1
        owner = (b // 32) * 16 + ((b // 2) % 4) * 4 + (b // 8) % 4
        gradient = g_ref[owner, b % 2]
        param = st_ref[old % 4, old // 4, 0, slot]
        first = beta_first * st_ref[old % 4, old // 4, 1, slot] + (1.0 - beta_first) * gradient
        second = beta_second * st_ref[old % 4, old // 4, 2, slot] + (1.0 - beta_second) * gradient * gradient
        first_hat = first / (1.0 - beta_first**STEP)
        second_hat = second / (1.0 - beta_second**STEP)
        param = param - learning_rate * (first_hat / (jnp.sqrt(second_hat) + epsilon) + decay_rate * param)
        for i in range(4):
            w_rows[i, pl.ds(b, 1), :] = param[i : i + 1, :]

        @pl.when(new == me)
        def _():
            p_out[to] = param
            f_out[to] = first
            s_out[to] = second

    w_out[...] = w_rows[...].astype(jnp.bfloat16)


def updated(place, old_owner, new_owner, gradient, state):
    block = jax.ShapeDtypeStruct((4, 4, KV * HD), jnp.float32)
    return pl.pallas_call(
        update_kernel,
        out_shape=(block, block, block, jax.ShapeDtypeStruct((4, 64, KV * HD), jnp.bfloat16)),
        in_specs=[SCALARS, SCALARS, SCALARS, WHOLE, WHOLE],
        out_specs=(WHOLE,) * 4,
        scratch_shapes=[
            pltpu.VMEM((4, 64, KV * HD), jnp.float32),
            pltpu.SMEM((16,), jnp.int32),
            pltpu.SMEM((16,), jnp.int32),
        ],
        compiler_params=pltpu.CompilerParams(vmem_limit_bytes=32 * MIB),
        cost_estimate=pl.CostEstimate(flops=4 * 10**6, bytes_accessed=4 * MIB, transcendentals=3 * 10**5),
        name="update",
    )(place, old_owner, new_owner, gradient, state)


def local(queries, keys, grad_out, inputs, old_owner, new_owner, param_old, first_old, second_old):
    here = queries.shape[0]
    zl = lax.axis_index("zl")
    y = lax.axis_index("y")
    shard = zl * 4 + lax.axis_index("x")

    by_group = keys.reshape(here, KV, HD).transpose(1, 0, 2)
    keys_all = swapped(jnp.broadcast_to(by_group, (4, KV, here, HD)).reshape(16, here, HD), ("zl", "x"))
    keys_all = keys_all.reshape(4 * PLANE, HD)
    q = swapped(queries.reshape(here, KV, GRP * HD).transpose(1, 0, 2), "x").reshape(PLANE, GRP * HD)
    d = swapped(grad_out.reshape(here, KV, GRP * HD).transpose(1, 0, 2), "x").reshape(PLANE, GRP * HD)
    pieces = swapped(inputs.reshape(here, 8, 1024).transpose(1, 0, 2), ("c", "x")).reshape(2 * PLANE, 1024)

    state = jnp.stack([a.transpose(1, 0, 2) for a in (param_old, first_old, second_old)])
    state = from_everyone(from_everyone(state, "zl"), "x")

    parts, own = value_terms(zl.reshape(1).astype(jnp.int32), q, keys_all, d)
    arrived = swapped(parts, "zl").astype(jnp.float32)
    source = jnp.arange(4)[:, None, None]
    values = (own + jnp.sum(jnp.where(source == zl, 0.0, arrived), axis=0)).astype(jnp.bfloat16)
    values = from_everyone(values, ("c", "x"))

    parts, own = gradient_terms(y.reshape(1).astype(jnp.int32), pieces, values)
    arrived = swapped(parts, "y").astype(jnp.float32)
    source = jnp.arange(8)[:, None, None, None]
    rows = own + jnp.sum(jnp.where(source == y, 0.0, arrived), axis=0)
    rows = rows.reshape(4, 2, 2, 8, KV * HD).transpose(2, 0, 1, 3, 4).reshape(8, 2, 8, KV * HD)
    rows = jnp.sum(swapped(rows, ("zh", "zl")), axis=0)
    by_core = rows.reshape(2, 2, 4, KV * HD).transpose(1, 0, 2, 3)
    by_core = jnp.broadcast_to(by_core[:, None], (2, 16, 2, 4, KV * HD)).reshape(32, 2, 4, KV * HD)
    gradient = swapped(by_core, ("c", "zl", "x"))

    *states, weights = updated(shard.reshape(1).astype(jnp.int32), old_owner, new_owner, gradient, state)
    return (*(a.transpose(1, 0, 2) for a in states), weights)


def solution(mesh):
    fine = Mesh(mesh.devices.reshape(2, 8, 2, 4, 4), ("zh", "y", "c", "zl", "x"))
    rep = ("zh", "y", "c")
    shard = ("zl", "x")
    tokens = P((*rep, *shard), None)
    placed = (tokens,) * 4 + (P(), P()) + (P(rep, shard, None),) * 3
    return jax.shard_map(
        local,
        mesh=fine,
        in_specs=placed,
        out_specs=(P(rep, shard, None),) * 3 + (P(rep, None, None),),
        check_vma=False,
    )
```

time: 361 us -> 287 us (0.80)
  blocking collectives: 154 us -> 16.9 us
  waiting for transfers between devices: 49.5 us -> 166 us
  matrix products: 51.5 us -> 0 us
  local copies, waits for them, and re-layouts: 30 us -> 15.5 us
  starting transfers between devices: 60.1 us -> 73.3 us
  Pallas kernels: 0 us -> 12.9 us
  other arithmetic: 10.2 us -> 0.59 us
    all_to_all x6 -> x10, waiting for transfers between devices: 49.5 us -> 166 us  [swapped(): return lax.all_to_all(x, axes, split_axis=0, concat_axis=0, tiled=True)]
    psum x1 -> x0, blocking collectives: 102 us -> none  [local(): values = lax.psum(value_part, 'shard').astype(jnp.bfloat16)]
    all_to_all x1, blocking collectives: 52.6 us -> 16.9 us  [swapped(): return lax.all_to_all(x, axes, split_axis=0, concat_axis=0, tiled=True)]
    sub x4 -> x0, matrix products: 29.1 us -> none  [one_group(): weights = jnp.exp(scores - highest)]
    dot_general x5 -> x0, matrix products: 22.4 us -> none  [the longest x4 21.1 us: one_group(): jnp.einsum('htu,htd->ud', probs, cotangent, preferred_element_type=jnp.fl...]
    all_to_all x6 -> x10, starting transfers between devices: 60.1 us -> 73.3 us  [swapped(): return lax.all_to_all(x, axes, split_axis=0, concat_axis=0, tiled=True)]
    pallas_call x0 -> x3, Pallas kernels: none -> 12.9 us  [the longest x1 5.11 us: value_terms(): pl.pallas_call(value_kernel, out_shape=(jax.ShapeDtypeStruct((4, PLANE, H...]
    unnamed x22 -> x19, local copies, waits for them, and re-layouts: 11.8 us -> 2.9 us
  transfers between devices with their start and end apart: 6 -> 10, of which waited for: 3 -> 10; matrix products, arithmetic and copies ran while one was open for 21% -> 2% of each run, Pallas kernels for 0% -> 0%
where the time goes in v1:
time: 287 us; the launch traced here: 286 us
  waiting for transfers between devices  166 us (58%)
  starting transfers between devices  73.3 us (26%)
  blocking collectives  16.9 us (6%)
  local copies, waits for them, and re-layouts  15.5 us (5%)
  Pallas kernels  12.9 us (4%)
    all_to_all x10, waiting for transfers between devices, swapped(): return lax.all_to_all(x, axes, split_axis=0, concat_axis=0, tiled=True)  166 us
    all_to_all x10, starting transfers between devices, swapped(): return lax.all_to_all(x, axes, split_axis=0, concat_axis=0, tiled=True)  73.3 us
    all_to_all x1, blocking collectives, swapped(): return lax.all_to_all(x, axes, split_axis=0, concat_axis=0, tiled=True)  16.9 us
  transfers between devices with their start and end apart: 10, of which 10 were waited for; matrix products, arithmetic and copies ran while one was open for 2% of the time, Pallas kernels for 0%

profile of v1, /device:TPU:1, one launch (start us, length us, event | category | flops | bytes accessed | tf_op | source)
XLA Modules:
  0.0 286.1 jit_solution(7552964840940234114)
XLA Ops:
  0.6 2.4 copy.46
  3.0 4.8 %all-to-all-start.3 = ((bf16[4,128,1024]{2,1,0:T(8,128)(2,1)}), bf16[4,128,1024]{2,1,0:T(8,128)(2,1)S(1)}, u32[]{:S(2)}, u32[]{:S(2)}) async-start(bf16[4,128,1024]{2,1,0:T(8,128)(2,1)} %bitcast.47), calls=%async_computation.3 | async-start | bytes 2097152 | tf_op jit(solution)/shard_map/all_to_all | solution.py:30
  7.9 1.1 copy.47
  8.9 8.6 %all-to-all-done.3 = bf16[4,128,1024]{2,1,0:T(8,128)(2,1)S(1)} async-done(((bf16[4,128,1024]{2,1,0:T(8,128)(2,1)}), bf16[4,128,1024]{2,1,0:T(8,128)(2,1)S(1)}, u32[]{:S(2)}, u32[]{:S(2)}) %all-to-all-start.3) | async-done | bytes 1048608 | tf_op jit(solution)/shard_map/all_to_all | solution.py:30
  17.6 3.5 %all-to-all-start.1 = ((bf16[4,128,1024]{2,1,0:T(8,128)(2,1)}), bf16[4,128,1024]{2,1,0:T(8,128)(2,1)S(1)}, u32[]{:S(2)}, u32[]{:S(2)}) async-start(bf16[4,128,1024]{2,1,0:T(8,128)(2,1)} %bitcast.49), calls=%async_computation.1 | async-start | bytes 2097152 | tf_op jit(solution)/shard_map/all_to_all | solution.py:30
  21.2 9.6 %all-to-all-done.1 = bf16[4,128,1024]{2,1,0:T(8,128)(2,1)S(1)} async-done(((bf16[4,128,1024]{2,1,0:T(8,128)(2,1)}), bf16[4,128,1024]{2,1,0:T(8,128)(2,1)S(1)}, u32[]{:S(2)}, u32[]{:S(2)}) %all-to-all-start.1) | async-done | bytes 1048608 | tf_op jit(solution)/shard_map/all_to_all | solution.py:30
  31.7 15.7 %all-to-all-start.2 = ((bf16[16,128,128]{2,1,0:T(8,128)(2,1)}), bf16[16,128,128]{2,1,0:T(8,128)(2,1)S(1)}, u32[]{:S(2)}, u32[]{:S(2)}) async-start(bf16[16,128,128]{2,1,0:T(8,128)(2,1)} %bitcast.8), calls=%async_computation.2 | async-start | bytes 1048576 | tf_op jit(solution)/shard_map/all_to_all | solution.py:30
  47.4 11.8 %all-to-all-done.2 = bf16[16,128,128]{2,1,0:T(8,128)(2,1)S(1)} async-done(((bf16[16,128,128]{2,1,0:T(8,128)(2,1)}), bf16[16,128,128]{2,1,0:T(8,128)(2,1)S(1)}, u32[]{:S(2)}, u32[]{:S(2)}) %all-to-all-start.2) | async-done | bytes 524320 | tf_op jit(solution)/shard_map/all_to_all | solution.py:30
  59.2 5.1 %values.1 = (bf16[4,512,128]{2,1,0:T(8,128)(2,1)}, f32[512,128]{1,0:T(8,128)S(1)}) custom-call(s32[1]{0:T(128)} %bitcast.4.place, bf16[512,1024]{1,0:T(8,128)(2,1)S(1)} %bitcast.52, bf16[2048,128]{1,0:T(8,128)(2,1)S(1)} %bitcast.53, bf16[512,1024]{1,0:T(8,128)(2,1)S(1)} %bitcast.51), custom_call_target="tpu_custom_call" | custom-call | flops 12000000000 | bytes 4194304 | tf_op jit(solution)/shard_map/values/pallas_call | solution.py:84
  64.3 16.3 %all-to-all-start.4 = ((bf16[4,512,128]{2,1,0:T(8,128)(2,1)}), bf16[4,512,128]{2,1,0:T(8,128)(2,1)S(1)}, u32[]{:S(2)}, u32[]{:S(2)}) async-start(bf16[4,512,128]{2,1,0:T(8,128)(2,1)} %get-tuple-element.13), calls=%async_computation.4 | async-start | bytes 1048576 | tf_op jit(solution)/shard_map/all_to_all | solution.py:30
  80.6 3.2 %copy.45 = bf16[16,8,8,1024]{3,2,0,1:T(8,128)(2,1)} copy(bf16[16,8,8,1024]{3,2,1,0:T(8,128)(2,1)} %bitcast.58) | data formatting | bytes 4194304 | tf_op jit(solution)/shard_map/reshape | solution.py:205
  83.7 8.4 %all-to-all-done.4 = bf16[4,512,128]{2,1,0:T(8,128)(2,1)S(1)} async-done(((bf16[4,512,128]{2,1,0:T(8,128)(2,1)}), bf16[4,512,128]{2,1,0:T(8,128)(2,1)S(1)}, u32[]{:S(2)}, u32[]{:S(2)}) %all-to-all-start.4) | async-done | bytes 524320 | tf_op jit(solution)/shard_map/all_to_all | solution.py:30
  92.1 7.4 %all-to-all-start = ((bf16[8,128,1024]{2,1,0:T(8,128)(2,1)}), bf16[8,128,1024]{2,1,0:T(8,128)(2,1)S(1)}, u32[]{:S(2)}, u32[]{:S(2)}) async-start(bf16[8,128,1024]{2,1,0:T(8,128)(2,1)} %bitcast.57), calls=%async_computation | async-start | bytes 4194304 | tf_op jit(solution)/shard_map/all_to_all | solution.py:30
  99.8 26.0 %all-to-all-done = bf16[8,128,1024]{2,1,0:T(8,128)(2,1)S(1)} async-done(((bf16[8,128,1024]{2,1,0:T(8,128)(2,1)}), bf16[8,128,1024]{2,1,0:T(8,128)(2,1)S(1)}, u32[]{:S(2)}, u32[]{:S(2)}) %all-to-all-start) | async-done | bytes 2097184 | tf_op jit(solution)/shard_map/all_to_all | solution.py:30
  125.8 1.1 broadcast_in_dim.47
  126.9 3.8 %all-to-all-start.5 = ((bf16[8,512,128]{2,1,0:T(8,128)(2,1)}), bf16[8,512,128]{2,1,0:T(8,128)(2,1)S(1)}, u32[]{:S(2)}, u32[]{:S(2)}) async-start(bf16[8,512,128]{2,1,0:T(8,128)(2,1)} %broadcast_in_dim.47), calls=%async_computation.5 | async-start | bytes 2097152 | tf_op jit(solution)/shard_map/all_to_all | solution.py:30
  130.7 15.0 %all-to-all-done.5.v_ref = bf16[8,512,128]{2,1,0:T(8,128)(2,1)S(1)} async-done(((bf16[8,512,128]{2,1,0:T(8,128)(2,1)}), bf16[8,512,128]{2,1,0:T(8,128)(2,1)S(1)}, u32[]{:S(2)}, u32[]{:S(2)}) %all-to-all-start.5) | async-done | bytes 1048608 | tf_op jit(solution)/shard_map/all_to_all | solution.py:30
  145.7 3.0 %gradient.1 = (bf16[8,8,16,512]{3,2,1,0:T(8,128)(2,1)S(1)}, f32[8,16,512]{2,1,0:T(8,128)S(1)}) custom-call(s32[1]{0:T(128)} %bitcast.1.place, bf16[1024,1024]{1,0:T(8,128)(2,1)S(1)} %bitcast.50, bf16[8,512,128]{2,1,0:T(8,128)(2,1)S(1)} %all-to-all-done.5.v_ref), custom_call_target="tpu_custom_call" | custom-call | flops 2000000000 | bytes 4194304 | tf_op jit(solution)/shard_map/gradient/pallas_call | solution.py:122
  148.8 1.0 copy-done
  149.8 6.9 %all-to-all-start.6 = ((bf16[8,8,16,512]{3,2,1,0:T(8,128)(2,1)}), bf16[8,8,16,512]{3,2,1,0:T(8,128)(2,1)S(1)}, u32[]{:S(2)}, u32[]{:S(2)}) async-start(bf16[8,8,16,512]{3,2,1,0:T(8,128)(2,1)} %copy-done), calls=%async_computation.6 | async-start | bytes 2097152 | tf_op jit(solution)/shard_map/all_to_all | solution.py:30
  156.8 29.2 %all-to-all-done.6 = bf16[8,8,16,512]{3,2,1,0:T(8,128)(2,1)S(1)} async-done(((bf16[8,8,16,512]{3,2,1,0:T(8,128)(2,1)}), bf16[8,8,16,512]{3,2,1,0:T(8,128)(2,1)S(1)}, u32[]{:S(2)}, u32[]{:S(2)}) %all-to-all-start.6) | async-done | bytes 1048608 | tf_op jit(solution)/shard_map/all_to_all | solution.py:30
  185.9 0.9 broadcast_in_dim.51
  186.9 3.5 %all-to-all-start.9 = ((f32[4,3,6,4,512]{4,3,2,1,0:T(4,128)}), f32[4,3,6,4,512]{4,3,2,1,0:T(4,128)S(1)}, u32[]{:S(2)}, u32[]{:S(2)}) async-start(f32[4,3,6,4,512]{4,3,2,1,0:T(4,128)} %broadcast_in_dim.51), calls=%async_computation.9 | async-start | bytes 1179648 | tf_op jit(solution)/shard_map/all_to_all | solution.py:30
  190.7 15.1 %all-to-all-done.9 = f32[4,3,6,4,512]{4,3,2,1,0:T(4,128)S(1)} async-done(((f32[4,3,6,4,512]{4,3,2,1,0:T(4,128)}), f32[4,3,6,4,512]{4,3,2,1,0:T(4,128)S(1)}, u32[]{:S(2)}, u32[]{:S(2)}) %all-to-all-start.9) | async-done | bytes 589856 | tf_op jit(solution)/shard_map/all_to_all | solution.py:30
  205.8 16.9 %all_to_all.55 = f32[8,2,8,512]{3,2,1,0:T(8,128)S(1)} all-to-all(f32[8,2,8,512]{3,2,1,0:T(8,128)S(1)} %bitcast.62), channel_id=1, replica_groups=mesh['zh'=2,'y'=8,'c'=2,'zl'=4,'x'=4] {'zh','zl'}, dimensions={0} | all-to-all | bytes 524288 | tf_op jit(solution)/shard_map/all_to_all | solution.py:30
  222.7 2.0 broadcast_in_dim.52
  224.7 3.8 %all-to-all-start.10 = ((f32[4,4,3,6,4,512]{5,4,3,2,1,0:T(4,128)}), f32[4,4,3,6,4,512]{5,4,3,2,1,0:T(4,128)S(1)}, u32[]{:S(2)}, u32[]{:S(2)}) async-start(f32[4,4,3,6,4,512]{5,4,3,2,1,0:T(4,128)} %broadcast_in_dim.52), calls=%async_computation.10 | async-start | bytes 4718592 | tf_op jit(solution)/shard_map/all_to_all | solution.py:30
  228.6 26.0 %all-to-all-done.10.st_ref = f32[4,4,3,6,4,512]{5,4,3,2,1,0:T(4,128)S(1)} async-done(((f32[4,4,3,6,4,512]{5,4,3,2,1,0:T(4,128)}), f32[4,4,3,6,4,512]{5,4,3,2,1,0:T(4,128)S(1)}, u32[]{:S(2)}, u32[]{:S(2)}) %all-to-all-start.10) | async-done | bytes 2359328 | tf_op jit(solution)/shard_map/all_to_all | solution.py:30
  254.6 0.9 broadcast_in_dim.50
  255.5 7.6 %all-to-all-start.8 = ((f32[32,2,4,512]{3,2,1,0:T(4,128)}), f32[32,2,4,512]{3,2,1,0:T(4,128)S(1)}, u32[]{:S(2)}, u32[]{:S(2)}) async-start(f32[32,2,4,512]{3,2,1,0:T(4,128)} %bitcast.17), calls=%async_computation.8 | async-start | bytes 1048576 | tf_op jit(solution)/shard_map/all_to_all | solution.py:30
  263.2 16.3 %all-to-all-done.8.g_ref = f32[32,2,4,512]{3,2,1,0:T(4,128)S(1)} async-done(((f32[32,2,4,512]{3,2,1,0:T(4,128)}), f32[32,2,4,512]{3,2,1,0:T(4,128)S(1)}, u32[]{:S(2)}, u32[]{:S(2)}) %all-to-all-start.8) | async-done | bytes 524320 | tf_op jit(solution)/shard_map/all_to_all | solution.py:30
  279.5 4.7 %update.1 = (f32[4,4,512]{2,1,0:T(4,128)S(1)}, f32[4,4,512]{2,1,0:T(4,128)S(1)}, f32[4,4,512]{2,1,0:T(4,128)S(1)}, bf16[4,64,512]{2,1,0:T(8,128)(2,1)}) custom-call(s32[1]{0:T(128)} %bitcast.place, s32[64]{0:T(128)S(1)} %copy-done.1, s32[64]{0:T(128)S(1)} %copy-done.2, f32[32,2,4,512]{3,2,1,0:T(4,128)S(1)} %all-to-all-done.8.g_ref, ...), custom_call_target="tpu_custom_call" | custom-call | flops 4000000 | bytes 4194304 | tf_op jit(solution)/shard_map/update/pallas_call | solution.py:178
  (32 shorter events, 3.5 us)
Async XLA Ops:
  0.6 7.2 %copy-start.3 = (bf16[128,4096]{1,0:T(8,128)(2,1)S(1)}, bf16[128,4096]{1,0:T(8,128)(2,1)}, u32[]{:S(2)}) copy-start(bf16[128,4096]{1,0:T(8,128)(2,1)} %param.9) | copy-start | bytes 3145732
  3.0 14.6 %all-to-all-start.3 = ((bf16[4,128,1024]{2,1,0:T(8,128)(2,1)}), bf16[4,128,1024]{2,1,0:T(8,128)(2,1)S(1)}, u32[]{:S(2)}, u32[]{:S(2)}) async-start(bf16[4,128,1024]{2,1,0:T(8,128)(2,1)} %bitcast.47), calls=%async_computation.3 | async-start | bytes 2097152 | tf_op jit(solution)/shard_map/all_to_all | solution.py:30
  7.9 13.3 %copy-start.4 = (bf16[128,512]{1,0:T(8,128)(2,1)S(1)}, bf16[128,512]{1,0:T(8,128)(2,1)}, u32[]{:S(2)}) copy-start(bf16[128,512]{1,0:T(8,128)(2,1)} %param.10) | copy-start | bytes 393220
  17.6 13.2 %all-to-all-start.1 = ((bf16[4,128,1024]{2,1,0:T(8,128)(2,1)}), bf16[4,128,1024]{2,1,0:T(8,128)(2,1)S(1)}, u32[]{:S(2)}, u32[]{:S(2)}) async-start(bf16[4,128,1024]{2,1,0:T(8,128)(2,1)} %bitcast.49), calls=%async_computation.1 | async-start | bytes 2097152 | tf_op jit(solution)/shard_map/all_to_all | solution.py:30
  31.7 27.4 %all-to-all-start.2 = ((bf16[16,128,128]{2,1,0:T(8,128)(2,1)}), bf16[16,128,128]{2,1,0:T(8,128)(2,1)S(1)}, u32[]{:S(2)}, u32[]{:S(2)}) async-start(bf16[16,128,128]{2,1,0:T(8,128)(2,1)} %bitcast.8), calls=%async_computation.2 | async-start | bytes 1048576 | tf_op jit(solution)/shard_map/all_to_all | solution.py:30
  64.3 27.8 %all-to-all-start.4 = ((bf16[4,512,128]{2,1,0:T(8,128)(2,1)}), bf16[4,512,128]{2,1,0:T(8,128)(2,1)S(1)}, u32[]{:S(2)}, u32[]{:S(2)}) async-start(bf16[4,512,128]{2,1,0:T(8,128)(2,1)} %get-tuple-element.13), calls=%async_computation.4 | async-start | bytes 1048576 | tf_op jit(solution)/shard_map/all_to_all | solution.py:30
  92.1 33.6 %all-to-all-start = ((bf16[8,128,1024]{2,1,0:T(8,128)(2,1)}), bf16[8,128,1024]{2,1,0:T(8,128)(2,1)S(1)}, u32[]{:S(2)}, u32[]{:S(2)}) async-start(bf16[8,128,1024]{2,1,0:T(8,128)(2,1)} %bitcast.57), calls=%async_computation | async-start | bytes 4194304 | tf_op jit(solution)/shard_map/all_to_all | solution.py:30
  126.9 18.8 %all-to-all-start.5 = ((bf16[8,512,128]{2,1,0:T(8,128)(2,1)}), bf16[8,512,128]{2,1,0:T(8,128)(2,1)S(1)}, u32[]{:S(2)}, u32[]{:S(2)}) async-start(bf16[8,512,128]{2,1,0:T(8,128)(2,1)} %broadcast_in_dim.47), calls=%async_computation.5 | async-start | bytes 2097152 | tf_op jit(solution)/shard_map/all_to_all | solution.py:30
  148.7 1.0 copy-start
  149.8 7.0 %copy-start.5 = (f32[4,6,512]{2,0,1:T(4,128)S(1)}, f32[4,6,512]{2,0,1:T(4,128)}, u32[]{:S(2)}) copy-start(f32[4,6,512]{2,0,1:T(4,128)} %param.17) | copy-start | bytes 147460
  149.8 7.0 %copy-start.6 = (f32[4,6,512]{2,0,1:T(4,128)S(1)}, f32[4,6,512]{2,0,1:T(4,128)}, u32[]{:S(2)}) copy-start(f32[4,6,512]{2,0,1:T(4,128)} %param.16) | copy-start | bytes 147460
  149.8 7.0 %copy-start.7 = (f32[4,6,512]{2,0,1:T(4,128)S(1)}, f32[4,6,512]{2,0,1:T(4,128)}, u32[]{:S(2)}) copy-start(f32[4,6,512]{2,0,1:T(4,128)} %param.15) | copy-start | bytes 147460
  149.8 36.2 %all-to-all-start.6 = ((bf16[8,8,16,512]{3,2,1,0:T(8,128)(2,1)}), bf16[8,8,16,512]{3,2,1,0:T(8,128)(2,1)S(1)}, u32[]{:S(2)}, u32[]{:S(2)}) async-start(bf16[8,8,16,512]{3,2,1,0:T(8,128)(2,1)} %copy-done), calls=%async_computation.6 | async-start | bytes 2097152 | tf_op jit(solution)/shard_map/all_to_all | solution.py:30
  186.9 19.0 %all-to-all-start.9 = ((f32[4,3,6,4,512]{4,3,2,1,0:T(4,128)}), f32[4,3,6,4,512]{4,3,2,1,0:T(4,128)S(1)}, u32[]{:S(2)}, u32[]{:S(2)}) async-start(f32[4,3,6,4,512]{4,3,2,1,0:T(4,128)} %broadcast_in_dim.51), calls=%async_computation.9 | async-start | bytes 1179648 | tf_op jit(solution)/shard_map/all_to_all | solution.py:30
  224.7 54.7 %copy-start.1 = (s32[64]{0:T(128)S(1)}, s32[64]{0:T(128)}, u32[]{:S(2)}) copy-start(s32[64]{0:T(128)} %old_owner.1) | copy-start | bytes 772
  224.7 54.7 %copy-start.2 = (s32[64]{0:T(128)S(1)}, s32[64]{0:T(128)}, u32[]{:S(2)}) copy-start(s32[64]{0:T(128)} %new_owner.1) | copy-start | bytes 772
  224.7 29.9 %all-to-all-start.10 = ((f32[4,4,3,6,4,512]{5,4,3,2,1,0:T(4,128)}), f32[4,4,3,6,4,512]{5,4,3,2,1,0:T(4,128)S(1)}, u32[]{:S(2)}, u32[]{:S(2)}) async-start(f32[4,4,3,6,4,512]{5,4,3,2,1,0:T(4,128)} %broadcast_in_dim.52), calls=%async_computation.10 | async-start | bytes 4718592 | tf_op jit(solution)/shard_map/all_to_all | solution.py:30
  255.5 23.9 %all-to-all-start.8 = ((f32[32,2,4,512]{3,2,1,0:T(4,128)}), f32[32,2,4,512]{3,2,1,0:T(4,128)S(1)}, u32[]{:S(2)}, u32[]{:S(2)}) async-start(f32[32,2,4,512]{3,2,1,0:T(4,128)} %bitcast.17), calls=%async_computation.8 | async-start | bytes 1048576 | tf_op jit(solution)/shard_map/all_to_all | solution.py:30

commit v2 on v1

v2 whole, which is shorter than its diff:
```python
import functools

import jax
import jax.numpy as jnp
from jax import lax
from jax.experimental import pallas as pl
from jax.experimental.pallas import tpu as pltpu
from jax.sharding import Mesh, PartitionSpec as P

KV = 4
HD = 128
GRP = 8
STEP = 1000
LOG2E = 1.4426950408889634
MIB = 1 << 20

beta_first = 0.9
beta_second = 0.95
learning_rate = 0.02
decay_rate = 0.1
epsilon = 1e-08

PLANE = 512
CHUNK = 256
ZH, Y, C, ZL, X = range(5)
WHOLE = pl.BlockSpec(memory_space=pltpu.VMEM)
SCALARS = pl.BlockSpec(memory_space=pltpu.SMEM)
NT = (((1,), (1,)), ((), ()))
TN = (((0,), (0,)), ((), ()))


def swapped(x, axes):
    return lax.all_to_all(x, axes, split_axis=0, concat_axis=0, tiled=True)


def shifted(x, axis, k):
    n = lax.axis_size(axis)
    return lax.ppermute(x, axis, [(i, (i + k) % n) for i in range(n)])


def around(own, axis, parts=None):
    return [own] + [shifted(own if parts is None else parts[k - 1], axis, k) for k in (1, 2, 3)]


def after(x, *done):
    return lax.optimization_barrier((x, *done))[0]


def call(kernel, name, out, scalars, arrays, scratch, flops=10**6, moved=4 * MIB, special=0, limit=40):
    return pl.pallas_call(
        kernel,
        out_shape=out,
        in_specs=[SCALARS] * len(scalars) + [WHOLE] * len(arrays),
        out_specs=jax.tree.map(lambda _: WHOLE, out),
        scratch_shapes=scratch,
        compiler_params=pltpu.CompilerParams(vmem_limit_bytes=limit * MIB),
        cost_estimate=pl.CostEstimate(flops=flops, bytes_accessed=moved, transcendentals=special),
        name=name,
    )(*scalars, *arrays)


def shape(*dims, dtype=jnp.bfloat16):
    return jax.ShapeDtypeStruct(dims, dtype)


def pack_heads_kernel(place, q_ref, d_ref, *out):
    for half in range(2):
        for k in range(4):
            at = ((place[X] + k) % 4) * GRP * HD + half * 512
            at = pl.ds(pl.multiple_of(at, 512), 512)
            out[4 * half + k][:, 0:512] = q_ref[:, at]
            out[4 * half + k][:, 512:1024] = d_ref[:, at]


def pack_inputs_kernel(place, in_ref, kept, sent):
    for k in range(4):
        at = ((place[X] + k) % 4) * 2048
        for c, out in ((place[C], kept), (1 - place[C], sent)):
            out[k] = in_ref[:, pl.ds(pl.multiple_of(at + c * 1024, 1024), 1024)]


def value_kernel(half, place, k_ref, r0, r1, r2, r3, *refs):
    plane = place[ZL]
    factor = HD**-0.5 * LOG2E
    if half == 0:
        total, q_ref, d_ref, s_a, s_b = refs
    else:
        before, out_ref, own_ref, q_ref, d_ref, s_a, s_b, total = refs
    for k, part in enumerate((r0, r1, r2, r3)):
        rows = pl.ds(pl.multiple_of(((place[X] + 4 - k) % 4) * 128, 128), 128)
        q_ref[rows, :] = part[:, 0:512]
        d_ref[rows, :] = part[:, 512:1024]

    def scores(h, last, s_ref):
        q = q_ref[:, pl.ds(pl.multiple_of(h * HD, HD), HD)]
        top = jnp.full((8, PLANE), -jnp.inf, jnp.float32)
        for at in range(0, (last + 1) * PLANE, CHUNK):
            s = lax.dot_general(k_ref[at : at + CHUNK, :], q, NT, preferred_element_type=jnp.float32)
            if at >= last * PLANE:
                key = lax.broadcasted_iota(jnp.int32, s.shape, 0) + (at - last * PLANE)
                s = jnp.where(key <= lax.broadcasted_iota(jnp.int32, s.shape, 1), s, -jnp.inf)
            s_ref[at : at + CHUNK, :] = s
            top = jnp.maximum(top, jnp.max(s.reshape(CHUNK // 8, 8, PLANE), axis=0))
        return jnp.max(top, axis=0, keepdims=True)

    def add_terms(h, last, s_ref, top):
        d = d_ref[:, pl.ds(pl.multiple_of(h * HD, HD), HD)]
        size = jnp.zeros((8, PLANE), jnp.float32)
        for at in range(0, (last + 1) * PLANE, CHUNK):
            w = jnp.exp2((s_ref[at : at + CHUNK, :] - top) * factor)
            s_ref[at : at + CHUNK, :] = w
            size = size + jnp.sum(w.reshape(CHUNK // 8, 8, PLANE), axis=0)
        inverse = 1.0 / jnp.sum(size, axis=0, keepdims=True)
        for at in range(0, (last + 1) * PLANE, CHUNK):
            p = (s_ref[at : at + CHUNK, :] * inverse).astype(jnp.bfloat16)
            total[at : at + CHUNK, :] += jnp.dot(p, d, preferred_element_type=jnp.float32)

    for last in range(4):

        @pl.when(plane == last)
        def _(last=last):
            if half == 0:
                total[...] = jnp.zeros_like(total)
            else:
                total[...] = before[...]

            @pl.loop(0, GRP // 4)
            def _(pair):
                top_a = scores(2 * pair, last, s_a)
                top_b = scores(2 * pair + 1, last, s_b)
                add_terms(2 * pair, last, s_a, top_a)
                add_terms(2 * pair + 1, last, s_b, top_b)

            if half == 1:
                own_ref[...] = total[last * PLANE : (last + 1) * PLANE, :]
                for k in range(4):
                    out_ref[k] = total[k * PLANE : (k + 1) * PLANE, :].astype(jnp.bfloat16)


def value_terms(half, place, keys, parts, before=None):
    total = shape(4 * PLANE, HD, dtype=jnp.float32)
    own = shape(PLANE, HD, dtype=jnp.float32)
    scratch = [
        pltpu.VMEM((PLANE, 512), jnp.bfloat16),
        pltpu.VMEM((PLANE, 512), jnp.bfloat16),
        pltpu.VMEM((4 * PLANE, PLANE), jnp.float32),
        pltpu.VMEM((4 * PLANE, PLANE), jnp.float32),
    ]
    return call(
        functools.partial(value_kernel, half),
        "values",
        total if half == 0 else (shape(4, PLANE, HD), own),
        [place],
        [keys, *parts, *([] if half == 0 else [before])],
        scratch if half == 0 else [*scratch, pltpu.VMEM((4 * PLANE, HD), jnp.float32)],
        flops=6 * 10**9,
        special=4 * 10**6,
    )


def sum_values_kernel(place, in_ref, own_ref, out_ref):
    total = own_ref[...] - in_ref[place[ZL]].astype(jnp.float32)
    for k in range(4):
        total = total + in_ref[k].astype(jnp.float32)
    rounded = total.astype(jnp.bfloat16)
    for k in range(8):
        out_ref[k] = rounded


def gradient_kernel(place, i0, i1, i2, i3, v_ref, out_ref, own_ref, values, rows_a, rows_b):
    for k in range(4):
        source = pl.ds(pl.multiple_of(((place[X] + 4 - k) % 4) * 128, 128), 128)
        for other in range(2):
            core = place[C] if other == 0 else 1 - place[C]
            at = (2 * k + other) * 128
            for g in range(KV):
                values[at : at + 128, g * HD : (g + 1) * HD] = v_ref[core * KV + g, source, :]

    @pl.loop(0, 4)
    def _(zl):
        for half, rows in enumerate((rows_a, rows_b)):
            at = pl.ds(pl.multiple_of(zl * 256 + half * 128, 128), 128)
            total = None
            for k, in_ref in enumerate((i0, i1, i2, i3)):
                term = lax.dot_general(
                    in_ref[:, at], values[256 * k : 256 * k + 256, :], TN, preferred_element_type=jnp.float32
                )
                total = term if total is None else total + term
            rows[...] = total
        for to in range(16):
            part = jnp.concatenate([rows_a[8 * to : 8 * to + 8, :], rows_b[8 * to : 8 * to + 8, :]], axis=0)
            out_ref[to * 4 + zl] = part.astype(jnp.bfloat16)

        @pl.when(zl == place[ZL])
        def _():
            mine = pl.ds(pl.multiple_of((place[ZH] * 8 + place[Y]) * 8, 8), 8)
            own_ref[0:8, :] = rows_a[mine, :]
            own_ref[8:16, :] = rows_b[mine, :]


def sum_rows_kernel(place, in_ref, own_ref, out_ref):
    total = own_ref[...] - in_ref[place[ZH] * 32 + place[Y] * 4 + place[ZL]].astype(jnp.float32)
    for k in range(64):
        total = total + in_ref[k].astype(jnp.float32)
    for c in range(2):
        for half in range(2):
            part = total[half * 8 + c * 4 : half * 8 + c * 4 + 4, :]
            for k in range(16):
                out_ref[16 * c + k, half] = part


def order_kernel(place, old_owner, s0, s1, s2, s3, out_ref, count):
    for i in range(16):
        count[i] = 0

    @pl.loop(0, 64)
    def _(b):
        old = old_owner[b]
        slot = count[old]
        count[old] = slot + 1
        kz = (place[ZL] + 4 - old // 4) % 4
        kx = (place[X] + 4 - old % 4) % 4
        for k, s_ref in enumerate((s0, s1, s2, s3)):

            @pl.when(kx == k)
            def _(s_ref=s_ref):
                for part in range(3):
                    out_ref[b, part] = s_ref[kz, part, slot]


def update_kernel(place, new_owner, g_ref, st_ref, p_out, f_out, s_out, w_out, w_rows, changed, count):
    @pl.loop(0, 64, unroll=4)
    def _(b):
        owner = ((b // 8) % 2) * 16 + ((b // 2) % 4) * 4 + b // 16
        gradient = g_ref[owner, b % 2]
        param = st_ref[b, 0]
        first = beta_first * st_ref[b, 1] + (1.0 - beta_first) * gradient
        second = beta_second * st_ref[b, 2] + (1.0 - beta_second) * gradient * gradient
        first_hat = first / (1.0 - beta_first**STEP)
        second_hat = second / (1.0 - beta_second**STEP)
        param = param - learning_rate * (first_hat / (jnp.sqrt(second_hat) + epsilon) + decay_rate * param)
        for i in range(4):
            w_rows[i, pl.ds(b, 1), :] = param[i : i + 1, :]
        changed[b, 0] = param
        changed[b, 1] = first
        changed[b, 2] = second

    w_out[...] = w_rows[...].astype(jnp.bfloat16)
    count[0] = 0

    @pl.loop(0, 64)
    def _(b):
        @pl.when(new_owner[b] == place[ZL] * 4 + place[X])
        def _():
            to = count[0]
            count[0] = to + 1
            for part, out in enumerate((p_out, f_out, s_out)):
                block = changed[b, part]
                for i in range(4):
                    out[i, pl.ds(to, 1), :] = block[i : i + 1, :]


def local(queries, keys, grad_out, inputs, old_owner, new_owner, param_old, first_old, second_old):
    f32 = jnp.float32
    here = queries.shape[0]
    place = jnp.stack([lax.axis_index(a) for a in ("zh", "y", "c", "zl", "x")]).astype(jnp.int32)

    by_group = keys.reshape(here, KV, HD).transpose(1, 0, 2)
    keys_all = swapped(jnp.broadcast_to(by_group, (4, KV, here, HD)).reshape(16, here, HD), ("zl", "x"))
    keys_all = keys_all.reshape(4 * PLANE, HD)
    packed = call(
        pack_heads_kernel, "pack_heads", (shape(here, 1024),) * 8, [place], [queries, grad_out], []
    )
    early = around(packed[0], "x", packed[1:4])
    late = around(packed[4], "x", packed[5:8])
    kept, sent = call(
        pack_inputs_kernel, "pack_inputs", (shape(4, here, 1024),) * 2, [place], [inputs], []
    )
    other = shifted(sent, "c", 1)

    total = value_terms(0, place, keys_all, early)
    kept, other, total = lax.optimization_barrier((kept, other, total))
    pieces = [jnp.concatenate([kept[k], other[k]], axis=0) for k in range(4)]
    pieces = around(pieces[0], "x", pieces[1:])
    parts, own = value_terms(1, place, keys_all, late, total)
    arrived = swapped(parts, "zl")
    values = call(sum_values_kernel, "sum_values", shape(8, PLANE, HD), [place], [arrived, own], [])

    state = jnp.stack([a.transpose(1, 0, 2) for a in (param_old, first_old, second_old)])
    state = jnp.stack(around(after(state, values), "zl"))
    values, pieces = lax.optimization_barrier((values, pieces))
    values = swapped(values, ("c", "x"))

    parts, own = call(
        gradient_kernel,
        "gradient",
        (shape(64, 16, KV * HD), shape(16, KV * HD, dtype=f32)),
        [place],
        [*pieces, values],
        [pltpu.VMEM((2 * PLANE, KV * HD), jnp.bfloat16)] + [pltpu.VMEM((128, KV * HD), f32)] * 2,
        flops=2 * 10**9,
    )
    state, parts = lax.optimization_barrier((state, parts))
    arrived = swapped(parts, ("zh", "y", "zl"))
    state = around(state, "x")
    state = call(
        order_kernel,
        "order",
        shape(64, 3, 4, KV * HD, dtype=f32),
        [place, old_owner],
        state,
        [pltpu.SMEM((16,), jnp.int32)],
    )
    rows = call(sum_rows_kernel, "sum_rows", shape(32, 2, 4, KV * HD, dtype=f32), [place], [arrived, own], [])
    rows, state = lax.optimization_barrier((rows, state))
    gradient = swapped(rows, ("c", "zl", "x"))
    block = shape(4, 4, KV * HD, dtype=f32)
    return call(
        update_kernel,
        "update",
        (block, block, block, shape(4, 64, KV * HD)),
        [place, new_owner],
        [gradient, state],
        [
            pltpu.VMEM((4, 64, KV * HD), f32),
            pltpu.VMEM((64, 3, 4, KV * HD), f32),
            pltpu.SMEM((1,), jnp.int32),
        ],
    )


def solution(mesh):
    fine = Mesh(mesh.devices.reshape(2, 8, 2, 4, 4), ("zh", "y", "c", "zl", "x"))
    rep = ("zh", "y", "c")
    shard = ("zl", "x")
    tokens = P((*rep, *shard), None)
    placed = (tokens,) * 4 + (P(), P()) + (P(rep, shard, None),) * 3
    return jax.shard_map(
        local,
        mesh=fine,
        in_specs=placed,
        out_specs=(P(rep, shard, None),) * 3 + (P(rep, None, None),),
        check_vma=False,
    )
```

time: 287 us -> 209 us (0.73)
  waiting for transfers between devices: 166 us -> 60.4 us
  starting transfers between devices: 73.3 us -> 91.4 us
  Pallas kernels: 12.9 us -> 23.3 us
  local copies, waits for them, and re-layouts: 15.5 us -> 7.39 us
  blocking collectives: 16.9 us -> 21.4 us
    all_to_all x10 -> x4, waiting for transfers between devices: 166 us -> 0.01 us  [swapped(): return lax.all_to_all(x, axes, split_axis=0, concat_axis=0, tiled=True)]
    ppermute x0 -> x16, waiting for transfers between devices: none -> 60.4 us  [shifted(): return lax.ppermute(x, axis, [(i, (i + k) % n) for i in range(n)])]
    ppermute x0 -> x16, starting transfers between devices: none -> 50.8 us  [shifted(): return lax.ppermute(x, axis, [(i, (i + k) % n) for i in range(n)])]
    all_to_all x10 -> x4, starting transfers between devices: 73.3 us -> 40.6 us  [swapped(): return lax.all_to_all(x, axes, split_axis=0, concat_axis=0, tiled=True)]
    pallas_call x3 -> x9, Pallas kernels: 12.9 us -> 23.3 us  [call(): pl.pallas_call(kernel, out_shape=out, in_specs=[SCALARS] * len(scalars) +...]
    reshape x4 -> x0, local copies, waits for them, and re-layouts: 6.64 us -> none  [the longest x1 3.16 us: local(): inputs.reshape(here, 8, 1024).transpose(1, 0, 2)]
    broadcast_in_dim x4 -> x0, local copies, waits for them, and re-layouts: 4.99 us -> none  [the longest x3 4.07 us: from_everyone(): return swapped(jnp.broadcast_to(x, (lax.axis_size(axes), *x.shape)), axes)]
    all_to_all x1, blocking collectives: 16.9 us -> 21.4 us  [swapped(): return lax.all_to_all(x, axes, split_axis=0, concat_axis=0, tiled=True)]
  transfers between devices with their start and end apart: 10 -> 20, of which waited for: 10 -> 9; matrix products, arithmetic and copies ran while one was open for 2% -> 2% of each run, Pallas kernels for 0% -> 5%
where the time goes in v2:
time: 209 us; the launch traced here: 208 us
  starting transfers between devices  91.4 us (44%)
  waiting for transfers between devices  60.4 us (29%)
  Pallas kernels  23.3 us (11%)
  blocking collectives  21.4 us (10%)
  local copies, waits for them, and re-layouts  7.39 us (4%)
  other arithmetic  2.74 us (1%)
    ppermute x16, waiting for transfers between devices, shifted(): return lax.ppermute(x, axis, [(i, (i + k) % n) for i in range(n)])  60.4 us
    ppermute x16, starting transfers between devices, shifted(): return lax.ppermute(x, axis, [(i, (i + k) % n) for i in range(n)])  50.8 us
    all_to_all x4, starting transfers between devices, swapped(): return lax.all_to_all(x, axes, split_axis=0, concat_axis=0, tiled=True)  40.6 us
    pallas_call x9, Pallas kernels, call(): pl.pallas_call(kernel, out_shape=out, in_specs=[SCALARS] * len(scalars) +...  23.3 us
    all_to_all x1, blocking collectives, swapped(): return lax.all_to_all(x, axes, split_axis=0, concat_axis=0, tiled=True)  21.4 us
  transfers between devices with their start and end apart: 20, of which 9 were waited for; matrix products, arithmetic and copies ran while one was open for 2% of the time, Pallas kernels for 5%

profile of v2, /device:TPU:1, one launch (start us, length us, event | category | flops | bytes accessed | tf_op | source)
XLA Modules:
  0.0 207.6 jit_solution(10854063266343393697)
XLA Ops:
  2.7 10.4 %all-to-all-start = ((bf16[16,128,128]{2,1,0:T(8,128)(2,1)}), bf16[16,128,128]{2,1,0:T(8,128)(2,1)}, u32[]{:S(2)}, u32[]{:S(2)}) async-start(bf16[16,128,128]{2,1,0:T(8,128)(2,1)} %bitcast.37), calls=%async_computation | async-start | bytes 1048576 | tf_op jit(solution)/shard_map/all_to_all | solution.py:33
  15.9 2.9 %collective-permute-start.3 = (bf16[4,128,1024]{2,1,0:T(8,128)(2,1)}, bf16[4,128,1024]{2,1,0:T(8,128)(2,1)}, u32[]{:S(2)}, u32[]{:S(2)}) collective-permute-start(bf16[4,128,1024]{2,1,0:T(8,128)(2,1)} %get-tuple-element.36), channel_id=1, source_target_pairs={{0,16},{16,0},{1,17},{17,1},{2,18},{18,2},{3,19},{19,3},{4,20},{20... | collective-permute-start | bytes 3145736 | tf_op jit(solution)/shard_map/ppermute | solution.py:38
  19.5 3.5 %collective-permute-start.4 = (bf16[128,1024]{1,0:T(8,128)(2,1)S(1)}, bf16[128,1024]{1,0:T(8,128)(2,1)S(1)}, u32[]{:S(2)}, u32[]{:S(2)}) collective-permute-start(bf16[128,1024]{1,0:T(8,128)(2,1)S(1)} %get-tuple-element.38), channel_id=1, source_target_pairs={{0,1},{1,2},{2,3},{3,0},{4,5},{5,6},{6,7},{7,4},{8,9},{9,10},{10,1... | collective-permute-start | bytes 786440 | tf_op jit(solution)/shard_map/ppermute | solution.py:38
  23.0 4.3 %collective-permute-start.5 = (bf16[128,1024]{1,0:T(8,128)(2,1)S(1)}, bf16[128,1024]{1,0:T(8,128)(2,1)S(1)}, u32[]{:S(2)}, u32[]{:S(2)}) collective-permute-start(bf16[128,1024]{1,0:T(8,128)(2,1)S(1)} %get-tuple-element.39), channel_id=1, source_target_pairs={{0,2},{1,3},{2,0},{3,1},{4,6},{5,7},{6,4},{7,5},{8,10},{9,11},{10,... | collective-permute-start | bytes 786440 | tf_op jit(solution)/shard_map/ppermute | solution.py:38
  27.3 3.1 %collective-permute-start.6 = (bf16[128,1024]{1,0:T(8,128)(2,1)S(1)}, bf16[128,1024]{1,0:T(8,128)(2,1)S(1)}, u32[]{:S(2)}, u32[]{:S(2)}) collective-permute-start(bf16[128,1024]{1,0:T(8,128)(2,1)S(1)} %get-tuple-element.40), channel_id=1, source_target_pairs={{0,3},{1,0},{2,1},{3,2},{4,7},{5,4},{6,5},{7,6},{8,11},{9,8},{10,9... | collective-permute-start | bytes 786440 | tf_op jit(solution)/shard_map/ppermute | solution.py:38
  30.4 2.2 %collective-permute-start = (bf16[128,1024]{1,0:T(8,128)(2,1)S(1)}, bf16[128,1024]{1,0:T(8,128)(2,1)S(1)}, u32[]{:S(2)}, u32[]{:S(2)}) collective-permute-start(bf16[128,1024]{1,0:T(8,128)(2,1)S(1)} %get-tuple-element.32), channel_id=1, source_target_pairs={{0,1},{1,2},{2,3},{3,0},{4,5},{5,6},{6,7},{7,4},{8,9},{9,10},{10,1... | collective-permute-start | bytes 786440 | tf_op jit(solution)/shard_map/ppermute | solution.py:38
  32.6 2.8 %collective-permute-start.1 = (bf16[128,1024]{1,0:T(8,128)(2,1)S(1)}, bf16[128,1024]{1,0:T(8,128)(2,1)S(1)}, u32[]{:S(2)}, u32[]{:S(2)}) collective-permute-start(bf16[128,1024]{1,0:T(8,128)(2,1)S(1)} %get-tuple-element.33), channel_id=1, source_target_pairs={{0,2},{1,3},{2,0},{3,1},{4,6},{5,7},{6,4},{7,5},{8,10},{9,11},{10,... | collective-permute-start | bytes 786440 | tf_op jit(solution)/shard_map/ppermute | solution.py:38
  35.4 3.2 %collective-permute-done.5.r2 = bf16[128,1024]{1,0:T(8,128)(2,1)S(1)} collective-permute-done((bf16[128,1024]{1,0:T(8,128)(2,1)S(1)}, bf16[128,1024]{1,0:T(8,128)(2,1)S(1)}, u32[]{:S(2)}, u32[]{:S(2)}) %collective-permute-start.5) | collective-permute-done | bytes 262176 | tf_op jit(solution)/shard_map/ppermute | solution.py:38
  40.6 3.2 %values.2.refs_0_ = f32[2048,128]{1,0:T(8,128)S(1)} custom-call(s32[5]{0:T(128)S(1)} %stack.50.place, bf16[2048,128]{1,0:T(8,128)(2,1)} %bitcast.13.k_ref, bf16[128,1024]{1,0:T(8,128)(2,1)S(1)} %get-tuple-element.37.r0, bf16[128,1024]{1,0:T(8,128)(2,1)S(1)} %collective-permute-done.4.r1, bf16[128,1024]{1,0:T(8,128)(2,1)S(1)} %collective-permute-done.5.r2, ...), custom_call_target="tpu_custom_call" | custom-call | flops 6000000000 | bytes 4194304 | tf_op jit(solution)/shard_map/values/pallas_call | solution.py:50
  44.5 5.4 %collective-permute-done.1.r2 = bf16[128,1024]{1,0:T(8,128)(2,1)S(1)} collective-permute-done((bf16[128,1024]{1,0:T(8,128)(2,1)S(1)}, bf16[128,1024]{1,0:T(8,128)(2,1)S(1)}, u32[]{:S(2)}, u32[]{:S(2)}) %collective-permute-start.1) | collective-permute-done | bytes 262176 | tf_op jit(solution)/shard_map/ppermute | solution.py:38
  49.9 4.4 %values.3 = (bf16[4,512,128]{2,1,0:T(8,128)(2,1)}, f32[512,128]{1,0:T(8,128)S(1)}) custom-call(s32[5]{0:T(128)S(1)} %stack.50.place, bf16[2048,128]{1,0:T(8,128)(2,1)} %bitcast.13.k_ref, bf16[128,1024]{1,0:T(8,128)(2,1)S(1)} %get-tuple-element.31.r0, bf16[128,1024]{1,0:T(8,128)(2,1)S(1)} %collective-permute-done.r1, ...), custom_call_target="tpu_custom_call" | custom-call | flops 6000000000 | bytes 4194304 | tf_op jit(solution)/shard_map/values/pallas_call | solution.py:50
  54.3 9.8 %all-to-all-start.1 = ((bf16[4,512,128]{2,1,0:T(8,128)(2,1)}), bf16[4,512,128]{2,1,0:T(8,128)(2,1)S(1)}, u32[]{:S(2)}, u32[]{:S(2)}) async-start(bf16[4,512,128]{2,1,0:T(8,128)(2,1)} %get-tuple-element.42), calls=%async_computation.1 | async-start | bytes 1048576 | tf_op jit(solution)/shard_map/all_to_all | solution.py:33
  66.3 5.0 %collective-permute-start.10 = (bf16[256,1024]{1,0:T(8,128)(2,1)}, bf16[256,1024]{1,0:T(8,128)(2,1)S(1)}, u32[]{:S(2)}, u32[]{:S(2)}) collective-permute-start(bf16[256,1024]{1,0:T(8,128)(2,1)} %pad_maximum_fusion.2), channel_id=1, source_target_pairs={{0,1},{1,2},{2,3},{3,0},{4,5},{5,6},{6,7},{7,4},{8,9},{9,10},{10,1... | collective-permute-start | bytes 1572872 | tf_op jit(solution)/shard_map/ppermute | solution.py:38
  72.1 2.9 %collective-permute-start.11 = (bf16[256,1024]{1,0:T(8,128)(2,1)}, bf16[256,1024]{1,0:T(8,128)(2,1)S(1)}, u32[]{:S(2)}, u32[]{:S(2)}) collective-permute-start(bf16[256,1024]{1,0:T(8,128)(2,1)} %pad_maximum_fusion.3), channel_id=1, source_target_pairs={{0,2},{1,3},{2,0},{3,1},{4,6},{5,7},{6,4},{7,5},{8,10},{9,11},{10,... | collective-permute-start | bytes 1572872 | tf_op jit(solution)/shard_map/ppermute | solution.py:38
  75.8 3.3 %collective-permute-start.12 = (bf16[256,1024]{1,0:T(8,128)(2,1)}, bf16[256,1024]{1,0:T(8,128)(2,1)S(1)}, u32[]{:S(2)}, u32[]{:S(2)}) collective-permute-start(bf16[256,1024]{1,0:T(8,128)(2,1)} %pad_maximum_fusion.4), channel_id=1, source_target_pairs={{0,3},{1,0},{2,1},{3,2},{4,7},{5,4},{6,5},{7,6},{8,11},{9,8},{10,9... | collective-permute-start | bytes 1572872 | tf_op jit(solution)/shard_map/ppermute | solution.py:38
  80.9 13.4 %collective-permute-done.11.i2 = bf16[256,1024]{1,0:T(8,128)(2,1)S(1)} collective-permute-done((bf16[256,1024]{1,0:T(8,128)(2,1)}, bf16[256,1024]{1,0:T(8,128)(2,1)S(1)}, u32[]{:S(2)}, u32[]{:S(2)}) %collective-permute-start.11) | collective-permute-done | bytes 524320 | tf_op jit(solution)/shard_map/ppermute | solution.py:38
  96.9 6.6 %all-to-all-start.2 = ((bf16[8,512,128]{2,1,0:T(8,128)(2,1)}), bf16[8,512,128]{2,1,0:T(8,128)(2,1)S(1)}, u32[]{:S(2)}, u32[]{:S(2)}) async-start(bf16[8,512,128]{2,1,0:T(8,128)(2,1)} %sum_values.1), calls=%async_computation.2 | async-start | bytes 2097152 | tf_op jit(solution)/shard_map/all_to_all | solution.py:33
  103.6 5.2 %collective-permute-start.9 = (f32[3,6,4,512]{3,2,1,0:T(4,128)S(1)}, f32[3,6,4,512]{3,2,1,0:T(4,128)S(1)}, u32[]{:S(2)}, u32[]{:S(2)}) collective-permute-start(f32[3,6,4,512]{3,2,1,0:T(4,128)S(1)} %pad_maximum_fusion.5), channel_id=1, source_target_pairs={{0,12},{4,0},{8,4},{12,8},{1,13},{5,1},{9,5},{13,9},{2,14},{6,2},{... | collective-permute-start | bytes 442376 | tf_op jit(solution)/shard_map/ppermute | solution.py:38
  108.7 1.9 collective-permute-start.8
  110.7 2.5 %collective-permute-start.7 = (f32[3,6,4,512]{3,2,1,0:T(4,128)S(1)}, f32[3,6,4,512]{3,2,1,0:T(4,128)S(1)}, u32[]{:S(2)}, u32[]{:S(2)}) collective-permute-start(f32[3,6,4,512]{3,2,1,0:T(4,128)S(1)} %pad_maximum_fusion.5), channel_id=1, source_target_pairs={{0,4},{4,8},{8,12},{12,0},{1,5},{5,9},{9,13},{13,1},{2,6},{6,10},{... | collective-permute-start | bytes 442376 | tf_op jit(solution)/shard_map/ppermute | solution.py:38
  113.2 9.7 %collective-permute-done.8 = f32[3,6,4,512]{3,2,1,0:T(4,128)S(1)} collective-permute-done((f32[3,6,4,512]{3,2,1,0:T(4,128)S(1)}, f32[3,6,4,512]{3,2,1,0:T(4,128)S(1)}, u32[]{:S(2)}, u32[]{:S(2)}) %collective-permute-start.8) | collective-permute-done | bytes 147488 | tf_op jit(solution)/shard_map/ppermute | solution.py:38
  125.1 3.7 %gradient.1 = (bf16[64,16,512]{2,1,0:T(8,128)(2,1)}, f32[16,512]{1,0:T(8,128)S(1)}) custom-call(s32[5]{0:T(128)S(1)} %stack.50.place, bf16[256,1024]{1,0:T(8,128)(2,1)S(1)} %pad_maximum_fusion.1.i0, bf16[256,1024]{1,0:T(8,128)(2,1)S(1)} %collective-permute-done.10.i1, bf16[256,1024]{1,0:T(8,128)(2,1)S(1)} %copy-done.8, bf16[256,1024]{1,0:T(8,128)(2,1)S(1)} %copy-done.10, ...), custom_call_target="tpu_custom_call" | custom-call | flops 2000000000 | bytes 4194304 | tf_op jit(solution)/shard_map/gradient/pallas_call | solution.py:50
  128.8 13.7 %all-to-all-start.3 = ((bf16[64,16,512]{2,1,0:T(8,128)(2,1)}), bf16[64,16,512]{2,1,0:T(8,128)(2,1)S(1)}, u32[]{:S(2)}, u32[]{:S(2)}) async-start(bf16[64,16,512]{2,1,0:T(8,128)(2,1)} %get-tuple-element.53), calls=%async_computation.3 | async-start | bytes 2097152 | tf_op jit(solution)/shard_map/all_to_all | solution.py:33
  142.6 4.5 %collective-permute-start.15 = (f32[4,3,6,4,512]{4,3,2,1,0:T(4,128)S(1)}, f32[4,3,6,4,512]{4,3,2,1,0:T(4,128)S(1)}, u32[]{:S(2)}, u32[]{:S(2)}) collective-permute-start(f32[4,3,6,4,512]{4,3,2,1,0:T(4,128)S(1)} %pad_maximum_fusion.s0), channel_id=1, source_target_pairs={{0,3},{1,0},{2,1},{3,2},{4,7},{5,4},{6,5},{7,6},{8,11},{9,8},{10,9... | collective-permute-start | bytes 1769480 | tf_op jit(solution)/shard_map/ppermute | solution.py:38
  147.0 2.5 %collective-permute-start.14 = (f32[4,3,6,4,512]{4,3,2,1,0:T(4,128)S(1)}, f32[4,3,6,4,512]{4,3,2,1,0:T(4,128)S(1)}, u32[]{:S(2)}, u32[]{:S(2)}) collective-permute-start(f32[4,3,6,4,512]{4,3,2,1,0:T(4,128)S(1)} %pad_maximum_fusion.s0), channel_id=1, source_target_pairs={{0,2},{1,3},{2,0},{3,1},{4,6},{5,7},{6,4},{7,5},{8,10},{9,11},{10,... | collective-permute-start | bytes 1769480 | tf_op jit(solution)/shard_map/ppermute | solution.py:38
  149.5 2.5 %collective-permute-start.13 = (f32[4,3,6,4,512]{4,3,2,1,0:T(4,128)S(1)}, f32[4,3,6,4,512]{4,3,2,1,0:T(4,128)S(1)}, u32[]{:S(2)}, u32[]{:S(2)}) collective-permute-start(f32[4,3,6,4,512]{4,3,2,1,0:T(4,128)S(1)} %pad_maximum_fusion.s0), channel_id=1, source_target_pairs={{0,1},{1,2},{2,3},{3,0},{4,5},{5,6},{6,7},{7,4},{8,9},{9,10},{10,1... | collective-permute-start | bytes 1769480 | tf_op jit(solution)/shard_map/ppermute | solution.py:38
  152.0 7.7 %collective-permute-done.15.s3 = f32[4,3,6,4,512]{4,3,2,1,0:T(4,128)S(1)} collective-permute-done((f32[4,3,6,4,512]{4,3,2,1,0:T(4,128)S(1)}, f32[4,3,6,4,512]{4,3,2,1,0:T(4,128)S(1)}, u32[]{:S(2)}, u32[]{:S(2)}) %collective-permute-start.15) | collective-permute-done | bytes 589856 | tf_op jit(solution)/shard_map/ppermute | solution.py:38
  159.8 4.5 %collective-permute-done.14.s2 = f32[4,3,6,4,512]{4,3,2,1,0:T(4,128)S(1)} collective-permute-done((f32[4,3,6,4,512]{4,3,2,1,0:T(4,128)S(1)}, f32[4,3,6,4,512]{4,3,2,1,0:T(4,128)S(1)}, u32[]{:S(2)}, u32[]{:S(2)}) %collective-permute-start.14) | collective-permute-done | bytes 589856 | tf_op jit(solution)/shard_map/ppermute | solution.py:38
  164.3 14.1 %collective-permute-done.13.s1 = f32[4,3,6,4,512]{4,3,2,1,0:T(4,128)S(1)} collective-permute-done((f32[4,3,6,4,512]{4,3,2,1,0:T(4,128)S(1)}, f32[4,3,6,4,512]{4,3,2,1,0:T(4,128)S(1)}, u32[]{:S(2)}, u32[]{:S(2)}) %collective-permute-start.13) | collective-permute-done | bytes 589856 | tf_op jit(solution)/shard_map/ppermute | solution.py:38
  178.3 3.3 %order.1.st_ref = f32[64,3,4,512]{3,2,1,0:T(4,128)S(1)} custom-call(s32[5]{0:T(128)S(1)} %stack.50.place, s32[64]{0:T(128)S(1)} %copy-done.5, f32[4,3,6,4,512]{4,3,2,1,0:T(4,128)S(1)} %pad_maximum_fusion.s0, f32[4,3,6,4,512]{4,3,2,1,0:T(4,128)S(1)} %collective-permute-done.13.s1, f32[4,3,6,4,512]{4,3,2,1,0:T(4,128)S(1)} %collective-permute-done.14.s2, ...), custom_call_target="tpu_custom_call" | custom-call | flops 1000000 | bytes 4194304 | tf_op jit(solution)/shard_map/order/pallas_call | solution.py:50
  182.4 21.4 %all_to_all.25.g_ref = f32[32,2,4,512]{3,2,1,0:T(4,128)S(1)} all-to-all(f32[32,2,4,512]{3,2,1,0:T(4,128)S(1)} %sum_rows.1), channel_id=1, replica_groups=mesh['zh'=2,'y'=8,'c'=2,'zl'=4,'x'=4] {'c','zl','x'}, dimensions={0} | all-to-all | bytes 1048576 | tf_op jit(solution)/shard_map/all_to_all | solution.py:33
  203.8 3.9 %update.1 = (f32[4,4,512]{2,1,0:T(4,128)}, f32[4,4,512]{2,1,0:T(4,128)}, f32[4,4,512]{2,1,0:T(4,128)}, bf16[4,64,512]{2,1,0:T(8,128)(2,1)}) custom-call(s32[5]{0:T(128)S(1)} %stack.50.place, s32[64]{0:T(128)S(1)} %copy-done.6, f32[32,2,4,512]{3,2,1,0:T(4,128)S(1)} %all_to_all.25.g_ref, f32[64,3,4,512]{3,2,1,0:T(4,128)S(1)} %order.1.st_ref), custom_call_target="tpu_custom_call" | custom-call | flops 1000000 | bytes 4194304 | tf_op jit(solution)/shard_map/update/pallas_call | solution.py:50
  (57 shorter events, 19.2 us)
Async XLA Ops:
  0.6 12.6 %copy-start = (bf16[128,8192]{1,0:T(8,128)(2,1)S(1)}, bf16[128,8192]{1,0:T(8,128)(2,1)}, u32[]{:S(2)}) copy-start(bf16[128,8192]{1,0:T(8,128)(2,1)} %in_ref.1) | copy-start | bytes 6291460
  1.7 17.0 %copy-start.1 = (bf16[128,4096]{1,0:T(8,128)(2,1)S(1)}, bf16[128,4096]{1,0:T(8,128)(2,1)}, u32[]{:S(2)}) copy-start(bf16[128,4096]{1,0:T(8,128)(2,1)} %q_ref.1) | copy-start | bytes 3145732
  2.7 37.9 %all-to-all-start = ((bf16[16,128,128]{2,1,0:T(8,128)(2,1)}), bf16[16,128,128]{2,1,0:T(8,128)(2,1)}, u32[]{:S(2)}, u32[]{:S(2)}) async-start(bf16[16,128,128]{2,1,0:T(8,128)(2,1)} %bitcast.37), calls=%async_computation | async-start | bytes 1048576 | tf_op jit(solution)/shard_map/all_to_all | solution.py:33
  13.2 5.5 %copy-start.2 = (bf16[128,4096]{1,0:T(8,128)(2,1)S(1)}, bf16[128,4096]{1,0:T(8,128)(2,1)}, u32[]{:S(2)}) copy-start(bf16[128,4096]{1,0:T(8,128)(2,1)} %d_ref.1) | copy-start | bytes 3145732
  15.9 28.0 %collective-permute-start.3 = (bf16[4,128,1024]{2,1,0:T(8,128)(2,1)}, bf16[4,128,1024]{2,1,0:T(8,128)(2,1)}, u32[]{:S(2)}, u32[]{:S(2)}) collective-permute-start(bf16[4,128,1024]{2,1,0:T(8,128)(2,1)} %get-tuple-element.36), channel_id=1, source_target_pairs={{0,16},{16,0},{1,17},{17,1},{2,18},{18,2},{3,19},{19,3},{4,20},{20... | collective-permute-start | bytes 3145736 | tf_op jit(solution)/shard_map/ppermute | solution.py:38
  19.5 13.1 %collective-permute-start.4 = (bf16[128,1024]{1,0:T(8,128)(2,1)S(1)}, bf16[128,1024]{1,0:T(8,128)(2,1)S(1)}, u32[]{:S(2)}, u32[]{:S(2)}) collective-permute-start(bf16[128,1024]{1,0:T(8,128)(2,1)S(1)} %get-tuple-element.38), channel_id=1, source_target_pairs={{0,1},{1,2},{2,3},{3,0},{4,5},{5,6},{6,7},{7,4},{8,9},{9,10},{10,1... | collective-permute-start | bytes 786440 | tf_op jit(solution)/shard_map/ppermute | solution.py:38
  23.0 15.7 %collective-permute-start.5 = (bf16[128,1024]{1,0:T(8,128)(2,1)S(1)}, bf16[128,1024]{1,0:T(8,128)(2,1)S(1)}, u32[]{:S(2)}, u32[]{:S(2)}) collective-permute-start(bf16[128,1024]{1,0:T(8,128)(2,1)S(1)} %get-tuple-element.39), channel_id=1, source_target_pairs={{0,2},{1,3},{2,0},{3,1},{4,6},{5,7},{6,4},{7,5},{8,10},{9,11},{10,... | collective-permute-start | bytes 786440 | tf_op jit(solution)/shard_map/ppermute | solution.py:38
  27.3 13.3 %collective-permute-start.6 = (bf16[128,1024]{1,0:T(8,128)(2,1)S(1)}, bf16[128,1024]{1,0:T(8,128)(2,1)S(1)}, u32[]{:S(2)}, u32[]{:S(2)}) collective-permute-start(bf16[128,1024]{1,0:T(8,128)(2,1)S(1)} %get-tuple-element.40), channel_id=1, source_target_pairs={{0,3},{1,0},{2,1},{3,2},{4,7},{5,4},{6,5},{7,6},{8,11},{9,8},{10,9... | collective-permute-start | bytes 786440 | tf_op jit(solution)/shard_map/ppermute | solution.py:38
  30.4 14.1 %collective-permute-start = (bf16[128,1024]{1,0:T(8,128)(2,1)S(1)}, bf16[128,1024]{1,0:T(8,128)(2,1)S(1)}, u32[]{:S(2)}, u32[]{:S(2)}) collective-permute-start(bf16[128,1024]{1,0:T(8,128)(2,1)S(1)} %get-tuple-element.32), channel_id=1, source_target_pairs={{0,1},{1,2},{2,3},{3,0},{4,5},{5,6},{6,7},{7,4},{8,9},{9,10},{10,1... | collective-permute-start | bytes 786440 | tf_op jit(solution)/shard_map/ppermute | solution.py:38
  32.6 17.3 %collective-permute-start.1 = (bf16[128,1024]{1,0:T(8,128)(2,1)S(1)}, bf16[128,1024]{1,0:T(8,128)(2,1)S(1)}, u32[]{:S(2)}, u32[]{:S(2)}) collective-permute-start(bf16[128,1024]{1,0:T(8,128)(2,1)S(1)} %get-tuple-element.33), channel_id=1, source_target_pairs={{0,2},{1,3},{2,0},{3,1},{4,6},{5,7},{6,4},{7,5},{8,10},{9,11},{10,... | collective-permute-start | bytes 786440 | tf_op jit(solution)/shard_map/ppermute | solution.py:38
  38.7 11.2 %collective-permute-start.2 = (bf16[128,1024]{1,0:T(8,128)(2,1)S(1)}, bf16[128,1024]{1,0:T(8,128)(2,1)S(1)}, u32[]{:S(2)}, u32[]{:S(2)}) collective-permute-start(bf16[128,1024]{1,0:T(8,128)(2,1)S(1)} %get-tuple-element.34), channel_id=1, source_target_pairs={{0,3},{1,0},{2,1},{3,2},{4,7},{5,4},{6,5},{7,6},{8,11},{9,8},{10,9... | collective-permute-start | bytes 786440 | tf_op jit(solution)/shard_map/ppermute | solution.py:38
  49.9 14.2 %copy-start.4 = (bf16[4,128,1024]{2,1,0:T(8,128)(2,1)S(1)}, bf16[4,128,1024]{2,1,0:T(8,128)(2,1)}, u32[]{:S(2)}) copy-start(bf16[4,128,1024]{2,1,0:T(8,128)(2,1)} %copy-done.3) | copy-start | bytes 3145732
  54.3 25.0 %all-to-all-start.1 = ((bf16[4,512,128]{2,1,0:T(8,128)(2,1)}), bf16[4,512,128]{2,1,0:T(8,128)(2,1)S(1)}, u32[]{:S(2)}, u32[]{:S(2)}) async-start(bf16[4,512,128]{2,1,0:T(8,128)(2,1)} %get-tuple-element.42), calls=%async_computation.1 | async-start | bytes 1048576 | tf_op jit(solution)/shard_map/all_to_all | solution.py:33
  66.3 14.6 %collective-permute-start.10 = (bf16[256,1024]{1,0:T(8,128)(2,1)}, bf16[256,1024]{1,0:T(8,128)(2,1)S(1)}, u32[]{:S(2)}, u32[]{:S(2)}) collective-permute-start(bf16[256,1024]{1,0:T(8,128)(2,1)} %pad_maximum_fusion.2), channel_id=1, source_target_pairs={{0,1},{1,2},{2,3},{3,0},{4,5},{5,6},{6,7},{7,4},{8,9},{9,10},{10,1... | collective-permute-start | bytes 1572872 | tf_op jit(solution)/shard_map/ppermute | solution.py:38
  72.1 22.2 %collective-permute-start.11 = (bf16[256,1024]{1,0:T(8,128)(2,1)}, bf16[256,1024]{1,0:T(8,128)(2,1)S(1)}, u32[]{:S(2)}, u32[]{:S(2)}) collective-permute-start(bf16[256,1024]{1,0:T(8,128)(2,1)} %pad_maximum_fusion.3), channel_id=1, source_target_pairs={{0,2},{1,3},{2,0},{3,1},{4,6},{5,7},{6,4},{7,5},{8,10},{9,11},{10,... | collective-permute-start | bytes 1572872 | tf_op jit(solution)/shard_map/ppermute | solution.py:38
  75.8 21.0 %collective-permute-start.12 = (bf16[256,1024]{1,0:T(8,128)(2,1)}, bf16[256,1024]{1,0:T(8,128)(2,1)S(1)}, u32[]{:S(2)}, u32[]{:S(2)}) collective-permute-start(bf16[256,1024]{1,0:T(8,128)(2,1)} %pad_maximum_fusion.4), channel_id=1, source_target_pairs={{0,3},{1,0},{2,1},{3,2},{4,7},{5,4},{6,5},{7,6},{8,11},{9,8},{10,9... | collective-permute-start | bytes 1572872 | tf_op jit(solution)/shard_map/ppermute | solution.py:38
  79.2 24.3 %copy-start.11 = (f32[4,6,512]{2,0,1:T(4,128)S(1)}, f32[4,6,512]{2,0,1:T(4,128)}, u32[]{:S(2)}) copy-start(f32[4,6,512]{2,0,1:T(4,128)} %param.17) | copy-start | bytes 147460
  79.2 24.3 %copy-start.12 = (f32[4,6,512]{2,0,1:T(4,128)S(1)}, f32[4,6,512]{2,0,1:T(4,128)}, u32[]{:S(2)}) copy-start(f32[4,6,512]{2,0,1:T(4,128)} %param.16) | copy-start | bytes 147460
  79.2 24.3 %copy-start.13 = (f32[4,6,512]{2,0,1:T(4,128)S(1)}, f32[4,6,512]{2,0,1:T(4,128)}, u32[]{:S(2)}) copy-start(f32[4,6,512]{2,0,1:T(4,128)} %param.15) | copy-start | bytes 147460
  96.9 26.0 %copy-start.9 = (bf16[256,1024]{1,0:T(8,128)(2,1)}, bf16[256,1024]{1,0:T(8,128)(2,1)S(1)}, u32[]{:S(2)}) copy-start(bf16[256,1024]{1,0:T(8,128)(2,1)S(1)} %collective-permute-done.12.i3) | copy-start | bytes 1572868
  96.9 26.1 %all-to-all-start.2 = ((bf16[8,512,128]{2,1,0:T(8,128)(2,1)}), bf16[8,512,128]{2,1,0:T(8,128)(2,1)S(1)}, u32[]{:S(2)}, u32[]{:S(2)}) async-start(bf16[8,512,128]{2,1,0:T(8,128)(2,1)} %sum_values.1), calls=%async_computation.2 | async-start | bytes 2097152 | tf_op jit(solution)/shard_map/all_to_all | solution.py:33
  103.6 9.6 %collective-permute-start.9 = (f32[3,6,4,512]{3,2,1,0:T(4,128)S(1)}, f32[3,6,4,512]{3,2,1,0:T(4,128)S(1)}, u32[]{:S(2)}, u32[]{:S(2)}) collective-permute-start(f32[3,6,4,512]{3,2,1,0:T(4,128)S(1)} %pad_maximum_fusion.5), channel_id=1, source_target_pairs={{0,12},{4,0},{8,4},{12,8},{1,13},{5,1},{9,5},{13,9},{2,14},{6,2},{... | collective-permute-start | bytes 442376 | tf_op jit(solution)/shard_map/ppermute | solution.py:38
  108.7 14.1 %collective-permute-start.8 = (f32[3,6,4,512]{3,2,1,0:T(4,128)S(1)}, f32[3,6,4,512]{3,2,1,0:T(4,128)S(1)}, u32[]{:S(2)}, u32[]{:S(2)}) collective-permute-start(f32[3,6,4,512]{3,2,1,0:T(4,128)S(1)} %pad_maximum_fusion.5), channel_id=1, source_target_pairs={{0,8},{4,12},{8,0},{12,4},{1,9},{5,13},{9,1},{13,5},{2,10},{6,14},... | collective-permute-start | bytes 442376 | tf_op jit(solution)/shard_map/ppermute | solution.py:38
  110.7 12.1 %collective-permute-start.7 = (f32[3,6,4,512]{3,2,1,0:T(4,128)S(1)}, f32[3,6,4,512]{3,2,1,0:T(4,128)S(1)}, u32[]{:S(2)}, u32[]{:S(2)}) collective-permute-start(f32[3,6,4,512]{3,2,1,0:T(4,128)S(1)} %pad_maximum_fusion.5), channel_id=1, source_target_pairs={{0,4},{4,8},{8,12},{12,0},{1,5},{5,9},{9,13},{13,1},{2,6},{6,10},{... | collective-permute-start | bytes 442376 | tf_op jit(solution)/shard_map/ppermute | solution.py:38
  123.0 1.0 copy-start.8
  124.0 1.0 copy-start.10
  128.8 49.5 %copy-start.5 = (s32[64]{0:T(128)S(1)}, s32[64]{0:T(128)}, u32[]{:S(2)}) copy-start(s32[64]{0:T(128)} %old_owner.1) | copy-start | bytes 772
  128.8 52.8 %all-to-all-start.3 = ((bf16[64,16,512]{2,1,0:T(8,128)(2,1)}), bf16[64,16,512]{2,1,0:T(8,128)(2,1)S(1)}, u32[]{:S(2)}, u32[]{:S(2)}) async-start(bf16[64,16,512]{2,1,0:T(8,128)(2,1)} %get-tuple-element.53), calls=%async_computation.3 | async-start | bytes 2097152 | tf_op jit(solution)/shard_map/all_to_all | solution.py:33
  142.6 17.2 %collective-permute-start.15 = (f32[4,3,6,4,512]{4,3,2,1,0:T(4,128)S(1)}, f32[4,3,6,4,512]{4,3,2,1,0:T(4,128)S(1)}, u32[]{:S(2)}, u32[]{:S(2)}) collective-permute-start(f32[4,3,6,4,512]{4,3,2,1,0:T(4,128)S(1)} %pad_maximum_fusion.s0), channel_id=1, source_target_pairs={{0,3},{1,0},{2,1},{3,2},{4,7},{5,4},{6,5},{7,6},{8,11},{9,8},{10,9... | collective-permute-start | bytes 1769480 | tf_op jit(solution)/shard_map/ppermute | solution.py:38
  147.0 17.2 %collective-permute-start.14 = (f32[4,3,6,4,512]{4,3,2,1,0:T(4,128)S(1)}, f32[4,3,6,4,512]{4,3,2,1,0:T(4,128)S(1)}, u32[]{:S(2)}, u32[]{:S(2)}) collective-permute-start(f32[4,3,6,4,512]{4,3,2,1,0:T(4,128)S(1)} %pad_maximum_fusion.s0), channel_id=1, source_target_pairs={{0,2},{1,3},{2,0},{3,1},{4,6},{5,7},{6,4},{7,5},{8,10},{9,11},{10,... | collective-permute-start | bytes 1769480 | tf_op jit(solution)/shard_map/ppermute | solution.py:38
  149.5 28.8 %collective-permute-start.13 = (f32[4,3,6,4,512]{4,3,2,1,0:T(4,128)S(1)}, f32[4,3,6,4,512]{4,3,2,1,0:T(4,128)S(1)}, u32[]{:S(2)}, u32[]{:S(2)}) collective-permute-start(f32[4,3,6,4,512]{4,3,2,1,0:T(4,128)S(1)} %pad_maximum_fusion.s0), channel_id=1, source_target_pairs={{0,1},{1,2},{2,3},{3,0},{4,5},{5,6},{6,7},{7,4},{8,9},{9,10},{10,1... | collective-permute-start | bytes 1769480 | tf_op jit(solution)/shard_map/ppermute | solution.py:38
  181.6 22.1 %copy-start.6 = (s32[64]{0:T(128)S(1)}, s32[64]{0:T(128)}, u32[]{:S(2)}) copy-start(s32[64]{0:T(128)} %new_owner.1) | copy-start | bytes 772
  (2 other events, 1.8 us)

commit v3 on v2

v3 whole, which is shorter than its diff:
```python
import functools

import jax
import jax.numpy as jnp
from jax import lax
from jax.experimental import pallas as pl
from jax.experimental.pallas import tpu as pltpu
from jax.sharding import Mesh, PartitionSpec as P

KV = 4
HD = 128
GRP = 8
STEP = 1000
LOG2E = 1.4426950408889634
MIB = 1 << 20

beta_first = 0.9
beta_second = 0.95
learning_rate = 0.02
decay_rate = 0.1
epsilon = 1e-08

PLANE = 512
CHUNK = 256
QUERIES = 256
FIRST, SECOND = (0, 1), (3, 2)
ZH, Y, C, ZL, X = range(5)
WHOLE = pl.BlockSpec(memory_space=pltpu.VMEM)
ELSEWHERE = pl.BlockSpec(memory_space=pl.ANY)
SCALARS = pl.BlockSpec(memory_space=pltpu.SMEM)
NT = (((1,), (1,)), ((), ()))
TN = (((0,), (0,)), ((), ()))


def swapped(x, axes):
    return lax.all_to_all(x, axes, split_axis=0, concat_axis=0, tiled=True)


def shifted(x, axis, k):
    n = lax.axis_size(axis)
    return lax.ppermute(x, axis, [(i, (i + k) % n) for i in range(n)])


def sent_down(x, k):
    return lax.ppermute(x, "zl", [(i, i - k) for i in range(k, 4)])


def old_planes(x, k):
    return lax.ppermute(x, "zl", [(i, (i + k) % 4) for i in range(3)])


def call(kernel, name, out, scalars, arrays, scratch, behind=(), limit=20):
    given = len(scalars) + len(arrays)

    def body(*refs):
        kernel(*refs[:given], *refs[given + len(behind) :])

    return pl.pallas_call(
        body,
        out_shape=out,
        in_specs=[SCALARS] * len(scalars) + [WHOLE] * len(arrays) + [ELSEWHERE] * len(behind),
        out_specs=jax.tree.map(lambda _: WHOLE, out),
        scratch_shapes=scratch,
        compiler_params=pltpu.CompilerParams(vmem_limit_bytes=limit * MIB),
        cost_estimate=pl.CostEstimate(flops=1, bytes_accessed=1024, transcendentals=0),
        name=name,
    )(*scalars, *arrays, *behind)


def shape(*dims, dtype=jnp.bfloat16):
    return jax.ShapeDtypeStruct(dims, dtype)


def pack_keys_kernel(k_ref, out_ref):
    for g in range(KV):
        part = k_ref[:, g * HD : (g + 1) * HD]
        for zl in range(4):
            out_ref[zl * 4 + g] = part


def pack_heads_kernel(place, q_ref, d_ref, *out):
    for k in range(4):
        at = pl.ds(pl.multiple_of(((place[X] + k) % 4) * GRP * HD, GRP * HD), GRP * HD)
        out[k][:, 0 : GRP * HD] = q_ref[:, at]
        out[k][:, GRP * HD :] = d_ref[:, at]


def pack_inputs_kernel(in_ref, out_ref):
    for k in range(8):
        out_ref[k] = in_ref[:, k * 1024 : (k + 1) * 1024]


def stack_kernel(*refs):
    *parts, out_ref = refs
    for k, ref in enumerate(parts):
        out_ref[k] = ref[...]


def pack_states_kernel(place, *refs):
    *from_planes, out_ref = refs
    for k, ref in enumerate(from_planes):
        plane = (place[ZL] + 4 - k) % 4

        @pl.when(plane < 3)
        def _(ref=ref, plane=plane):
            out_ref[plane] = ref[...]


def value_kernel(steps, place, k_ref, ra, rb, *refs):
    plane = place[ZL]
    factor = HD**-0.5 * LOG2E
    if steps == FIRST:
        total, q_ref, d_ref, s_a, s_b = refs
    else:
        before, own_ref, *down, q_ref, d_ref, s_a, s_b, total = refs
    width = GRP * HD
    for at, part in ((0, ra), (128, rb)):
        q_ref[at : at + 128, :] = part[:, 0:width]
        d_ref[at : at + 128, :] = part[:, width:]
    starts = [((place[X] + 4 - k) % 4) * 128 for k in steps]
    column = lax.broadcasted_iota(jnp.int32, (CHUNK, QUERIES), 1)
    position = jnp.where(column < 128, column + starts[0], column - 128 + starts[1])
    ahead = position - lax.broadcasted_iota(jnp.int32, (CHUNK, QUERIES), 0)

    def scores(h, last, s_ref):
        q = q_ref[:, pl.ds(pl.multiple_of(h * HD, HD), HD)]
        top = jnp.full((8, QUERIES), -jnp.inf, jnp.float32)
        for at in range(0, (last + 1) * PLANE, CHUNK):
            s = lax.dot_general(k_ref[at : at + CHUNK, :], q, NT, preferred_element_type=jnp.float32)
            if at >= last * PLANE:
                s = jnp.where(ahead >= at - last * PLANE, s, -jnp.inf)
            s_ref[at : at + CHUNK, :] = s
            top = jnp.maximum(top, jnp.max(s.reshape(CHUNK // 8, 8, QUERIES), axis=0))
        return jnp.max(top, axis=0, keepdims=True)

    def add_terms(h, last, s_ref, top):
        d = d_ref[:, pl.ds(pl.multiple_of(h * HD, HD), HD)]
        size = jnp.zeros((8, QUERIES), jnp.float32)
        for at in range(0, (last + 1) * PLANE, CHUNK):
            w = jnp.exp2((s_ref[at : at + CHUNK, :] - top) * factor)
            s_ref[at : at + CHUNK, :] = w
            size = size + jnp.sum(w.reshape(CHUNK // 8, 8, QUERIES), axis=0)
        inverse = 1.0 / jnp.sum(size, axis=0, keepdims=True)
        for at in range(0, (last + 1) * PLANE, CHUNK):
            p = (s_ref[at : at + CHUNK, :] * inverse).astype(jnp.bfloat16)
            total[at : at + CHUNK, :] += jnp.dot(p, d, preferred_element_type=jnp.float32)

    for last in range(4):

        @pl.when(plane == last)
        def _(last=last):
            used = slice(0, (last + 1) * PLANE)
            if steps == FIRST:
                total[used, :] = jnp.zeros(((last + 1) * PLANE, HD), jnp.float32)
            else:
                total[used, :] = before[used, :]

            @pl.loop(0, GRP // 2)
            def _(pair):
                top_a = scores(2 * pair, last, s_a)
                top_b = scores(2 * pair + 1, last, s_b)
                add_terms(2 * pair, last, s_a, top_a)
                add_terms(2 * pair + 1, last, s_b, top_b)

            if steps != FIRST:
                own_ref[...] = total[last * PLANE : (last + 1) * PLANE, :]
                for k in range(1, last + 1):
                    down[k - 1][...] = total[(last - k) * PLANE : (last - k + 1) * PLANE, :].astype(jnp.bfloat16)


def value_terms(steps, place, keys, parts, before=None, behind=()):
    total = shape(4 * PLANE, HD, dtype=jnp.float32)
    own = shape(PLANE, HD, dtype=jnp.float32)
    scratch = [
        pltpu.VMEM((QUERIES, GRP * HD), jnp.bfloat16),
        pltpu.VMEM((QUERIES, GRP * HD), jnp.bfloat16),
        pltpu.VMEM((4 * PLANE, QUERIES), jnp.float32),
        pltpu.VMEM((4 * PLANE, QUERIES), jnp.float32),
    ]
    return call(
        functools.partial(value_kernel, steps),
        "values",
        total if steps == FIRST else (own, *(shape(PLANE, HD),) * 3),
        [place],
        [keys, *(parts[k] for k in steps), *([] if before is None else [before])],
        scratch if steps == FIRST else [*scratch, pltpu.VMEM((4 * PLANE, HD), jnp.float32)],
        behind,
    )


def sum_values_kernel(own_ref, a_ref, b_ref, c_ref, out_ref):
    total = own_ref[...]
    for ref in (a_ref, b_ref, c_ref):
        total = total + ref[...].astype(jnp.float32)
    rounded = total.astype(jnp.bfloat16)
    for k in range(8):
        out_ref[k] = rounded


def gradient_kernel(place, in_ref, v_ref, out_ref, own_ref, values, rows_a, rows_b):
    for c in range(2):
        for g in range(KV):
            values[c * PLANE : (c + 1) * PLANE, g * HD : (g + 1) * HD] = v_ref[c * KV + g]

    @pl.loop(0, 4)
    def _(zl):
        for half, rows in enumerate((rows_a, rows_b)):
            lhs = in_ref[:, pl.ds(pl.multiple_of(zl * 256 + half * 128, 128), 128)]
            rows[...] = lax.dot_general(lhs, values[...], TN, preferred_element_type=jnp.float32)
        for to in range(16):
            part = jnp.concatenate([rows_a[8 * to : 8 * to + 8, :], rows_b[8 * to : 8 * to + 8, :]], axis=0)
            out_ref[to * 4 + zl] = part.astype(jnp.bfloat16)

        @pl.when(zl == place[ZL])
        def _():
            mine = pl.ds(pl.multiple_of((place[ZH] * 8 + place[Y]) * 8, 8), 8)
            own_ref[0:8, :] = rows_a[mine, :]
            own_ref[8:16, :] = rows_b[mine, :]


def sum_rows_kernel(place, in_ref, own_ref, out_ref):
    total = own_ref[...] - in_ref[place[ZH] * 32 + place[Y] * 4 + place[ZL]].astype(jnp.float32)
    for k in range(64):
        total = total + in_ref[k].astype(jnp.float32)
    for c in range(2):
        for half in range(2):
            part = total[half * 8 + c * 4 : half * 8 + c * 4 + 4, :]
            for k in range(16):
                out_ref[16 * c + k, half] = part


def order_kernel(place, old_owner, s0, s1, s2, s3, out_ref, count):
    for i in range(16):
        count[i] = 0

    @pl.loop(0, 64)
    def _(b):
        old = old_owner[b]
        slot = count[old]
        count[old] = slot + 1
        kx = (place[X] + 4 - old % 4) % 4
        for k, s_ref in enumerate((s0, s1, s2, s3)):

            @pl.when(kx == k)
            def _(s_ref=s_ref):
                for part in range(3):
                    out_ref[b, part] = s_ref[old // 4, part, slot]


def update_kernel(place, new_owner, g_ref, st_ref, p_out, f_out, s_out, w_out, w_rows, changed, count):
    @pl.loop(0, 64, unroll=4)
    def _(b):
        owner = (b // 32) * 16 + ((b // 2) % 4) * 4 + (b // 8) % 4
        gradient = g_ref[owner, b % 2]
        param = st_ref[b, 0]
        first = beta_first * st_ref[b, 1] + (1.0 - beta_first) * gradient
        second = beta_second * st_ref[b, 2] + (1.0 - beta_second) * gradient * gradient
        first_hat = first / (1.0 - beta_first**STEP)
        second_hat = second / (1.0 - beta_second**STEP)
        param = param - learning_rate * (first_hat / (jnp.sqrt(second_hat) + epsilon) + decay_rate * param)
        for i in range(4):
            w_rows[i, pl.ds(b, 1), :] = param[i : i + 1, :]
        changed[b, 0] = param
        changed[b, 1] = first
        changed[b, 2] = second

    w_out[...] = w_rows[...].astype(jnp.bfloat16)
    count[0] = 0

    @pl.loop(0, 64)
    def _(b):
        @pl.when(new_owner[b] == place[ZL] * 4 + place[X])
        def _():
            to = count[0]
            count[0] = to + 1
            for part, out in enumerate((p_out, f_out, s_out)):
                block = changed[b, part]
                for i in range(4):
                    out[i, pl.ds(to, 1), :] = block[i : i + 1, :]


def local(queries, keys, grad_out, inputs, old_owner, new_owner, param_old, first_old, second_old):
    f32 = jnp.float32
    here = queries.shape[0]
    columns = KV * HD
    place = jnp.stack([lax.axis_index(a) for a in ("zh", "y", "c", "zl", "x")]).astype(jnp.int32)

    keys_all = call(pack_keys_kernel, "pack_keys", shape(16, here, HD), [], [keys], [])
    keys_all = swapped(keys_all, ("zl", "x")).reshape(4 * PLANE, HD)
    packed = call(
        pack_heads_kernel, "pack_heads", (shape(here, 2 * GRP * HD),) * 4, [place], [queries, grad_out], []
    )
    heads = {0: packed[0], **{k: shifted(packed[k], "x", k) for k in (1, 3, 2)}}
    total = value_terms(FIRST, place, keys_all, heads)
    late = [heads[2], heads[3], total]
    packed = call(pack_inputs_kernel, "pack_inputs", shape(8, here, 1024), [], [inputs], [], late)
    pieces = swapped(packed, ("c", "x"))
    own, *parts = value_terms(SECOND, place, keys_all, heads, total, [packed])
    parts = [sent_down(parts[k - 1], k) for k in (1, 2, 3)]
    values = call(sum_values_kernel, "sum_values", shape(8, PLANE, HD), [], [own, *parts], [], [pieces])
    state = [a.transpose(1, 0, 2) for a in (param_old, first_old, second_old)]
    state = call(stack_kernel, "stack", shape(3, *state[0].shape, dtype=f32), [], state, [], [values])
    planes = [state, *(old_planes(state, k) for k in (1, 2, 3))]
    values = swapped(values, ("c", "x"))
    state = call(
        pack_states_kernel, "pack_states", shape(3, *state.shape, dtype=f32), [place], planes, []
    )
    parts, own = call(
        gradient_kernel,
        "gradient",
        (shape(64, 16, columns), shape(16, columns, dtype=f32)),
        [place],
        [pieces.reshape(2 * PLANE, 1024), values],
        [pltpu.VMEM((2 * PLANE, columns), jnp.bfloat16)] + [pltpu.VMEM((128, columns), f32)] * 2,
        planes[1:],
    )
    arrived = swapped(parts, ("zh", "y", "zl"))
    state = [state, *(shifted(state, "x", k) for k in (1, 2, 3))]
    state = call(
        order_kernel,
        "order",
        shape(64, 3, 4, columns, dtype=f32),
        [place, old_owner],
        state,
        [pltpu.SMEM((16,), jnp.int32)],
    )
    rows = call(sum_rows_kernel, "sum_rows", shape(32, 2, 4, columns, dtype=f32), [place], [arrived, own], [], [state])
    gradient = swapped(rows, ("c", "zl", "x"))
    block = shape(4, 4, columns, dtype=f32)
    return call(
        update_kernel,
        "update",
        (block, block, block, shape(4, 64, columns)),
        [place, new_owner],
        [gradient, state],
        [
            pltpu.VMEM((4, 64, columns), f32),
            pltpu.VMEM((64, 3, 4, columns), f32),
            pltpu.SMEM((1,), jnp.int32),
        ],
    )


def solution(mesh):
    fine = Mesh(mesh.devices.reshape(2, 8, 2, 4, 4), ("zh", "y", "c", "zl", "x"))
    rep = ("zh", "y", "c")
    shard = ("zl", "x")
    tokens = P((*rep, *shard), None)
    placed = (tokens,) * 4 + (P(), P()) + (P(rep, shard, None),) * 3
    return jax.shard_map(
        local,
        mesh=fine,
        in_specs=placed,
        out_specs=(P(rep, shard, None),) * 3 + (P(rep, None, None),),
        check_vma=False,
    )
```

time: 209 us -> 195 us (0.933)
  starting transfers between devices: 91.4 us -> 74.1 us
  local copies, waits for them, and re-layouts: 7.39 us -> 14.1 us
  other arithmetic: 2.74 us -> 0 us
    ppermute x16 -> x6, starting transfers between devices: 50.8 us -> 20.1 us  [shifted(): return lax.ppermute(x, axis, [(i, (i + k) % n) for i in range(n)])]
    ppermute x16 -> x6, waiting for transfers between devices: 60.4 us -> 34.2 us  [shifted(): return lax.ppermute(x, axis, [(i, (i + k) % n) for i in range(n)])]
    ppermute x0 -> x6, waiting for transfers between devices: none -> 24.9 us  [the longest x3 19.6 us: sent_down(): return lax.ppermute(x, 'zl', [(i, i - k) for i in range(k, 4)])]
    ppermute x0 -> x6, starting transfers between devices: none -> 11.7 us  [the longest x3 7.69 us: old_planes(): return lax.ppermute(x, 'zl', [(i, (i + k) % 4) for i in range(3)])]
    unnamed x28 -> x54, local copies, waits for them, and re-layouts: 3.91 us -> 14 us
    concatenate x4 -> x0, other arithmetic: 2.56 us -> none  [local(): pieces = [jnp.concatenate([kept[k], other[k]], axis=0) for k in range(4)]]
    pallas_call x9 -> x12, Pallas kernels: 23.3 us -> 23.8 us  [call(): pl.pallas_call(body, out_shape=out, in_specs=[SCALARS] * len(scalars) + [...]
  transfers between devices with their start and end apart: 20 -> 16, of which waited for: 9 -> 11; matrix products, arithmetic and copies ran while one was open for 2% -> 0% of each run, Pallas kernels for 5% -> 7%
where the time goes in v3:
time: 195 us; the launch traced here: 194 us
  starting transfers between devices  74.1 us (38%)
  waiting for transfers between devices  59.7 us (31%)
  Pallas kernels  23.8 us (12%)
  blocking collectives  21.4 us (11%)
  local copies, waits for them, and re-layouts  14.1 us (7%)
    all_to_all x4, starting transfers between devices, swapped(): return lax.all_to_all(x, axes, split_axis=0, concat_axis=0, tiled=True)  42.3 us
    ppermute x6, waiting for transfers between devices, shifted(): return lax.ppermute(x, axis, [(i, (i + k) % n) for i in range(n)])  34.2 us
    pallas_call x12, Pallas kernels, call(): pl.pallas_call(body, out_shape=out, in_specs=[SCALARS] * len(scalars) + [...  23.8 us
    all_to_all x1, blocking collectives, swapped(): return lax.all_to_all(x, axes, split_axis=0, concat_axis=0, tiled=True)  21.4 us
    ppermute x6, starting transfers between devices, shifted(): return lax.ppermute(x, axis, [(i, (i + k) % n) for i in range(n)])  20.1 us
    ppermute x3, waiting for transfers between devices, sent_down(): return lax.ppermute(x, 'zl', [(i, i - k) for i in range(k, 4)])  19.6 us
    unnamed x54, local copies, waits for them, and re-layouts  14 us
    ppermute x3, starting transfers between devices, old_planes(): return lax.ppermute(x, 'zl', [(i, (i + k) % 4) for i in range(3)])  7.69 us
  transfers between devices with their start and end apart: 16, of which 11 were waited for; matrix products, arithmetic and copies ran while one was open for 0% of the time, Pallas kernels for 7%

profile of v3, /device:TPU:1, one launch (start us, length us, event | category | flops | bytes accessed | tf_op | source)
XLA Modules:
  0.0 193.9 jit_solution(16894587857068975054)
XLA Ops:
  2.5 10.4 %all-to-all-start = ((bf16[16,128,128]{2,1,0:T(8,128)(2,1)}), bf16[16,128,128]{2,1,0:T(8,128)(2,1)S(1)}, u32[]{:S(2)}, u32[]{:S(2)}) async-start(bf16[16,128,128]{2,1,0:T(8,128)(2,1)} %pack_keys.1), calls=%async_computation | async-start | bytes 1048576 | tf_op jit(solution)/shard_map/all_to_all | solution.py:36
  14.2 1.7 pack_heads.1
  15.9 3.3 %collective-permute-start.2 = (bf16[128,2048]{1,0:T(8,128)(2,1)S(1)}, bf16[128,2048]{1,0:T(8,128)(2,1)S(1)}, u32[]{:S(2)}, u32[]{:S(2)}) collective-permute-start(bf16[128,2048]{1,0:T(8,128)(2,1)S(1)} %get-tuple-element.17), channel_id=1, source_target_pairs={{0,1},{1,2},{2,3},{3,0},{4,5},{5,6},{6,7},{7,4},{8,9},{9,10},{10,1... | collective-permute-start | bytes 1572872 | tf_op jit(solution)/shard_map/ppermute | solution.py:41
  19.2 4.3 %collective-permute-start = (bf16[128,2048]{1,0:T(8,128)(2,1)}, bf16[128,2048]{1,0:T(8,128)(2,1)S(1)}, u32[]{:S(2)}, u32[]{:S(2)}) collective-permute-start(bf16[128,2048]{1,0:T(8,128)(2,1)} %get-tuple-element.14), channel_id=1, source_target_pairs={{0,2},{1,3},{2,0},{3,1},{4,6},{5,7},{6,4},{7,5},{8,10},{9,11},{10,... | collective-permute-start | bytes 1572872 | tf_op jit(solution)/shard_map/ppermute | solution.py:41
  23.5 3.1 %collective-permute-start.1 = (bf16[128,2048]{1,0:T(8,128)(2,1)}, bf16[128,2048]{1,0:T(8,128)(2,1)S(1)}, u32[]{:S(2)}, u32[]{:S(2)}) collective-permute-start(bf16[128,2048]{1,0:T(8,128)(2,1)} %get-tuple-element.15), channel_id=1, source_target_pairs={{0,3},{1,0},{2,1},{3,2},{4,7},{5,4},{6,5},{7,6},{8,11},{9,8},{10,9... | collective-permute-start | bytes 1572872 | tf_op jit(solution)/shard_map/ppermute | solution.py:41
  26.6 8.0 %collective-permute-done.2.refs_3_ = bf16[128,2048]{1,0:T(8,128)(2,1)S(1)} collective-permute-done((bf16[128,2048]{1,0:T(8,128)(2,1)S(1)}, bf16[128,2048]{1,0:T(8,128)(2,1)S(1)}, u32[]{:S(2)}, u32[]{:S(2)}) %collective-permute-start.2) | collective-permute-done | bytes 524320 | tf_op jit(solution)/shard_map/ppermute | solution.py:41
  36.7 3.6 %values.2.refs_3_.refs_4_ = f32[2048,128]{1,0:T(8,128)S(1)} custom-call(s32[5]{0:T(128)S(1)} %stack.24.refs_0_, bf16[2048,128]{1,0:T(8,128)(2,1)S(1)} %bitcast.11, bf16[128,2048]{1,0:T(8,128)(2,1)S(1)} %get-tuple-element.16.refs_2_, bf16[128,2048]{1,0:T(8,128)(2,1)S(1)} %copy-done.17), custom_call_target="tpu_custom_call" | custom-call | flops 1 | bytes 1024 | tf_op jit(solution)/shard_map/values/pallas_call | solution.py:58
  40.3 6.2 %collective-permute-done.refs_1_.refs_3_ = bf16[128,2048]{1,0:T(8,128)(2,1)S(1)} collective-permute-done((bf16[128,2048]{1,0:T(8,128)(2,1)}, bf16[128,2048]{1,0:T(8,128)(2,1)S(1)}, u32[]{:S(2)}, u32[]{:S(2)}) %collective-permute-start) | collective-permute-done | bytes 524320 | tf_op jit(solution)/shard_map/ppermute | solution.py:41
  46.5 1.8 copy-done.2
  48.3 1.5 pack_inputs.1.refs_5_
  49.8 9.1 %all-to-all-start.1 = ((bf16[8,128,1024]{2,1,0:T(8,128)(2,1)}), bf16[8,128,1024]{2,1,0:T(8,128)(2,1)S(1)}, u32[]{:S(2)}, u32[]{:S(2)}) async-start(bf16[8,128,1024]{2,1,0:T(8,128)(2,1)} %pack_inputs.1.refs_5_), calls=%async_computation.1 | async-start | bytes 4194304 | tf_op jit(solution)/shard_map/all_to_all | solution.py:36
  62.0 3.6 %values.3 = (f32[512,128]{1,0:T(8,128)S(1)}, bf16[512,128]{1,0:T(8,128)(2,1)S(1)}, bf16[512,128]{1,0:T(8,128)(2,1)S(1)}, bf16[512,128]{1,0:T(8,128)(2,1)S(1)}) custom-call(s32[5]{0:T(128)S(1)} %stack.24.refs_0_, bf16[2048,128]{1,0:T(8,128)(2,1)S(1)} %bitcast.12, bf16[128,2048]{1,0:T(8,128)(2,1)S(1)} %copy-done.6, bf16[128,2048]{1,0:T(8,128)(2,1)S(1)} %copy-done.4, ...), custom_call_target="tpu_custom_call" | custom-call | flops 1 | bytes 1024 | tf_op jit(solution)/shard_map/values/pallas_call | solution.py:58
  65.6 1.5 collective-permute-start.3
  69.7 6.5 %collective-permute-done.3.refs_1_ = bf16[512,128]{1,0:T(8,128)(2,1)S(1)} collective-permute-done((bf16[512,128]{1,0:T(8,128)(2,1)S(1)}, bf16[512,128]{1,0:T(8,128)(2,1)S(1)}, u32[]{:S(2)}, u32[]{:S(2)}) %collective-permute-start.3) | collective-permute-done | bytes 131104 | tf_op jit(solution)/shard_map/ppermute | solution.py:45
  76.2 3.8 %collective-permute-done.4.refs_2_ = bf16[512,128]{1,0:T(8,128)(2,1)S(1)} collective-permute-done((bf16[512,128]{1,0:T(8,128)(2,1)S(1)}, bf16[512,128]{1,0:T(8,128)(2,1)S(1)}, u32[]{:S(2)}, u32[]{:S(2)}) %collective-permute-start.4) | collective-permute-done | bytes 131104 | tf_op jit(solution)/shard_map/ppermute | solution.py:45
  80.0 9.3 %collective-permute-done.5.refs_3_ = bf16[512,128]{1,0:T(8,128)(2,1)S(1)} collective-permute-done((bf16[512,128]{1,0:T(8,128)(2,1)S(1)}, bf16[512,128]{1,0:T(8,128)(2,1)S(1)}, u32[]{:S(2)}, u32[]{:S(2)}) %collective-permute-start.5) | collective-permute-done | bytes 131104 | tf_op jit(solution)/shard_map/ppermute | solution.py:45
  90.4 5.0 %all-to-all-start.2 = ((bf16[8,512,128]{2,1,0:T(8,128)(2,1)}), bf16[8,512,128]{2,1,0:T(8,128)(2,1)S(1)}, u32[]{:S(2)}, u32[]{:S(2)}) async-start(bf16[8,512,128]{2,1,0:T(8,128)(2,1)} %sum_values.1.refs_3_), calls=%async_computation.2 | async-start | bytes 2097152 | tf_op jit(solution)/shard_map/all_to_all | solution.py:36
  95.4 4.2 %collective-permute-start.8 = (f32[3,6,4,512]{3,2,1,0:T(4,128)S(1)}, f32[3,6,4,512]{3,2,1,0:T(4,128)S(1)}, u32[]{:S(2)}, u32[]{:S(2)}) collective-permute-start(f32[3,6,4,512]{3,2,1,0:T(4,128)S(1)} %stack.25.refs_1_), channel_id=1, source_target_pairs={{0,12},{4,0},{8,4},{1,13},{5,1},{9,5},{2,14},{6,2},{10,6},{3,15},{... | collective-permute-start | bytes 442376 | tf_op jit(solution)/shard_map/ppermute | solution.py:49
  99.6 1.9 collective-permute-start.7
  101.6 1.6 collective-permute-start.6
  103.2 4.3 %collective-permute-done.7.refs_4_.refs_3_ = f32[3,6,4,512]{3,2,1,0:T(4,128)S(1)} collective-permute-done((f32[3,6,4,512]{3,2,1,0:T(4,128)S(1)}, f32[3,6,4,512]{3,2,1,0:T(4,128)S(1)}, u32[]{:S(2)}, u32[]{:S(2)}) %collective-permute-start.7) | collective-permute-done | bytes 147488 | tf_op jit(solution)/shard_map/ppermute | solution.py:49
  112.9 2.7 %gradient.1 = (bf16[64,16,512]{2,1,0:T(8,128)(2,1)S(1)}, f32[16,512]{1,0:T(8,128)S(1)}) custom-call(s32[5]{0:T(128)S(1)} %copy-done.23, bf16[1024,1024]{1,0:T(8,128)(2,1)S(1)} %bitcast.10, bf16[8,512,128]{2,1,0:T(8,128)(2,1)S(1)} %all-to-all-done.2.refs_2_, f32[3,6,4,512]{3,2,1,0:T(4,128)S(1)} %copy-done.14, f32[3,6,4,512]{3,2,1,0:T(4,128)S(1)} %copy-done.11, ...), custom_call_target="tpu_custom_call" | custom-call | flops 1 | bytes 1024 | tf_op jit(solution)/shard_map/gradient/pallas_call | solution.py:58
  116.5 17.8 %all-to-all-start.3 = ((bf16[64,16,512]{2,1,0:T(8,128)(2,1)}), bf16[64,16,512]{2,1,0:T(8,128)(2,1)S(1)}, u32[]{:S(2)}, u32[]{:S(2)}) async-start(bf16[64,16,512]{2,1,0:T(8,128)(2,1)} %copy-done.9), calls=%async_computation.3 | async-start | bytes 2097152 | tf_op jit(solution)/shard_map/all_to_all | solution.py:36
  135.0 4.5 %collective-permute-start.11 = (f32[3,3,6,4,512]{4,3,2,1,0:T(4,128)S(1)}, f32[3,3,6,4,512]{4,3,2,1,0:T(4,128)S(1)}, u32[]{:S(2)}, u32[]{:S(2)}) collective-permute-start(f32[3,3,6,4,512]{4,3,2,1,0:T(4,128)S(1)} %pack_states.1.refs_2_), channel_id=1, source_target_pairs={{0,3},{1,0},{2,1},{3,2},{4,7},{5,4},{6,5},{7,6},{8,11},{9,8},{10,9... | collective-permute-start | bytes 1327112 | tf_op jit(solution)/shard_map/ppermute | solution.py:41
  139.4 2.5 %collective-permute-start.10 = (f32[3,3,6,4,512]{4,3,2,1,0:T(4,128)S(1)}, f32[3,3,6,4,512]{4,3,2,1,0:T(4,128)S(1)}, u32[]{:S(2)}, u32[]{:S(2)}) collective-permute-start(f32[3,3,6,4,512]{4,3,2,1,0:T(4,128)S(1)} %pack_states.1.refs_2_), channel_id=1, source_target_pairs={{0,2},{1,3},{2,0},{3,1},{4,6},{5,7},{6,4},{7,5},{8,10},{9,11},{10,... | collective-permute-start | bytes 1327112 | tf_op jit(solution)/shard_map/ppermute | solution.py:41
  141.9 2.5 %collective-permute-start.9 = (f32[3,3,6,4,512]{4,3,2,1,0:T(4,128)S(1)}, f32[3,3,6,4,512]{4,3,2,1,0:T(4,128)S(1)}, u32[]{:S(2)}, u32[]{:S(2)}) collective-permute-start(f32[3,3,6,4,512]{4,3,2,1,0:T(4,128)S(1)} %pack_states.1.refs_2_), channel_id=1, source_target_pairs={{0,1},{1,2},{2,3},{3,0},{4,5},{5,6},{6,7},{7,4},{8,9},{9,10},{10,1... | collective-permute-start | bytes 1327112 | tf_op jit(solution)/shard_map/ppermute | solution.py:41
  144.4 4.6 %collective-permute-done.11.refs_5_ = f32[3,3,6,4,512]{4,3,2,1,0:T(4,128)S(1)} collective-permute-done((f32[3,3,6,4,512]{4,3,2,1,0:T(4,128)S(1)}, f32[3,3,6,4,512]{4,3,2,1,0:T(4,128)S(1)}, u32[]{:S(2)}, u32[]{:S(2)}) %collective-permute-start.11) | collective-permute-done | bytes 442400 | tf_op jit(solution)/shard_map/ppermute | solution.py:41
  149.0 4.5 %collective-permute-done.10.refs_4_ = f32[3,3,6,4,512]{4,3,2,1,0:T(4,128)S(1)} collective-permute-done((f32[3,3,6,4,512]{4,3,2,1,0:T(4,128)S(1)}, f32[3,3,6,4,512]{4,3,2,1,0:T(4,128)S(1)}, u32[]{:S(2)}, u32[]{:S(2)}) %collective-permute-start.10) | collective-permute-done | bytes 442400 | tf_op jit(solution)/shard_map/ppermute | solution.py:41
  153.5 10.9 %collective-permute-done.9.refs_3_ = f32[3,3,6,4,512]{4,3,2,1,0:T(4,128)S(1)} collective-permute-done((f32[3,3,6,4,512]{4,3,2,1,0:T(4,128)S(1)}, f32[3,3,6,4,512]{4,3,2,1,0:T(4,128)S(1)}, u32[]{:S(2)}, u32[]{:S(2)}) %collective-permute-start.9) | collective-permute-done | bytes 442400 | tf_op jit(solution)/shard_map/ppermute | solution.py:41
  164.4 3.5 %order.1.refs_3_ = f32[64,3,4,512]{3,2,1,0:T(4,128)S(1)} custom-call(s32[5]{0:T(128)S(1)} %copy-done.24, s32[64]{0:T(128)S(1)} %copy-done.25, f32[3,3,6,4,512]{4,3,2,1,0:T(4,128)S(1)} %pack_states.1.refs_2_, f32[3,3,6,4,512]{4,3,2,1,0:T(4,128)S(1)} %collective-permute-done.9.refs_3_, f32[3,3,6,4,512]{4,3,2,1,0:T(4,128)S(1)} %collective-permute-done.10.refs_4_, ...), custom_call_target="tpu_custom_call" | custom-call | flops 1 | bytes 1024 | tf_op jit(solution)/shard_map/order/pallas_call | solution.py:58
  168.7 21.4 %all_to_all.25.refs_2_ = f32[32,2,4,512]{3,2,1,0:T(4,128)S(1)} all-to-all(f32[32,2,4,512]{3,2,1,0:T(4,128)S(1)} %sum_rows.1), channel_id=1, replica_groups=mesh['zh'=2,'y'=8,'c'=2,'zl'=4,'x'=4] {'c','zl','x'}, dimensions={0} | all-to-all | bytes 1048576 | tf_op jit(solution)/shard_map/all_to_all | solution.py:36
  190.0 3.9 %update.1 = (f32[4,4,512]{2,1,0:T(4,128)}, f32[4,4,512]{2,1,0:T(4,128)}, f32[4,4,512]{2,1,0:T(4,128)}, bf16[4,64,512]{2,1,0:T(8,128)(2,1)}) custom-call(s32[5]{0:T(128)S(1)} %copy-done.24, s32[64]{0:T(128)S(1)} %copy-done.26, f32[32,2,4,512]{3,2,1,0:T(4,128)S(1)} %all_to_all.25.refs_2_, f32[64,3,4,512]{3,2,1,0:T(4,128)S(1)} %order.1.refs_3_), custom_call_target="tpu_custom_call" | custom-call | flops 1 | bytes 1024 | tf_op jit(solution)/shard_map/update/pallas_call | solution.py:58
  (68 shorter events, 19.8 us)
Async XLA Ops:
  0.6 12.4 %copy-start.7 = (bf16[128,4096]{1,0:T(8,128)(2,1)S(1)}, bf16[128,4096]{1,0:T(8,128)(2,1)}, u32[]{:S(2)}) copy-start(bf16[128,4096]{1,0:T(8,128)(2,1)} %refs_1_.3) | copy-start | bytes 3145732
  2.5 32.9 %all-to-all-start = ((bf16[16,128,128]{2,1,0:T(8,128)(2,1)}), bf16[16,128,128]{2,1,0:T(8,128)(2,1)S(1)}, u32[]{:S(2)}, u32[]{:S(2)}) async-start(bf16[16,128,128]{2,1,0:T(8,128)(2,1)} %pack_keys.1), calls=%async_computation | async-start | bytes 1048576 | tf_op jit(solution)/shard_map/all_to_all | solution.py:36
  13.0 1.2 copy-start.8
  14.2 44.6 %copy-start.22 = (s32[5]{0:T(128)}, s32[5]{0:T(128)S(1)}, u32[]{:S(2)}) copy-start(s32[5]{0:T(128)S(1)} %stack.24.refs_0_) | copy-start | bytes 64
  15.9 18.7 %collective-permute-start.2 = (bf16[128,2048]{1,0:T(8,128)(2,1)S(1)}, bf16[128,2048]{1,0:T(8,128)(2,1)S(1)}, u32[]{:S(2)}, u32[]{:S(2)}) collective-permute-start(bf16[128,2048]{1,0:T(8,128)(2,1)S(1)} %get-tuple-element.17), channel_id=1, source_target_pairs={{0,1},{1,2},{2,3},{3,0},{4,5},{5,6},{6,7},{7,4},{8,9},{9,10},{10,1... | collective-permute-start | bytes 1572872 | tf_op jit(solution)/shard_map/ppermute | solution.py:41
  19.2 27.3 %collective-permute-start = (bf16[128,2048]{1,0:T(8,128)(2,1)}, bf16[128,2048]{1,0:T(8,128)(2,1)S(1)}, u32[]{:S(2)}, u32[]{:S(2)}) collective-permute-start(bf16[128,2048]{1,0:T(8,128)(2,1)} %get-tuple-element.14), channel_id=1, source_target_pairs={{0,2},{1,3},{2,0},{3,1},{4,6},{5,7},{6,4},{7,5},{8,10},{9,11},{10,... | collective-permute-start | bytes 1572872 | tf_op jit(solution)/shard_map/ppermute | solution.py:41
  23.5 23.0 %collective-permute-start.1 = (bf16[128,2048]{1,0:T(8,128)(2,1)}, bf16[128,2048]{1,0:T(8,128)(2,1)S(1)}, u32[]{:S(2)}, u32[]{:S(2)}) collective-permute-start(bf16[128,2048]{1,0:T(8,128)(2,1)} %get-tuple-element.15), channel_id=1, source_target_pairs={{0,3},{1,0},{2,1},{3,2},{4,7},{5,4},{6,5},{7,6},{8,11},{9,8},{10,9... | collective-permute-start | bytes 1572872 | tf_op jit(solution)/shard_map/ppermute | solution.py:41
  35.4 14.3 %copy-start = (bf16[16,128,128]{2,1,0:T(8,128)(2,1)}, bf16[16,128,128]{2,1,0:T(8,128)(2,1)S(1)}, u32[]{:S(2)}) copy-start(bf16[16,128,128]{2,1,0:T(8,128)(2,1)S(1)} %all-to-all-done) | copy-start | bytes 1572868
  35.4 1.2 copy-start.17
  46.5 3.3 %copy-start.3 = (bf16[128,2048]{1,0:T(8,128)(2,1)}, bf16[128,2048]{1,0:T(8,128)(2,1)S(1)}, u32[]{:S(2)}) copy-start(bf16[128,2048]{1,0:T(8,128)(2,1)S(1)} %collective-permute-done.refs_1_.refs_3_) | copy-start | bytes 1572868
  46.5 1.8 copy-start.2
  48.3 1.5 copy-start.5
  49.8 39.5 %all-to-all-start.1 = ((bf16[8,128,1024]{2,1,0:T(8,128)(2,1)}), bf16[8,128,1024]{2,1,0:T(8,128)(2,1)S(1)}, u32[]{:S(2)}, u32[]{:S(2)}) async-start(bf16[8,128,1024]{2,1,0:T(8,128)(2,1)} %pack_inputs.1.refs_5_), calls=%async_computation.1 | async-start | bytes 4194304 | tf_op jit(solution)/shard_map/all_to_all | solution.py:36
  65.6 10.6 %collective-permute-start.3 = (bf16[512,128]{1,0:T(8,128)(2,1)S(1)}, bf16[512,128]{1,0:T(8,128)(2,1)S(1)}, u32[]{:S(2)}, u32[]{:S(2)}) collective-permute-start(bf16[512,128]{1,0:T(8,128)(2,1)S(1)} %get-tuple-element.19), channel_id=1, source_target_pairs={{4,0},{8,4},{12,8},{5,1},{9,5},{13,9},{6,2},{10,6},{14,10},{7,3},{... | collective-permute-start | bytes 393224 | tf_op jit(solution)/shard_map/ppermute | solution.py:45
  67.1 12.9 %collective-permute-start.4 = (bf16[512,128]{1,0:T(8,128)(2,1)S(1)}, bf16[512,128]{1,0:T(8,128)(2,1)S(1)}, u32[]{:S(2)}, u32[]{:S(2)}) collective-permute-start(bf16[512,128]{1,0:T(8,128)(2,1)S(1)} %get-tuple-element.20), channel_id=1, source_target_pairs={{8,0},{12,4},{9,1},{13,5},{10,2},{14,6},{11,3},{15,7},{24,16},{28,... | collective-permute-start | bytes 393224 | tf_op jit(solution)/shard_map/ppermute | solution.py:45
  68.4 20.9 %collective-permute-start.5 = (bf16[512,128]{1,0:T(8,128)(2,1)S(1)}, bf16[512,128]{1,0:T(8,128)(2,1)S(1)}, u32[]{:S(2)}, u32[]{:S(2)}) collective-permute-start(bf16[512,128]{1,0:T(8,128)(2,1)S(1)} %get-tuple-element.21), channel_id=1, source_target_pairs={{12,0},{13,1},{14,2},{15,3},{28,16},{29,17},{30,18},{31,19},{44,32... | collective-permute-start | bytes 393224 | tf_op jit(solution)/shard_map/ppermute | solution.py:45
  89.3 6.1 %copy-start.19 = (f32[4,6,512]{2,0,1:T(4,128)S(1)}, f32[4,6,512]{2,0,1:T(4,128)}, u32[]{:S(2)}) copy-start(f32[4,6,512]{2,0,1:T(4,128)} %param.15) | copy-start | bytes 147460
  89.3 6.1 %copy-start.20 = (f32[4,6,512]{2,0,1:T(4,128)S(1)}, f32[4,6,512]{2,0,1:T(4,128)}, u32[]{:S(2)}) copy-start(f32[4,6,512]{2,0,1:T(4,128)} %param.16) | copy-start | bytes 147460
  89.3 6.1 %copy-start.21 = (f32[4,6,512]{2,0,1:T(4,128)S(1)}, f32[4,6,512]{2,0,1:T(4,128)}, u32[]{:S(2)}) copy-start(f32[4,6,512]{2,0,1:T(4,128)} %param.17) | copy-start | bytes 147460
  90.4 20.0 %all-to-all-start.2 = ((bf16[8,512,128]{2,1,0:T(8,128)(2,1)}), bf16[8,512,128]{2,1,0:T(8,128)(2,1)S(1)}, u32[]{:S(2)}, u32[]{:S(2)}) async-start(bf16[8,512,128]{2,1,0:T(8,128)(2,1)} %sum_values.1.refs_3_), calls=%async_computation.2 | async-start | bytes 2097152 | tf_op jit(solution)/shard_map/all_to_all | solution.py:36
  95.4 7.7 %collective-permute-start.8 = (f32[3,6,4,512]{3,2,1,0:T(4,128)S(1)}, f32[3,6,4,512]{3,2,1,0:T(4,128)S(1)}, u32[]{:S(2)}, u32[]{:S(2)}) collective-permute-start(f32[3,6,4,512]{3,2,1,0:T(4,128)S(1)} %stack.25.refs_1_), channel_id=1, source_target_pairs={{0,12},{4,0},{8,4},{1,13},{5,1},{9,5},{2,14},{6,2},{10,6},{3,15},{... | collective-permute-start | bytes 442376 | tf_op jit(solution)/shard_map/ppermute | solution.py:49
  99.6 7.9 %collective-permute-start.7 = (f32[3,6,4,512]{3,2,1,0:T(4,128)S(1)}, f32[3,6,4,512]{3,2,1,0:T(4,128)S(1)}, u32[]{:S(2)}, u32[]{:S(2)}) collective-permute-start(f32[3,6,4,512]{3,2,1,0:T(4,128)S(1)} %stack.25.refs_1_), channel_id=1, source_target_pairs={{0,8},{4,12},{8,0},{1,9},{5,13},{9,1},{2,10},{6,14},{10,2},{3,11},... | collective-permute-start | bytes 442376 | tf_op jit(solution)/shard_map/ppermute | solution.py:49
  101.6 7.6 %collective-permute-start.6 = (f32[3,6,4,512]{3,2,1,0:T(4,128)S(1)}, f32[3,6,4,512]{3,2,1,0:T(4,128)S(1)}, u32[]{:S(2)}, u32[]{:S(2)}) collective-permute-start(f32[3,6,4,512]{3,2,1,0:T(4,128)S(1)} %stack.25.refs_1_), channel_id=1, source_target_pairs={{0,4},{4,8},{8,12},{1,5},{5,9},{9,13},{2,6},{6,10},{10,14},{3,7},{... | collective-permute-start | bytes 442376 | tf_op jit(solution)/shard_map/ppermute | solution.py:49
  112.9 21.5 %copy-start.24 = (s32[5]{0:T(128)S(1)}, s32[5]{0:T(128)}, u32[]{:S(2)}) copy-start(s32[5]{0:T(128)} %copy-done.22) | copy-start | bytes 64
  116.5 17.8 %copy-start.12 = (f32[3,6,4,512]{3,2,1,0:T(4,128)S(1)}, f32[3,6,4,512]{3,2,1,0:T(4,128)}, u32[]{:S(2)}) copy-start(f32[3,6,4,512]{3,2,1,0:T(4,128)} %copy-done.10) | copy-start | bytes 442372
  116.5 17.8 %copy-start.15 = (f32[3,6,4,512]{3,2,1,0:T(4,128)S(1)}, f32[3,6,4,512]{3,2,1,0:T(4,128)}, u32[]{:S(2)}) copy-start(f32[3,6,4,512]{3,2,1,0:T(4,128)} %copy-done.13) | copy-start | bytes 442372
  116.5 47.9 %copy-start.25 = (s32[64]{0:T(128)S(1)}, s32[64]{0:T(128)}, u32[]{:S(2)}) copy-start(s32[64]{0:T(128)} %refs_1_.4) | copy-start | bytes 772
  116.5 51.4 %all-to-all-start.3 = ((bf16[64,16,512]{2,1,0:T(8,128)(2,1)}), bf16[64,16,512]{2,1,0:T(8,128)(2,1)S(1)}, u32[]{:S(2)}, u32[]{:S(2)}) async-start(bf16[64,16,512]{2,1,0:T(8,128)(2,1)} %copy-done.9), calls=%async_computation.3 | async-start | bytes 2097152 | tf_op jit(solution)/shard_map/all_to_all | solution.py:36
  135.0 14.0 %collective-permute-start.11 = (f32[3,3,6,4,512]{4,3,2,1,0:T(4,128)S(1)}, f32[3,3,6,4,512]{4,3,2,1,0:T(4,128)S(1)}, u32[]{:S(2)}, u32[]{:S(2)}) collective-permute-start(f32[3,3,6,4,512]{4,3,2,1,0:T(4,128)S(1)} %pack_states.1.refs_2_), channel_id=1, source_target_pairs={{0,3},{1,0},{2,1},{3,2},{4,7},{5,4},{6,5},{7,6},{8,11},{9,8},{10,9... | collective-permute-start | bytes 1327112 | tf_op jit(solution)/shard_map/ppermute | solution.py:41
  139.4 14.1 %collective-permute-start.10 = (f32[3,3,6,4,512]{4,3,2,1,0:T(4,128)S(1)}, f32[3,3,6,4,512]{4,3,2,1,0:T(4,128)S(1)}, u32[]{:S(2)}, u32[]{:S(2)}) collective-permute-start(f32[3,3,6,4,512]{4,3,2,1,0:T(4,128)S(1)} %pack_states.1.refs_2_), channel_id=1, source_target_pairs={{0,2},{1,3},{2,0},{3,1},{4,6},{5,7},{6,4},{7,5},{8,10},{9,11},{10,... | collective-permute-start | bytes 1327112 | tf_op jit(solution)/shard_map/ppermute | solution.py:41
  141.9 22.5 %collective-permute-start.9 = (f32[3,3,6,4,512]{4,3,2,1,0:T(4,128)S(1)}, f32[3,3,6,4,512]{4,3,2,1,0:T(4,128)S(1)}, u32[]{:S(2)}, u32[]{:S(2)}) collective-permute-start(f32[3,3,6,4,512]{4,3,2,1,0:T(4,128)S(1)} %pack_states.1.refs_2_), channel_id=1, source_target_pairs={{0,1},{1,2},{2,3},{3,0},{4,5},{5,6},{6,7},{7,4},{8,9},{9,10},{10,1... | collective-permute-start | bytes 1327112 | tf_op jit(solution)/shard_map/ppermute | solution.py:41
  167.9 22.1 %copy-start.26 = (s32[64]{0:T(128)S(1)}, s32[64]{0:T(128)}, u32[]{:S(2)}) copy-start(s32[64]{0:T(128)} %refs_1_.5) | copy-start | bytes 772
  (11 other events, 9.7 us)

commit v4 on v3

--- a/solution.py
+++ b/solution.py
@@ -1,5 +1,3 @@
-import functools
-
 import jax
 import jax.numpy as jnp
 from jax import lax
@@ -22,10 +20,9 @@
 
 PLANE = 512
 CHUNK = 256
-QUERIES = 256
-FIRST, SECOND = (0, 1), (3, 2)
 ZH, Y, C, ZL, X = range(5)
 WHOLE = pl.BlockSpec(memory_space=pltpu.VMEM)
+IN_HBM = pl.BlockSpec(memory_space=pltpu.HBM)
 ELSEWHERE = pl.BlockSpec(memory_space=pl.ANY)
 SCALARS = pl.BlockSpec(memory_space=pltpu.SMEM)
 NT = (((1,), (1,)), ((), ()))
@@ -41,6 +38,10 @@
     return lax.ppermute(x, axis, [(i, (i + k) % n) for i in range(n)])
 
 
+def sent_up(x, k):
+    return lax.ppermute(x, "zl", [(i, i + k) for i in range(4 - k)])
+
+
 def sent_down(x, k):
     return lax.ppermute(x, "zl", [(i, i - k) for i in range(k, 4)])
 
@@ -49,7 +50,7 @@
     return lax.ppermute(x, "zl", [(i, (i + k) % 4) for i in range(3)])
 
 
-def call(kernel, name, out, scalars, arrays, scratch, behind=(), limit=20):
+def call(kernel, name, out, scalars, arrays, scratch, behind=(), limit=12):
     given = len(scalars) + len(arrays)
 
     def body(*refs):
@@ -67,22 +68,33 @@
     )(*scalars, *arrays, *behind)
 
 
+def gate(x, *behind):
+    return pl.pallas_call(
+        lambda *refs: None,
+        out_shape=jax.ShapeDtypeStruct(x.shape, x.dtype),
+        in_specs=[IN_HBM] + [ELSEWHERE] * len(behind),
+        out_specs=IN_HBM,
+        input_output_aliases={0: 0},
+        compiler_params=pltpu.CompilerParams(vmem_limit_bytes=MIB),
+        cost_estimate=pl.CostEstimate(flops=1, bytes_accessed=1024, transcendentals=0),
+        name="gate",
+    )(x, *behind)
+
+
 def shape(*dims, dtype=jnp.bfloat16):
     return jax.ShapeDtypeStruct(dims, dtype)
 
 
 def pack_keys_kernel(k_ref, out_ref):
     for g in range(KV):
-        part = k_ref[:, g * HD : (g + 1) * HD]
-        for zl in range(4):
-            out_ref[zl * 4 + g] = part
-
-
-def pack_heads_kernel(place, q_ref, d_ref, *out):
-    for k in range(4):
-        at = pl.ds(pl.multiple_of(((place[X] + k) % 4) * GRP * HD, GRP * HD), GRP * HD)
-        out[k][:, 0 : GRP * HD] = q_ref[:, at]
-        out[k][:, GRP * HD :] = d_ref[:, at]
+        out_ref[g] = k_ref[:, g * HD : (g + 1) * HD]
+
+
+def pack_heads_kernel(q_ref, d_ref, out_ref):
+    width = GRP * HD
+    for g in range(KV):
+        out_ref[g, :, 0:width] = q_ref[:, g * width : (g + 1) * width]
+        out_ref[g, :, width:] = d_ref[:, g * width : (g + 1) * width]
 
 
 def pack_inputs_kernel(in_ref, out_ref):
@@ -106,40 +118,36 @@
             out_ref[plane] = ref[...]
 
 
-def value_kernel(steps, place, k_ref, ra, rb, *refs):
+def value_kernel(place, heads, k0, k1, k2, k3, own_ref, down1, down2, down3, s_a, s_b, total):
     plane = place[ZL]
     factor = HD**-0.5 * LOG2E
-    if steps == FIRST:
-        total, q_ref, d_ref, s_a, s_b = refs
-    else:
-        before, own_ref, *down, q_ref, d_ref, s_a, s_b, total = refs
     width = GRP * HD
-    for at, part in ((0, ra), (128, rb)):
-        q_ref[at : at + 128, :] = part[:, 0:width]
-        d_ref[at : at + 128, :] = part[:, width:]
-    starts = [((place[X] + 4 - k) % 4) * 128 for k in steps]
-    column = lax.broadcasted_iota(jnp.int32, (CHUNK, QUERIES), 1)
-    position = jnp.where(column < 128, column + starts[0], column - 128 + starts[1])
-    ahead = position - lax.broadcasted_iota(jnp.int32, (CHUNK, QUERIES), 0)
+
+    def columns(start):
+        at = pl.ds(pl.multiple_of(start, HD), HD)
+        return heads[:, :, at].reshape(PLANE, HD)
 
     def scores(h, last, s_ref):
-        q = q_ref[:, pl.ds(pl.multiple_of(h * HD, HD), HD)]
-        top = jnp.full((8, QUERIES), -jnp.inf, jnp.float32)
+        q = columns(h * HD)
+        top = jnp.full((8, PLANE), -jnp.inf, jnp.float32)
         for at in range(0, (last + 1) * PLANE, CHUNK):
-            s = lax.dot_general(k_ref[at : at + CHUNK, :], q, NT, preferred_element_type=jnp.float32)
+            k_ref = (k0, k1, k2, k3)[last - at // PLANE]
+            k = k_ref[at % PLANE : at % PLANE + CHUNK, :]
+            s = lax.dot_general(k, q, NT, preferred_element_type=jnp.float32)
             if at >= last * PLANE:
-                s = jnp.where(ahead >= at - last * PLANE, s, -jnp.inf)
+                key = lax.broadcasted_iota(jnp.int32, s.shape, 0) + (at - last * PLANE)
+                s = jnp.where(key <= lax.broadcasted_iota(jnp.int32, s.shape, 1), s, -jnp.inf)
             s_ref[at : at + CHUNK, :] = s
-            top = jnp.maximum(top, jnp.max(s.reshape(CHUNK // 8, 8, QUERIES), axis=0))
+            top = jnp.maximum(top, jnp.max(s.reshape(CHUNK // 8, 8, PLANE), axis=0))
         return jnp.max(top, axis=0, keepdims=True)
 
     def add_terms(h, last, s_ref, top):
-        d = d_ref[:, pl.ds(pl.multiple_of(h * HD, HD), HD)]
-        size = jnp.zeros((8, QUERIES), jnp.float32)
+        d = columns(h * HD + width)
+        size = jnp.zeros((8, PLANE), jnp.float32)
         for at in range(0, (last + 1) * PLANE, CHUNK):
             w = jnp.exp2((s_ref[at : at + CHUNK, :] - top) * factor)
             s_ref[at : at + CHUNK, :] = w
-            size = size + jnp.sum(w.reshape(CHUNK // 8, 8, QUERIES), axis=0)
+            size = size + jnp.sum(w.reshape(CHUNK // 8, 8, PLANE), axis=0)
         inverse = 1.0 / jnp.sum(size, axis=0, keepdims=True)
         for at in range(0, (last + 1) * PLANE, CHUNK):
             p = (s_ref[at : at + CHUNK, :] * inverse).astype(jnp.bfloat16)
@@ -149,11 +157,8 @@
 
         @pl.when(plane == last)
         def _(last=last):
-            used = slice(0, (last + 1) * PLANE)
-            if steps == FIRST:
-                total[used, :] = jnp.zeros(((last + 1) * PLANE, HD), jnp.float32)
-            else:
-                total[used, :] = before[used, :]
+            used = (last + 1) * PLANE
+            total[0:used, :] = jnp.zeros((used, HD), jnp.float32)
 
             @pl.loop(0, GRP // 2)
             def _(pair):
@@ -162,30 +167,9 @@
                 add_terms(2 * pair, last, s_a, top_a)
                 add_terms(2 * pair + 1, last, s_b, top_b)
 
-            if steps != FIRST:
-                own_ref[...] = total[last * PLANE : (last + 1) * PLANE, :]
-                for k in range(1, last + 1):
-                    down[k - 1][...] = total[(last - k) * PLANE : (last - k + 1) * PLANE, :].astype(jnp.bfloat16)
-
-
-def value_terms(steps, place, keys, parts, before=None, behind=()):
-    total = shape(4 * PLANE, HD, dtype=jnp.float32)
-    own = shape(PLANE, HD, dtype=jnp.float32)
-    scratch = [
-        pltpu.VMEM((QUERIES, GRP * HD), jnp.bfloat16),
-        pltpu.VMEM((QUERIES, GRP * HD), jnp.bfloat16),
-        pltpu.VMEM((4 * PLANE, QUERIES), jnp.float32),
-        pltpu.VMEM((4 * PLANE, QUERIES), jnp.float32),
-    ]
-    return call(
-        functools.partial(value_kernel, steps),
-        "values",
-        total if steps == FIRST else (own, *(shape(PLANE, HD),) * 3),
-        [place],
-        [keys, *(parts[k] for k in steps), *([] if before is None else [before])],
-        scratch if steps == FIRST else [*scratch, pltpu.VMEM((4 * PLANE, HD), jnp.float32)],
-        behind,
-    )
+            own_ref[...] = total[last * PLANE : used, :]
+            for k, out in enumerate((down1, down2, down3)[:last], 1):
+                out[...] = total[(last - k) * PLANE : (last - k + 1) * PLANE, :].astype(jnp.bfloat16)
 
 
 def sum_values_kernel(own_ref, a_ref, b_ref, c_ref, out_ref):
@@ -285,26 +269,36 @@
     columns = KV * HD
     place = jnp.stack([lax.axis_index(a) for a in ("zh", "y", "c", "zl", "x")]).astype(jnp.int32)
 
-    keys_all = call(pack_keys_kernel, "pack_keys", shape(16, here, HD), [], [keys], [])
-    keys_all = swapped(keys_all, ("zl", "x")).reshape(4 * PLANE, HD)
+    packed = call(pack_keys_kernel, "pack_keys", shape(KV, here, HD), [], [keys], [])
+    plane_keys = swapped(packed, "x").reshape(PLANE, HD)
     packed = call(
-        pack_heads_kernel, "pack_heads", (shape(here, 2 * GRP * HD),) * 4, [place], [queries, grad_out], []
-    )
-    heads = {0: packed[0], **{k: shifted(packed[k], "x", k) for k in (1, 3, 2)}}
-    total = value_terms(FIRST, place, keys_all, heads)
-    late = [heads[2], heads[3], total]
-    packed = call(pack_inputs_kernel, "pack_inputs", shape(8, here, 1024), [], [inputs], [], late)
-    pieces = swapped(packed, ("c", "x"))
-    own, *parts = value_terms(SECOND, place, keys_all, heads, total, [packed])
+        pack_heads_kernel, "pack_heads", shape(KV, here, 2 * GRP * HD), [], [queries, grad_out], []
+    )
+    heads = swapped(gate(packed, plane_keys), "x")
+    all_keys = [plane_keys, *(sent_up(plane_keys, k) for k in (1, 2, 3))]
+    state = [a.transpose(1, 0, 2) for a in (param_old, first_old, second_old)]
+    state = call(stack_kernel, "stack", shape(3, *state[0].shape, dtype=f32), [], state, [])
+    planes = [state, *(old_planes(state, k) for k in (1, 2, 3))]
+    packed = call(pack_inputs_kernel, "pack_inputs", shape(8, here, 1024), [], [inputs], [])
+    pieces = swapped(gate(packed, heads, *all_keys[1:], *planes[1:]), ("c", "x"))
+
+    own, *parts = call(
+        value_kernel,
+        "values",
+        (shape(PLANE, HD, dtype=f32), *(shape(PLANE, HD),) * 3),
+        [place],
+        [heads, *all_keys],
+        [pltpu.VMEM((4 * PLANE, PLANE), f32)] * 2 + [pltpu.VMEM((4 * PLANE, HD), f32)],
+        limit=24,
+    )
     parts = [sent_down(parts[k - 1], k) for k in (1, 2, 3)]
     values = call(sum_values_kernel, "sum_values", shape(8, PLANE, HD), [], [own, *parts], [], [pieces])
-    state = [a.transpose(1, 0, 2) for a in (param_old, first_old, second_old)]
-    state = call(stack_kernel, "stack", shape(3, *state[0].shape, dtype=f32), [], state, [], [values])
-    planes = [state, *(old_planes(state, k) for k in (1, 2, 3))]
+    packed = call(
+        pack_states_kernel, "pack_states", shape(3, *state.shape, dtype=f32), [place], planes, [], [values]
+    )
     values = swapped(values, ("c", "x"))
-    state = call(
-        pack_states_kernel, "pack_states", shape(3, *state.shape, dtype=f32), [place], planes, []
-    )
+    state = [packed, *(shifted(packed, "x", k) for k in (1, 2, 3))]
+
     parts, own = call(
         gradient_kernel,
         "gradient",
@@ -312,10 +306,9 @@
         [place],
         [pieces.reshape(2 * PLANE, 1024), values],
         [pltpu.VMEM((2 * PLANE, columns), jnp.bfloat16)] + [pltpu.VMEM((128, columns), f32)] * 2,
-        planes[1:],
+        state[1:2],
     )
     arrived = swapped(parts, ("zh", "y", "zl"))
-    state = [state, *(shifted(state, "x", k) for k in (1, 2, 3))]
     state = call(
         order_kernel,
         "order",

time: 195 us -> 193 us (0.990)
  waiting for transfers between devices: 59.7 us -> 69.8 us
  starting transfers between devices: 74.1 us -> 65.7 us
  blocking collectives: 21.4 us -> 25.1 us
  Pallas kernels: 23.8 us -> 20.2 us
  local copies, waits for them, and re-layouts: 14.1 us -> 10.6 us
    ppermute x6 -> x3, starting transfers between devices: 20.1 us -> 8.55 us  [shifted(): return lax.ppermute(x, axis, [(i, (i + k) % n) for i in range(n)])]
    all_to_all x4 -> x5, starting transfers between devices: 42.3 us -> 35.6 us  [swapped(): return lax.all_to_all(x, axes, split_axis=0, concat_axis=0, tiled=True)]
    ppermute x3, waiting for transfers between devices: 19.6 us -> 26.1 us  [sent_down(): return lax.ppermute(x, 'zl', [(i, i - k) for i in range(k, 4)])]
    ppermute x0 -> x3, starting transfers between devices: none -> 5.96 us  [sent_up(): return lax.ppermute(x, 'zl', [(i, i + k) for i in range(4 - k)])]
    ppermute x3, waiting for transfers between devices: 5.35 us -> 0.01 us  [old_planes(): return lax.ppermute(x, 'zl', [(i, (i + k) % 4) for i in range(3)])]
    ppermute x3, starting transfers between devices: 7.69 us -> 11.7 us  [old_planes(): return lax.ppermute(x, 'zl', [(i, (i + k) % 4) for i in range(3)])]
    all_to_all x1, blocking collectives: 21.4 us -> 25.1 us  [swapped(): return lax.all_to_all(x, axes, split_axis=0, concat_axis=0, tiled=True)]
    pallas_call x12 -> x11, Pallas kernels: 23.8 us -> 20.2 us  [call(): pl.pallas_call(body, out_shape=out, in_specs=[SCALARS] * len(scalars) + [...]
  transfers between devices with their start and end apart: 16 -> 17, of which waited for: 11 -> 9; matrix products, arithmetic and copies ran while one was open for 0% -> 0% of each run, Pallas kernels for 7% -> 5%
where the time goes in v4:
time: 193 us; the launch traced here: 192 us
  waiting for transfers between devices  69.8 us (36%)
  starting transfers between devices  65.7 us (34%)
  blocking collectives  25.1 us (13%)
  Pallas kernels  20.2 us (10%)
  local copies, waits for them, and re-layouts  10.6 us (5%)
    ppermute x3, waiting for transfers between devices, shifted(): return lax.ppermute(x, axis, [(i, (i + k) % n) for i in range(n)])  37.3 us
    all_to_all x5, starting transfers between devices, swapped(): return lax.all_to_all(x, axes, split_axis=0, concat_axis=0, tiled=True)  35.6 us
    ppermute x3, waiting for transfers between devices, sent_down(): return lax.ppermute(x, 'zl', [(i, i - k) for i in range(k, 4)])  26.1 us
    all_to_all x1, blocking collectives, swapped(): return lax.all_to_all(x, axes, split_axis=0, concat_axis=0, tiled=True)  25.1 us
    pallas_call x11, Pallas kernels, call(): pl.pallas_call(body, out_shape=out, in_specs=[SCALARS] * len(scalars) + [...  20.2 us
    ppermute x3, starting transfers between devices, old_planes(): return lax.ppermute(x, 'zl', [(i, (i + k) % 4) for i in range(3)])  11.7 us
    unnamed x26, local copies, waits for them, and re-layouts  10.5 us
    ppermute x3, starting transfers between devices, shifted(): return lax.ppermute(x, axis, [(i, (i + k) % n) for i in range(n)])  8.55 us
  transfers between devices with their start and end apart: 17, of which 9 were waited for; matrix products, arithmetic and copies ran while one was open for 0% of the time, Pallas kernels for 5%

profile of v4, /device:TPU:1, one launch (start us, length us, event | category | flops | bytes accessed | tf_op | source)
XLA Modules:
  0.0 192.3 jit_solution(9221124535018073835)
XLA Ops:
  2.2 4.8 %all-to-all-start = ((bf16[4,128,128]{2,1,0:T(8,128)(2,1)}), bf16[4,128,128]{2,1,0:T(8,128)(2,1)S(1)}, u32[]{:S(2)}, u32[]{:S(2)}) async-start(bf16[4,128,128]{2,1,0:T(8,128)(2,1)} %pack_keys.1), calls=%async_computation | async-start | bytes 262144 | tf_op jit(solution)/shard_map/all_to_all | solution.py:33
  9.6 2.2 %all-to-all-done = bf16[4,128,128]{2,1,0:T(8,128)(2,1)S(1)} async-done(((bf16[4,128,128]{2,1,0:T(8,128)(2,1)}), bf16[4,128,128]{2,1,0:T(8,128)(2,1)S(1)}, u32[]{:S(2)}, u32[]{:S(2)}) %all-to-all-start) | async-done | bytes 131104 | tf_op jit(solution)/shard_map/all_to_all | solution.py:33
  11.9 1.3 copy-done.3
  13.2 3.7 %all-to-all-start.1 = ((bf16[4,128,2048]{2,1,0:T(8,128)(2,1)}), bf16[4,128,2048]{2,1,0:T(8,128)(2,1)S(1)}, u32[]{:S(2)}, u32[]{:S(2)}) async-start(bf16[4,128,2048]{2,1,0:T(8,128)(2,1)} %copy-done.3), calls=%async_computation.1 | async-start | bytes 4194304 | tf_op jit(solution)/shard_map/all_to_all | solution.py:33
  17.0 4.0 %collective-permute-start.3 = (f32[3,6,4,512]{3,2,1,0:T(4,128)S(1)}, f32[3,6,4,512]{3,2,1,0:T(4,128)S(1)}, u32[]{:S(2)}, u32[]{:S(2)}) collective-permute-start(f32[3,6,4,512]{3,2,1,0:T(4,128)S(1)} %stack.25.refs_1_), channel_id=1, source_target_pairs={{0,4},{4,8},{8,12},{1,5},{5,9},{9,13},{2,6},{6,10},{10,14},{3,7},{... | collective-permute-start | bytes 442376 | tf_op jit(solution)/shard_map/ppermute | solution.py:50
  21.0 5.8 %collective-permute-start.4 = (f32[3,6,4,512]{3,2,1,0:T(4,128)S(1)}, f32[3,6,4,512]{3,2,1,0:T(4,128)S(1)}, u32[]{:S(2)}, u32[]{:S(2)}) collective-permute-start(f32[3,6,4,512]{3,2,1,0:T(4,128)S(1)} %stack.25.refs_1_), channel_id=1, source_target_pairs={{0,8},{4,12},{8,0},{1,9},{5,13},{9,1},{2,10},{6,14},{10,2},{3,11},... | collective-permute-start | bytes 442376 | tf_op jit(solution)/shard_map/ppermute | solution.py:50
  26.8 1.9 collective-permute-start.5
  28.8 3.4 %collective-permute-start = (bf16[512,128]{1,0:T(8,128)(2,1)S(1)}, bf16[512,128]{1,0:T(8,128)(2,1)S(1)}, u32[]{:S(2)}, u32[]{:S(2)}) collective-permute-start(bf16[512,128]{1,0:T(8,128)(2,1)S(1)} %bitcast.11), channel_id=1, source_target_pairs={{0,4},{4,8},{8,12},{1,5},{5,9},{9,13},{2,6},{6,10},{10,14},{3,7},{... | collective-permute-start | bytes 393224 | tf_op jit(solution)/shard_map/ppermute | solution.py:42
  33.5 1.3 collective-permute-start.2
  34.8 1.6 copy-done.4
  36.5 1.3 copy-done
  37.9 2.5 %collective-permute-done.2.refs_4_.refs_5_ = bf16[512,128]{1,0:T(8,128)(2,1)S(1)} collective-permute-done((bf16[512,128]{1,0:T(8,128)(2,1)S(1)}, bf16[512,128]{1,0:T(8,128)(2,1)S(1)}, u32[]{:S(2)}, u32[]{:S(2)}) %collective-permute-start.2) | collective-permute-done | bytes 131104 | tf_op jit(solution)/shard_map/ppermute | solution.py:42
  40.3 1.6 copy-done.1
  41.9 1.3 copy-done.2
  43.2 8.1 %all-to-all-start.2 = ((bf16[8,128,1024]{2,1,0:T(8,128)(2,1)}), bf16[8,128,1024]{2,1,0:T(8,128)(2,1)}, u32[]{:S(2)}, u32[]{:S(2)}) async-start(bf16[8,128,1024]{2,1,0:T(8,128)(2,1)} %copy-done.2), calls=%async_computation.2 | async-start | bytes 4194304 | tf_op jit(solution)/shard_map/all_to_all | solution.py:33
  51.4 4.7 %values.1 = (f32[512,128]{1,0:T(8,128)S(1)}, bf16[512,128]{1,0:T(8,128)(2,1)S(1)}, bf16[512,128]{1,0:T(8,128)(2,1)S(1)}, bf16[512,128]{1,0:T(8,128)(2,1)S(1)}) custom-call(s32[5]{0:T(128)S(1)} %stack.24.refs_0_, bf16[4,128,2048]{2,1,0:T(8,128)(2,1)S(1)} %all-to-all-done.1.refs_1_, bf16[512,128]{1,0:T(8,128)(2,1)S(1)} %bitcast.14, ...), custom_call_target="tpu_custom_call" | custom-call | flops 1 | bytes 1024 | tf_op jit(solution)/shard_map/values/pallas_call | solution.py:59
  60.1 10.9 %collective-permute-done.6.refs_1_ = bf16[512,128]{1,0:T(8,128)(2,1)S(1)} collective-permute-done((bf16[512,128]{1,0:T(8,128)(2,1)S(1)}, bf16[512,128]{1,0:T(8,128)(2,1)S(1)}, u32[]{:S(2)}, u32[]{:S(2)}) %collective-permute-start.6) | collective-permute-done | bytes 131104 | tf_op jit(solution)/shard_map/ppermute | solution.py:46
  71.0 7.2 %collective-permute-done.7.refs_2_ = bf16[512,128]{1,0:T(8,128)(2,1)S(1)} collective-permute-done((bf16[512,128]{1,0:T(8,128)(2,1)S(1)}, bf16[512,128]{1,0:T(8,128)(2,1)S(1)}, u32[]{:S(2)}, u32[]{:S(2)}) %collective-permute-start.7) | collective-permute-done | bytes 131104 | tf_op jit(solution)/shard_map/ppermute | solution.py:46
  78.2 8.0 %collective-permute-done.8.refs_3_ = bf16[512,128]{1,0:T(8,128)(2,1)S(1)} collective-permute-done((bf16[512,128]{1,0:T(8,128)(2,1)S(1)}, bf16[512,128]{1,0:T(8,128)(2,1)S(1)}, u32[]{:S(2)}, u32[]{:S(2)}) %collective-permute-start.8) | collective-permute-done | bytes 131104 | tf_op jit(solution)/shard_map/ppermute | solution.py:46
  87.3 5.0 %all-to-all-start.3 = ((bf16[8,512,128]{2,1,0:T(8,128)(2,1)}), bf16[8,512,128]{2,1,0:T(8,128)(2,1)S(1)}, u32[]{:S(2)}, u32[]{:S(2)}) async-start(bf16[8,512,128]{2,1,0:T(8,128)(2,1)} %sum_values.1.refs_5_), calls=%async_computation.3 | async-start | bytes 2097152 | tf_op jit(solution)/shard_map/all_to_all | solution.py:33
  93.0 3.3 %collective-permute-start.9 = (f32[3,3,6,4,512]{4,3,2,1,0:T(4,128)S(1)}, f32[3,3,6,4,512]{4,3,2,1,0:T(4,128)S(1)}, u32[]{:S(2)}, u32[]{:S(2)}) collective-permute-start(f32[3,3,6,4,512]{4,3,2,1,0:T(4,128)S(1)} %pack_states.1.refs_2_), channel_id=1, source_target_pairs={{0,1},{1,2},{2,3},{3,0},{4,5},{5,6},{6,7},{7,4},{8,9},{9,10},{10,1... | collective-permute-start | bytes 1327112 | tf_op jit(solution)/shard_map/ppermute | solution.py:38
  96.3 20.5 %collective-permute-done.9.refs_3_ = f32[3,3,6,4,512]{4,3,2,1,0:T(4,128)S(1)} collective-permute-done((f32[3,3,6,4,512]{4,3,2,1,0:T(4,128)S(1)}, f32[3,3,6,4,512]{4,3,2,1,0:T(4,128)S(1)}, u32[]{:S(2)}, u32[]{:S(2)}) %collective-permute-start.9) | collective-permute-done | bytes 442400 | tf_op jit(solution)/shard_map/ppermute | solution.py:38
  116.8 4.7 %gradient.1 = (bf16[64,16,512]{2,1,0:T(8,128)(2,1)}, f32[16,512]{1,0:T(8,128)S(1)}) custom-call(s32[5]{0:T(128)S(1)} %stack.24.refs_0_, bf16[1024,1024]{1,0:T(8,128)(2,1)} %bitcast.9.refs_1_, bf16[8,512,128]{2,1,0:T(8,128)(2,1)S(1)} %all-to-all-done.3.refs_2_, f32[3,3,6,4,512]{4,3,2,1,0:T(4,128)S(1)} %collective-permute-done.9.refs_3_), custom_call_target="tpu_custom_call" | custom-call | flops 1 | bytes 1024 | tf_op jit(solution)/shard_map/gradient/pallas_call | solution.py:59
  121.5 13.8 %all-to-all-start.4 = ((bf16[64,16,512]{2,1,0:T(8,128)(2,1)}), bf16[64,16,512]{2,1,0:T(8,128)(2,1)S(1)}, u32[]{:S(2)}, u32[]{:S(2)}) async-start(bf16[64,16,512]{2,1,0:T(8,128)(2,1)} %get-tuple-element.14), calls=%async_computation.4 | async-start | bytes 2097152 | tf_op jit(solution)/shard_map/all_to_all | solution.py:33
  135.4 2.6 %collective-permute-start.10 = (f32[3,3,6,4,512]{4,3,2,1,0:T(4,128)S(1)}, f32[3,3,6,4,512]{4,3,2,1,0:T(4,128)S(1)}, u32[]{:S(2)}, u32[]{:S(2)}) collective-permute-start(f32[3,3,6,4,512]{4,3,2,1,0:T(4,128)S(1)} %pack_states.1.refs_2_), channel_id=1, source_target_pairs={{0,2},{1,3},{2,0},{3,1},{4,6},{5,7},{6,4},{7,5},{8,10},{9,11},{10,... | collective-permute-start | bytes 1327112 | tf_op jit(solution)/shard_map/ppermute | solution.py:38
  137.9 2.7 %collective-permute-start.11 = (f32[3,3,6,4,512]{4,3,2,1,0:T(4,128)S(1)}, f32[3,3,6,4,512]{4,3,2,1,0:T(4,128)S(1)}, u32[]{:S(2)}, u32[]{:S(2)}) collective-permute-start(f32[3,3,6,4,512]{4,3,2,1,0:T(4,128)S(1)} %pack_states.1.refs_2_), channel_id=1, source_target_pairs={{0,3},{1,0},{2,1},{3,2},{4,7},{5,4},{6,5},{7,6},{8,11},{9,8},{10,9... | collective-permute-start | bytes 1327112 | tf_op jit(solution)/shard_map/ppermute | solution.py:38
  140.7 8.8 %collective-permute-done.10.refs_4_ = f32[3,3,6,4,512]{4,3,2,1,0:T(4,128)S(1)} collective-permute-done((f32[3,3,6,4,512]{4,3,2,1,0:T(4,128)S(1)}, f32[3,3,6,4,512]{4,3,2,1,0:T(4,128)S(1)}, u32[]{:S(2)}, u32[]{:S(2)}) %collective-permute-start.10) | collective-permute-done | bytes 442400 | tf_op jit(solution)/shard_map/ppermute | solution.py:38
  149.4 8.0 %collective-permute-done.11.refs_5_ = f32[3,3,6,4,512]{4,3,2,1,0:T(4,128)S(1)} collective-permute-done((f32[3,3,6,4,512]{4,3,2,1,0:T(4,128)S(1)}, f32[3,3,6,4,512]{4,3,2,1,0:T(4,128)S(1)}, u32[]{:S(2)}, u32[]{:S(2)}) %collective-permute-start.11) | collective-permute-done | bytes 442400 | tf_op jit(solution)/shard_map/ppermute | solution.py:38
  157.4 3.5 %order.1.refs_3_ = f32[64,3,4,512]{3,2,1,0:T(4,128)S(1)} custom-call(s32[5]{0:T(128)S(1)} %stack.24.refs_0_, s32[64]{0:T(128)S(1)} %copy-done.11, f32[3,3,6,4,512]{4,3,2,1,0:T(4,128)S(1)} %pack_states.1.refs_2_, f32[3,3,6,4,512]{4,3,2,1,0:T(4,128)S(1)} %collective-permute-done.9.refs_3_, f32[3,3,6,4,512]{4,3,2,1,0:T(4,128)S(1)} %collective-permute-done.10.refs_4_, ...), custom_call_target="tpu_custom_call" | custom-call | flops 1 | bytes 1024 | tf_op jit(solution)/shard_map/order/pallas_call | solution.py:59
  160.9 1.7 all-to-all-done.4.refs_1_
  163.3 25.1 %all_to_all.30.refs_2_ = f32[32,2,4,512]{3,2,1,0:T(4,128)S(1)} all-to-all(f32[32,2,4,512]{3,2,1,0:T(4,128)S(1)} %sum_rows.1), channel_id=1, replica_groups=mesh['zh'=2,'y'=8,'c'=2,'zl'=4,'x'=4] {'c','zl','x'}, dimensions={0} | all-to-all | bytes 1048576 | tf_op jit(solution)/shard_map/all_to_all | solution.py:33
  188.4 3.9 %update.1 = (f32[4,4,512]{2,1,0:T(4,128)}, f32[4,4,512]{2,1,0:T(4,128)}, f32[4,4,512]{2,1,0:T(4,128)}, bf16[4,64,512]{2,1,0:T(8,128)(2,1)}) custom-call(s32[5]{0:T(128)S(1)} %stack.24.refs_0_, s32[64]{0:T(128)S(1)} %copy-done.12, f32[32,2,4,512]{3,2,1,0:T(4,128)S(1)} %all_to_all.30.refs_2_, f32[64,3,4,512]{3,2,1,0:T(4,128)S(1)} %order.1.refs_3_), custom_call_target="tpu_custom_call" | custom-call | flops 1 | bytes 1024 | tf_op jit(solution)/shard_map/update/pallas_call | solution.py:59
  (43 shorter events, 12.0 us)
Async XLA Ops:
  0.6 0.9 copy-start.7
  2.2 9.7 %all-to-all-start = ((bf16[4,128,128]{2,1,0:T(8,128)(2,1)}), bf16[4,128,128]{2,1,0:T(8,128)(2,1)S(1)}, u32[]{:S(2)}, u32[]{:S(2)}) async-start(bf16[4,128,128]{2,1,0:T(8,128)(2,1)} %pack_keys.1), calls=%async_computation | async-start | bytes 262144 | tf_op jit(solution)/shard_map/all_to_all | solution.py:33
  7.1 1.2 copy-start.5
  8.3 1.2 copy-start.6
  11.9 1.3 copy-start.3
  13.2 3.8 %copy-start.8 = (f32[4,6,512]{2,0,1:T(4,128)S(1)}, f32[4,6,512]{2,0,1:T(4,128)}, u32[]{:S(2)}) copy-start(f32[4,6,512]{2,0,1:T(4,128)} %param.15) | copy-start | bytes 147460
  13.2 3.8 %copy-start.9 = (f32[4,6,512]{2,0,1:T(4,128)S(1)}, f32[4,6,512]{2,0,1:T(4,128)}, u32[]{:S(2)}) copy-start(f32[4,6,512]{2,0,1:T(4,128)} %param.16) | copy-start | bytes 147460
  13.2 3.8 %copy-start.10 = (f32[4,6,512]{2,0,1:T(4,128)S(1)}, f32[4,6,512]{2,0,1:T(4,128)}, u32[]{:S(2)}) copy-start(f32[4,6,512]{2,0,1:T(4,128)} %param.17) | copy-start | bytes 147460
  13.2 27.1 %all-to-all-start.1 = ((bf16[4,128,2048]{2,1,0:T(8,128)(2,1)}), bf16[4,128,2048]{2,1,0:T(8,128)(2,1)S(1)}, u32[]{:S(2)}, u32[]{:S(2)}) async-start(bf16[4,128,2048]{2,1,0:T(8,128)(2,1)} %copy-done.3), calls=%async_computation.1 | async-start | bytes 4194304 | tf_op jit(solution)/shard_map/all_to_all | solution.py:33
  17.0 16.4 %collective-permute-start.3 = (f32[3,6,4,512]{3,2,1,0:T(4,128)S(1)}, f32[3,6,4,512]{3,2,1,0:T(4,128)S(1)}, u32[]{:S(2)}, u32[]{:S(2)}) collective-permute-start(f32[3,6,4,512]{3,2,1,0:T(4,128)S(1)} %stack.25.refs_1_), channel_id=1, source_target_pairs={{0,4},{4,8},{8,12},{1,5},{5,9},{9,13},{2,6},{6,10},{10,14},{3,7},{... | collective-permute-start | bytes 442376 | tf_op jit(solution)/shard_map/ppermute | solution.py:50
  21.0 16.8 %collective-permute-start.4 = (f32[3,6,4,512]{3,2,1,0:T(4,128)S(1)}, f32[3,6,4,512]{3,2,1,0:T(4,128)S(1)}, u32[]{:S(2)}, u32[]{:S(2)}) collective-permute-start(f32[3,6,4,512]{3,2,1,0:T(4,128)S(1)} %stack.25.refs_1_), channel_id=1, source_target_pairs={{0,8},{4,12},{8,0},{1,9},{5,13},{9,1},{2,10},{6,14},{10,2},{3,11},... | collective-permute-start | bytes 442376 | tf_op jit(solution)/shard_map/ppermute | solution.py:50
  26.8 11.0 %collective-permute-start.5 = (f32[3,6,4,512]{3,2,1,0:T(4,128)S(1)}, f32[3,6,4,512]{3,2,1,0:T(4,128)S(1)}, u32[]{:S(2)}, u32[]{:S(2)}) collective-permute-start(f32[3,6,4,512]{3,2,1,0:T(4,128)S(1)} %stack.25.refs_1_), channel_id=1, source_target_pairs={{0,12},{4,0},{8,4},{1,13},{5,1},{9,5},{2,14},{6,2},{10,6},{3,15},{... | collective-permute-start | bytes 442376 | tf_op jit(solution)/shard_map/ppermute | solution.py:50
  28.8 9.1 %collective-permute-start = (bf16[512,128]{1,0:T(8,128)(2,1)S(1)}, bf16[512,128]{1,0:T(8,128)(2,1)S(1)}, u32[]{:S(2)}, u32[]{:S(2)}) collective-permute-start(bf16[512,128]{1,0:T(8,128)(2,1)S(1)} %bitcast.11), channel_id=1, source_target_pairs={{0,4},{4,8},{8,12},{1,5},{5,9},{9,13},{2,6},{6,10},{10,14},{3,7},{... | collective-permute-start | bytes 393224 | tf_op jit(solution)/shard_map/ppermute | solution.py:42
  32.1 5.7 %collective-permute-start.1 = (bf16[512,128]{1,0:T(8,128)(2,1)S(1)}, bf16[512,128]{1,0:T(8,128)(2,1)S(1)}, u32[]{:S(2)}, u32[]{:S(2)}) collective-permute-start(bf16[512,128]{1,0:T(8,128)(2,1)S(1)} %bitcast.12), channel_id=1, source_target_pairs={{0,8},{4,12},{1,9},{5,13},{2,10},{6,14},{3,11},{7,15},{16,24},{20,... | collective-permute-start | bytes 393224 | tf_op jit(solution)/shard_map/ppermute | solution.py:42
  33.5 6.9 %collective-permute-start.2 = (bf16[512,128]{1,0:T(8,128)(2,1)S(1)}, bf16[512,128]{1,0:T(8,128)(2,1)S(1)}, u32[]{:S(2)}, u32[]{:S(2)}) collective-permute-start(bf16[512,128]{1,0:T(8,128)(2,1)S(1)} %bitcast.13), channel_id=1, source_target_pairs={{0,12},{1,13},{2,14},{3,15},{16,28},{17,29},{18,30},{19,31},{32,44... | collective-permute-start | bytes 393224 | tf_op jit(solution)/shard_map/ppermute | solution.py:42
  34.8 1.6 copy-start.4
  36.5 1.3 copy-start
  40.3 1.6 copy-start.1
  41.9 1.3 copy-start.2
  43.2 43.0 %all-to-all-start.2 = ((bf16[8,128,1024]{2,1,0:T(8,128)(2,1)}), bf16[8,128,1024]{2,1,0:T(8,128)(2,1)}, u32[]{:S(2)}, u32[]{:S(2)}) async-start(bf16[8,128,1024]{2,1,0:T(8,128)(2,1)} %copy-done.2), calls=%async_computation.2 | async-start | bytes 4194304 | tf_op jit(solution)/shard_map/all_to_all | solution.py:33
  56.2 14.8 %collective-permute-start.6 = (bf16[512,128]{1,0:T(8,128)(2,1)S(1)}, bf16[512,128]{1,0:T(8,128)(2,1)S(1)}, u32[]{:S(2)}, u32[]{:S(2)}) collective-permute-start(bf16[512,128]{1,0:T(8,128)(2,1)S(1)} %get-tuple-element.11), channel_id=1, source_target_pairs={{4,0},{8,4},{12,8},{5,1},{9,5},{13,9},{6,2},{10,6},{14,10},{7,3},{... | collective-permute-start | bytes 393224 | tf_op jit(solution)/shard_map/ppermute | solution.py:46
  57.5 20.7 %collective-permute-start.7 = (bf16[512,128]{1,0:T(8,128)(2,1)S(1)}, bf16[512,128]{1,0:T(8,128)(2,1)S(1)}, u32[]{:S(2)}, u32[]{:S(2)}) collective-permute-start(bf16[512,128]{1,0:T(8,128)(2,1)S(1)} %get-tuple-element.12), channel_id=1, source_target_pairs={{8,0},{12,4},{9,1},{13,5},{10,2},{14,6},{11,3},{15,7},{24,16},{28,... | collective-permute-start | bytes 393224 | tf_op jit(solution)/shard_map/ppermute | solution.py:46
  58.8 27.4 %collective-permute-start.8 = (bf16[512,128]{1,0:T(8,128)(2,1)S(1)}, bf16[512,128]{1,0:T(8,128)(2,1)S(1)}, u32[]{:S(2)}, u32[]{:S(2)}) collective-permute-start(bf16[512,128]{1,0:T(8,128)(2,1)S(1)} %get-tuple-element.13), channel_id=1, source_target_pairs={{12,0},{13,1},{14,2},{15,3},{28,16},{29,17},{30,18},{31,19},{44,32... | collective-permute-start | bytes 393224 | tf_op jit(solution)/shard_map/ppermute | solution.py:46
  87.3 29.5 %all-to-all-start.3 = ((bf16[8,512,128]{2,1,0:T(8,128)(2,1)}), bf16[8,512,128]{2,1,0:T(8,128)(2,1)S(1)}, u32[]{:S(2)}, u32[]{:S(2)}) async-start(bf16[8,512,128]{2,1,0:T(8,128)(2,1)} %sum_values.1.refs_5_), calls=%async_computation.3 | async-start | bytes 2097152 | tf_op jit(solution)/shard_map/all_to_all | solution.py:33
  93.0 23.8 %collective-permute-start.9 = (f32[3,3,6,4,512]{4,3,2,1,0:T(4,128)S(1)}, f32[3,3,6,4,512]{4,3,2,1,0:T(4,128)S(1)}, u32[]{:S(2)}, u32[]{:S(2)}) collective-permute-start(f32[3,3,6,4,512]{4,3,2,1,0:T(4,128)S(1)} %pack_states.1.refs_2_), channel_id=1, source_target_pairs={{0,1},{1,2},{2,3},{3,0},{4,5},{5,6},{6,7},{7,4},{8,9},{9,10},{10,1... | collective-permute-start | bytes 1327112 | tf_op jit(solution)/shard_map/ppermute | solution.py:38
  116.8 40.6 %copy-start.11 = (s32[64]{0:T(128)S(1)}, s32[64]{0:T(128)}, u32[]{:S(2)}) copy-start(s32[64]{0:T(128)} %refs_1_.4) | copy-start | bytes 772
  121.5 41.0 %all-to-all-start.4 = ((bf16[64,16,512]{2,1,0:T(8,128)(2,1)}), bf16[64,16,512]{2,1,0:T(8,128)(2,1)S(1)}, u32[]{:S(2)}, u32[]{:S(2)}) async-start(bf16[64,16,512]{2,1,0:T(8,128)(2,1)} %get-tuple-element.14), calls=%async_computation.4 | async-start | bytes 2097152 | tf_op jit(solution)/shard_map/all_to_all | solution.py:33
  135.4 14.1 %collective-permute-start.10 = (f32[3,3,6,4,512]{4,3,2,1,0:T(4,128)S(1)}, f32[3,3,6,4,512]{4,3,2,1,0:T(4,128)S(1)}, u32[]{:S(2)}, u32[]{:S(2)}) collective-permute-start(f32[3,3,6,4,512]{4,3,2,1,0:T(4,128)S(1)} %pack_states.1.refs_2_), channel_id=1, source_target_pairs={{0,2},{1,3},{2,0},{3,1},{4,6},{5,7},{6,4},{7,5},{8,10},{9,11},{10,... | collective-permute-start | bytes 1327112 | tf_op jit(solution)/shard_map/ppermute | solution.py:38
  137.9 19.5 %collective-permute-start.11 = (f32[3,3,6,4,512]{4,3,2,1,0:T(4,128)S(1)}, f32[3,3,6,4,512]{4,3,2,1,0:T(4,128)S(1)}, u32[]{:S(2)}, u32[]{:S(2)}) collective-permute-start(f32[3,3,6,4,512]{4,3,2,1,0:T(4,128)S(1)} %pack_states.1.refs_2_), channel_id=1, source_target_pairs={{0,3},{1,0},{2,1},{3,2},{4,7},{5,4},{6,5},{7,6},{8,11},{9,8},{10,9... | collective-permute-start | bytes 1327112 | tf_op jit(solution)/shard_map/ppermute | solution.py:38
  162.6 25.9 %copy-start.12 = (s32[64]{0:T(128)S(1)}, s32[64]{0:T(128)}, u32[]{:S(2)}) copy-start(s32[64]{0:T(128)} %refs_1_.5) | copy-start | bytes 772

commit v5 on v4

--- a/solution.py
+++ b/solution.py
@@ -1,3 +1,5 @@
+import functools
+
 import jax
 import jax.numpy as jnp
 from jax import lax
@@ -50,7 +52,7 @@
     return lax.ppermute(x, "zl", [(i, (i + k) % 4) for i in range(3)])
 
 
-def call(kernel, name, out, scalars, arrays, scratch, behind=(), limit=12):
+def call(kernel, name, out, scalars, arrays, scratch, behind=(), limit=8):
     given = len(scalars) + len(arrays)
 
     def body(*refs):
@@ -68,47 +70,70 @@
     )(*scalars, *arrays, *behind)
 
 
-def gate(x, *behind):
-    return pl.pallas_call(
-        lambda *refs: None,
-        out_shape=jax.ShapeDtypeStruct(x.shape, x.dtype),
-        in_specs=[IN_HBM] + [ELSEWHERE] * len(behind),
-        out_specs=IN_HBM,
-        input_output_aliases={0: 0},
-        compiler_params=pltpu.CompilerParams(vmem_limit_bytes=MIB),
-        cost_estimate=pl.CostEstimate(flops=1, bytes_accessed=1024, transcendentals=0),
-        name="gate",
-    )(x, *behind)
-
-
 def shape(*dims, dtype=jnp.bfloat16):
     return jax.ShapeDtypeStruct(dims, dtype)
 
 
-def pack_keys_kernel(k_ref, out_ref):
+def copy_all(pairs, done):
+    copies = [pltpu.make_async_copy(a, b, done.at[i]) for i, (a, b) in enumerate(pairs)]
+    for copy in copies:
+        copy.start()
+    for copy in copies:
+        copy.wait()
+
+
+def pack_heads_kernel(q_ref, d_ref, out_ref, done):
+    width = GRP * HD
+    pairs = []
     for g in range(KV):
-        out_ref[g] = k_ref[:, g * HD : (g + 1) * HD]
-
-
-def pack_heads_kernel(q_ref, d_ref, out_ref):
-    width = GRP * HD
-    for g in range(KV):
-        out_ref[g, :, 0:width] = q_ref[:, g * width : (g + 1) * width]
-        out_ref[g, :, width:] = d_ref[:, g * width : (g + 1) * width]
-
-
-def pack_inputs_kernel(in_ref, out_ref):
-    for k in range(8):
-        out_ref[k] = in_ref[:, k * 1024 : (k + 1) * 1024]
-
-
-def stack_kernel(*refs):
+        at = pl.ds(g * width, width)
+        pairs.append((q_ref.at[:, at], out_ref.at[g, :, pl.ds(0, width)]))
+        pairs.append((d_ref.at[:, at], out_ref.at[g, :, pl.ds(width, width)]))
+    copy_all(pairs, done)
+
+
+def pack_inputs_kernel(in_ref, out_ref, done):
+    copy_all([(in_ref.at[:, pl.ds(k * 1024, 1024)], out_ref.at[k]) for k in range(8)], done)
+
+
+def packed_in_hbm(kernel, name, out, arrays, limit, behind=()):
+    given = len(arrays)
+
+    def body(*refs):
+        kernel(*refs[:given], *refs[given + len(behind) :])
+
+    return pl.pallas_call(
+        body,
+        out_shape=out,
+        in_specs=[IN_HBM] * given + [ELSEWHERE] * len(behind),
+        out_specs=IN_HBM,
+        scratch_shapes=[pltpu.SemaphoreType.DMA((8,))],
+        compiler_params=pltpu.CompilerParams(vmem_limit_bytes=limit * MIB),
+        cost_estimate=pl.CostEstimate(flops=1, bytes_accessed=1024, transcendentals=0),
+        name=name,
+    )(*arrays, *behind)
+
+
+def pack_keys_kernel(place, k_ref, *out):
+    for k, ref in enumerate(out):
+        ref[...] = k_ref[:, pl.ds(pl.multiple_of(((place[X] + k) % 4) * HD, HD), HD)]
+
+
+def join_keys_kernel(place, *refs):
     *parts, out_ref = refs
-    for k, ref in enumerate(parts):
-        out_ref[k] = ref[...]
-
-
-def pack_states_kernel(place, *refs):
+    for k, part in enumerate(parts):
+        out_ref[pl.ds(pl.multiple_of(((place[X] + 4 - k) % 4) * 128, 128), 128), :] = part[...]
+
+
+def pack_states_kernel(p_ref, f_ref, s_ref, out_ref):
+    for slot in range(6):
+        param = p_ref[slot]
+        high = param.astype(jnp.bfloat16).astype(jnp.float32)
+        rows = jnp.concatenate([high, param - high, f_ref[slot], s_ref[slot]], axis=0)
+        out_ref[slot] = rows.astype(jnp.bfloat16)
+
+
+def join_planes_kernel(place, *refs):
     *from_planes, out_ref = refs
     for k, ref in enumerate(from_planes):
         plane = (place[ZL] + 4 - k) % 4
@@ -181,25 +206,52 @@
         out_ref[k] = rounded
 
 
-def gradient_kernel(place, in_ref, v_ref, out_ref, own_ref, values, rows_a, rows_b):
-    for c in range(2):
-        for g in range(KV):
-            values[c * PLANE : (c + 1) * PLANE, g * HD : (g + 1) * HD] = v_ref[c * KV + g]
-
-    @pl.loop(0, 4)
-    def _(zl):
-        for half, rows in enumerate((rows_a, rows_b)):
-            lhs = in_ref[:, pl.ds(pl.multiple_of(zl * 256 + half * 128, 128), 128)]
-            rows[...] = lax.dot_general(lhs, values[...], TN, preferred_element_type=jnp.float32)
-        for to in range(16):
-            part = jnp.concatenate([rows_a[8 * to : 8 * to + 8, :], rows_b[8 * to : 8 * to + 8, :]], axis=0)
-            out_ref[to * 4 + zl] = part.astype(jnp.bfloat16)
-
-        @pl.when(zl == place[ZL])
-        def _():
-            mine = pl.ds(pl.multiple_of((place[ZH] * 8 + place[Y]) * 8, 8), 8)
-            own_ref[0:8, :] = rows_a[mine, :]
-            own_ref[8:16, :] = rows_b[mine, :]
+def gradient_kernel(behind, place, in_ref, v_ref, *refs):
+    out_ref, own_ref, values, rows_a, rows_b = refs[behind:]
+    zl = pl.program_id(0)
+
+    @pl.when(zl == 0)
+    def _():
+        for c in range(2):
+            for g in range(KV):
+                values[c * PLANE : (c + 1) * PLANE, g * HD : (g + 1) * HD] = v_ref[c * KV + g]
+
+    for half, rows in enumerate((rows_a, rows_b)):
+        lhs = in_ref[:, half * 128 : half * 128 + 128]
+        rows[...] = lax.dot_general(lhs, values[...], TN, preferred_element_type=jnp.float32)
+    for to in range(16):
+        part = jnp.concatenate([rows_a[8 * to : 8 * to + 8, :], rows_b[8 * to : 8 * to + 8, :]], axis=0)
+        out_ref[to, 0] = part.astype(jnp.bfloat16)
+
+    @pl.when(zl == place[ZL])
+    def _():
+        mine = pl.ds(pl.multiple_of((place[ZH] * 8 + place[Y]) * 8, 8), 8)
+        own_ref[0:8, :] = rows_a[mine, :]
+        own_ref[8:16, :] = rows_b[mine, :]
+
+
+def gradient_terms(place, pieces, values, behind):
+    columns = KV * HD
+    parts, own = pl.pallas_call(
+        functools.partial(gradient_kernel, len(behind)),
+        grid=(4,),
+        out_shape=(shape(16, 4, 16, columns), shape(16, columns, dtype=jnp.float32)),
+        in_specs=[
+            SCALARS,
+            pl.BlockSpec((2 * PLANE, 256), lambda i: (0, i)),
+            pl.BlockSpec((8, PLANE, HD), lambda i: (0, 0, 0)),
+            *[ELSEWHERE] * len(behind),
+        ],
+        out_specs=(
+            pl.BlockSpec((16, 1, 16, columns), lambda i: (0, i, 0, 0)),
+            pl.BlockSpec((16, columns), lambda i: (0, 0)),
+        ),
+        scratch_shapes=[pltpu.VMEM((2 * PLANE, columns), jnp.bfloat16)] + [pltpu.VMEM((128, columns), jnp.float32)] * 2,
+        compiler_params=pltpu.CompilerParams(vmem_limit_bytes=8 * MIB),
+        cost_estimate=pl.CostEstimate(flops=1, bytes_accessed=1024, transcendentals=0),
+        name="gradient",
+    )(place, pieces, values, *behind)
+    return parts.reshape(64, 16, columns), own
 
 
 def sum_rows_kernel(place, in_ref, own_ref, out_ref):
@@ -227,8 +279,10 @@
 
             @pl.when(kx == k)
             def _(s_ref=s_ref):
-                for part in range(3):
-                    out_ref[b, part] = s_ref[old // 4, part, slot]
+                rows = s_ref[old // 4, slot].astype(jnp.float32)
+                out_ref[b, 0] = rows[0:4, :] + rows[4:8, :]
+                out_ref[b, 1] = rows[8:12, :]
+                out_ref[b, 2] = rows[12:16, :]
 
 
 def update_kernel(place, new_owner, g_ref, st_ref, p_out, f_out, s_out, w_out, w_rows, changed, count):
@@ -269,18 +323,18 @@
     columns = KV * HD
     place = jnp.stack([lax.axis_index(a) for a in ("zh", "y", "c", "zl", "x")]).astype(jnp.int32)
 
-    packed = call(pack_keys_kernel, "pack_keys", shape(KV, here, HD), [], [keys], [])
-    plane_keys = swapped(packed, "x").reshape(PLANE, HD)
-    packed = call(
-        pack_heads_kernel, "pack_heads", shape(KV, here, 2 * GRP * HD), [], [queries, grad_out], []
-    )
-    heads = swapped(gate(packed, plane_keys), "x")
+    packed = packed_in_hbm(
+        pack_heads_kernel, "pack_heads", shape(KV, here, 2 * GRP * HD), [queries, grad_out], 60
+    )
+    heads = swapped(packed, "x")
+    own, *packed = call(pack_keys_kernel, "pack_keys", (shape(here, HD),) * 4, [place], [keys], [])
+    plane_keys = [own, *(shifted(packed[k - 1], "x", k) for k in (1, 2, 3))]
+    plane_keys = call(join_keys_kernel, "join_keys", shape(PLANE, HD), [place], plane_keys, [])
     all_keys = [plane_keys, *(sent_up(plane_keys, k) for k in (1, 2, 3))]
-    state = [a.transpose(1, 0, 2) for a in (param_old, first_old, second_old)]
-    state = call(stack_kernel, "stack", shape(3, *state[0].shape, dtype=f32), [], state, [])
-    planes = [state, *(old_planes(state, k) for k in (1, 2, 3))]
-    packed = call(pack_inputs_kernel, "pack_inputs", shape(8, here, 1024), [], [inputs], [])
-    pieces = swapped(gate(packed, heads, *all_keys[1:], *planes[1:]), ("c", "x"))
+    packed = packed_in_hbm(
+        pack_inputs_kernel, "pack_inputs", shape(8, here, 1024), [inputs], 1, all_keys[1:]
+    )
+    pieces = swapped(packed, ("c", "x"))
 
     own, *parts = call(
         value_kernel,
@@ -289,26 +343,20 @@
         [place],
         [heads, *all_keys],
         [pltpu.VMEM((4 * PLANE, PLANE), f32)] * 2 + [pltpu.VMEM((4 * PLANE, HD), f32)],
-        limit=24,
+        limit=16,
     )
     parts = [sent_down(parts[k - 1], k) for k in (1, 2, 3)]
     values = call(sum_values_kernel, "sum_values", shape(8, PLANE, HD), [], [own, *parts], [], [pieces])
-    packed = call(
-        pack_states_kernel, "pack_states", shape(3, *state.shape, dtype=f32), [place], planes, [], [values]
-    )
+    state = [a.transpose(1, 0, 2) for a in (param_old, first_old, second_old)]
+    state = call(pack_states_kernel, "pack_states", shape(6, 16, columns), [], state, [], [values])
+    planes = [state, *(old_planes(state, k) for k in (1, 2, 3))]
     values = swapped(values, ("c", "x"))
-    state = [packed, *(shifted(packed, "x", k) for k in (1, 2, 3))]
-
-    parts, own = call(
-        gradient_kernel,
-        "gradient",
-        (shape(64, 16, columns), shape(16, columns, dtype=f32)),
-        [place],
-        [pieces.reshape(2 * PLANE, 1024), values],
-        [pltpu.VMEM((2 * PLANE, columns), jnp.bfloat16)] + [pltpu.VMEM((128, columns), f32)] * 2,
-        state[1:2],
-    )
+
+    parts, own = gradient_terms(place, pieces.reshape(2 * PLANE, 1024), values, planes[1:])
+    state = call(join_planes_kernel, "join_planes", shape(3, 6, 16, columns), [place], planes, [])
+    state = [state, *(shifted(state, "x", k) for k in (1, 2, 3))]
     arrived = swapped(parts, ("zh", "y", "zl"))
+    rows = call(sum_rows_kernel, "sum_rows", shape(32, 2, 4, columns, dtype=f32), [place], [arrived, own], [], state[1:])
     state = call(
         order_kernel,
         "order",
@@ -317,7 +365,6 @@
         state,
         [pltpu.SMEM((16,), jnp.int32)],
     )
-    rows = call(sum_rows_kernel, "sum_rows", shape(32, 2, 4, columns, dtype=f32), [place], [arrived, own], [], [state])
     gradient = swapped(rows, ("c", "zl", "x"))
     block = shape(4, 4, columns, dtype=f32)
     return call(

time: 193 us -> 256 us (1.33)
  Pallas kernels: 20.2 us -> 84.5 us
  blocking collectives: 25.1 us -> 0 us
  starting transfers between devices: 65.7 us -> 84.5 us
  waiting for transfers between devices: 69.8 us -> 77.4 us
  local copies, waits for them, and re-layouts: 10.6 us -> 7.58 us
    pallas_call x2 -> x3, Pallas kernels: 0.01 us -> 67.9 us  [the longest x2 64.9 us: packed_in_hbm(): pl.pallas_call(body, out_shape=out, in_specs=[IN_HBM] * given + [ELSEWHER...]
    all_to_all x1 -> x0, blocking collectives: 25.1 us -> none  [swapped(): return lax.all_to_all(x, axes, split_axis=0, concat_axis=0, tiled=True)]
    all_to_all x5, waiting for transfers between devices: 3.93 us -> 23.5 us  [swapped(): return lax.all_to_all(x, axes, split_axis=0, concat_axis=0, tiled=True)]
    ppermute x3 -> x6, waiting for transfers between devices: 37.3 us -> 24.1 us  [shifted(): return lax.ppermute(x, axis, [(i, (i + k) % n) for i in range(n)])]
    ppermute x3 -> x6, starting transfers between devices: 8.55 us -> 18.9 us  [shifted(): return lax.ppermute(x, axis, [(i, (i + k) % n) for i in range(n)])]
    ppermute x3, starting transfers between devices: 5.96 us -> 15.8 us  [sent_up(): return lax.ppermute(x, 'zl', [(i, i + k) for i in range(4 - k)])]
    ppermute x3, starting transfers between devices: 11.7 us -> 6.58 us  [old_planes(): return lax.ppermute(x, 'zl', [(i, (i + k) % 4) for i in range(3)])]
    all_to_all x5, starting transfers between devices: 35.6 us -> 39.4 us  [swapped(): return lax.all_to_all(x, axes, split_axis=0, concat_axis=0, tiled=True)]
  transfers between devices with their start and end apart: 17 -> 20, of which waited for: 9 -> 13; matrix products, arithmetic and copies ran while one was open for 0% -> 0% of each run, Pallas kernels for 5% -> 4%
where the time goes in v5:
time: 256 us; the launch traced here: 255 us
  Pallas kernels  84.5 us (33%)
  starting transfers between devices  84.5 us (33%)
  waiting for transfers between devices  77.4 us (30%)
  local copies, waits for them, and re-layouts  7.58 us (3%)
    pallas_call x2, Pallas kernels, packed_in_hbm(): pl.pallas_call(body, out_shape=out, in_specs=[IN_HBM] * given + [ELSEWHER...  64.9 us
    all_to_all x5, starting transfers between devices, swapped(): return lax.all_to_all(x, axes, split_axis=0, concat_axis=0, tiled=True)  39.4 us
    ppermute x6, waiting for transfers between devices, shifted(): return lax.ppermute(x, axis, [(i, (i + k) % n) for i in range(n)])  24.1 us
    ppermute x3, waiting for transfers between devices, sent_down(): return lax.ppermute(x, 'zl', [(i, i - k) for i in range(k, 4)])  24 us
    all_to_all x5, waiting for transfers between devices, swapped(): return lax.all_to_all(x, axes, split_axis=0, concat_axis=0, tiled=True)  23.5 us
    ppermute x6, starting transfers between devices, shifted(): return lax.ppermute(x, axis, [(i, (i + k) % n) for i in range(n)])  18.9 us
    pallas_call x9, Pallas kernels, call(): pl.pallas_call(body, out_shape=out, in_specs=[SCALARS] * len(scalars) + [...  16.6 us
    ppermute x3, starting transfers between devices, sent_up(): return lax.ppermute(x, 'zl', [(i, i + k) for i in range(4 - k)])  15.8 us
  transfers between devices with their start and end apart: 20, of which 13 were waited for; matrix products, arithmetic and copies ran while one was open for 0% of the time, Pallas kernels for 4%

profile of v5, /device:TPU:1, one launch (start us, length us, event | category | flops | bytes accessed | tf_op | source)
XLA Modules:
  0.0 254.9 jit_solution(7110563945983622364)
XLA Ops:
  0.6 64.7 %pack_heads.1 = bf16[4,128,2048]{2,1,0:T(8,128)(2,1)} custom-call(bf16[128,4096]{1,0:T(8,128)(2,1)} %refs_0_.3, bf16[128,4096]{1,0:T(8,128)(2,1)} %refs_1_.5), custom_call_target="tpu_custom_call" | custom-call | flops 1 | bytes 1024 | tf_op jit(solution)/shard_map/pack_heads/pallas_call | solution.py:105
  65.4 5.0 %all-to-all-start.1 = ((bf16[4,128,2048]{2,1,0:T(8,128)(2,1)}), bf16[4,128,2048]{2,1,0:T(8,128)(2,1)S(1)}, u32[]{:S(2)}, u32[]{:S(2)}) async-start(bf16[4,128,2048]{2,1,0:T(8,128)(2,1)} %pack_heads.1), calls=%async_computation.1 | async-start | bytes 4194304 | tf_op jit(solution)/shard_map/all_to_all | solution.py:35
  71.0 3.4 %collective-permute-start = (bf16[128,128]{1,0:T(8,128)(2,1)S(1)}, bf16[128,128]{1,0:T(8,128)(2,1)S(1)}, u32[]{:S(2)}, u32[]{:S(2)}) collective-permute-start(bf16[128,128]{1,0:T(8,128)(2,1)S(1)} %get-tuple-element.15), channel_id=1, source_target_pairs={{0,1},{1,2},{2,3},{3,0},{4,5},{5,6},{6,7},{7,4},{8,9},{9,10},{10,1... | collective-permute-start | bytes 98312 | tf_op jit(solution)/shard_map/ppermute | solution.py:40
  74.4 4.3 %collective-permute-start.1 = (bf16[128,128]{1,0:T(8,128)(2,1)S(1)}, bf16[128,128]{1,0:T(8,128)(2,1)S(1)}, u32[]{:S(2)}, u32[]{:S(2)}) collective-permute-start(bf16[128,128]{1,0:T(8,128)(2,1)S(1)} %get-tuple-element.16), channel_id=1, source_target_pairs={{0,2},{1,3},{2,0},{3,1},{4,6},{5,7},{6,4},{7,5},{8,10},{9,11},{10,... | collective-permute-start | bytes 98312 | tf_op jit(solution)/shard_map/ppermute | solution.py:40
  78.7 3.1 %collective-permute-start.2 = (bf16[128,128]{1,0:T(8,128)(2,1)S(1)}, bf16[128,128]{1,0:T(8,128)(2,1)S(1)}, u32[]{:S(2)}, u32[]{:S(2)}) collective-permute-start(bf16[128,128]{1,0:T(8,128)(2,1)S(1)} %get-tuple-element.17), channel_id=1, source_target_pairs={{0,3},{1,0},{2,1},{3,2},{4,7},{5,4},{6,5},{7,6},{8,11},{9,8},{10,9... | collective-permute-start | bytes 98312 | tf_op jit(solution)/shard_map/ppermute | solution.py:40
  81.8 6.6 %collective-permute-done.refs_2_ = bf16[128,128]{1,0:T(8,128)(2,1)S(1)} collective-permute-done((bf16[128,128]{1,0:T(8,128)(2,1)S(1)}, bf16[128,128]{1,0:T(8,128)(2,1)S(1)}, u32[]{:S(2)}, u32[]{:S(2)}) %collective-permute-start) | collective-permute-done | bytes 32800 | tf_op jit(solution)/shard_map/ppermute | solution.py:40
  88.4 4.1 %collective-permute-done.1.refs_3_ = bf16[128,128]{1,0:T(8,128)(2,1)S(1)} collective-permute-done((bf16[128,128]{1,0:T(8,128)(2,1)S(1)}, bf16[128,128]{1,0:T(8,128)(2,1)S(1)}, u32[]{:S(2)}, u32[]{:S(2)}) %collective-permute-start.1) | collective-permute-done | bytes 32800 | tf_op jit(solution)/shard_map/ppermute | solution.py:40
  93.1 12.3 %collective-permute-start.5 = (bf16[512,128]{1,0:T(8,128)(2,1)S(1)}, bf16[512,128]{1,0:T(8,128)(2,1)S(1)}, u32[]{:S(2)}, u32[]{:S(2)}) collective-permute-start(bf16[512,128]{1,0:T(8,128)(2,1)S(1)} %join_keys.1.refs_2_), channel_id=1, source_target_pairs={{0,12},{1,13},{2,14},{3,15},{16,28},{17,29},{18,30},{19,31},{32,44... | collective-permute-start | bytes 393224 | tf_op jit(solution)/shard_map/ppermute | solution.py:44
  106.7 2.2 collective-permute-start.3
  109.2 3.0 %collective-permute-done.3.refs_1_.refs_3_ = bf16[512,128]{1,0:T(8,128)(2,1)S(1)} collective-permute-done((bf16[512,128]{1,0:T(8,128)(2,1)S(1)}, bf16[512,128]{1,0:T(8,128)(2,1)S(1)}, u32[]{:S(2)}, u32[]{:S(2)}) %collective-permute-start.3) | collective-permute-done | bytes 131104 | tf_op jit(solution)/shard_map/ppermute | solution.py:44
  116.8 6.1 %all-to-all-start = ((bf16[8,128,1024]{2,1,0:T(8,128)(2,1)}), bf16[8,128,1024]{2,1,0:T(8,128)(2,1)S(1)}, u32[]{:S(2)}, u32[]{:S(2)}) async-start(bf16[8,128,1024]{2,1,0:T(8,128)(2,1)} %copy-done.2), calls=%async_computation | async-start | bytes 4194304 | tf_op jit(solution)/shard_map/all_to_all | solution.py:35
  124.4 4.7 %values.1 = (f32[512,128]{1,0:T(8,128)S(1)}, bf16[512,128]{1,0:T(8,128)(2,1)S(1)}, bf16[512,128]{1,0:T(8,128)(2,1)S(1)}, bf16[512,128]{1,0:T(8,128)(2,1)S(1)}) custom-call(s32[5]{0:T(128)S(1)} %stack.23.refs_0_.place, bf16[4,128,2048]{2,1,0:T(8,128)(2,1)S(1)} %copy-done.1, bf16[512,128]{1,0:T(8,128)(2,1)S(1)} %join_keys.1.refs_2_, ...), custom_call_target="tpu_custom_call" | custom-call | flops 1 | bytes 1024 | tf_op jit(solution)/shard_map/values/pallas_call | solution.py:61
  133.0 9.5 %collective-permute-done.6.refs_1_ = bf16[512,128]{1,0:T(8,128)(2,1)S(1)} collective-permute-done((bf16[512,128]{1,0:T(8,128)(2,1)S(1)}, bf16[512,128]{1,0:T(8,128)(2,1)S(1)}, u32[]{:S(2)}, u32[]{:S(2)}) %collective-permute-start.6) | collective-permute-done | bytes 131104 | tf_op jit(solution)/shard_map/ppermute | solution.py:48
  142.6 14.4 %collective-permute-done.7.refs_2_ = bf16[512,128]{1,0:T(8,128)(2,1)S(1)} collective-permute-done((bf16[512,128]{1,0:T(8,128)(2,1)S(1)}, bf16[512,128]{1,0:T(8,128)(2,1)S(1)}, u32[]{:S(2)}, u32[]{:S(2)}) %collective-permute-start.7) | collective-permute-done | bytes 131104 | tf_op jit(solution)/shard_map/ppermute | solution.py:48
  158.1 5.1 %all-to-all-start.2 = ((bf16[8,512,128]{2,1,0:T(8,128)(2,1)}), bf16[8,512,128]{2,1,0:T(8,128)(2,1)S(1)}, u32[]{:S(2)}, u32[]{:S(2)}) async-start(bf16[8,512,128]{2,1,0:T(8,128)(2,1)} %sum_values.1.refs_3_), calls=%async_computation.2 | async-start | bytes 2097152 | tf_op jit(solution)/shard_map/all_to_all | solution.py:35
  163.3 1.9 collective-permute-start.11
  165.2 1.9 collective-permute-start.10
  167.1 2.7 %collective-permute-start.9 = (bf16[6,16,512]{2,1,0:T(8,128)(2,1)S(1)}, bf16[6,16,512]{2,1,0:T(8,128)(2,1)S(1)}, u32[]{:S(2)}, u32[]{:S(2)}) collective-permute-start(bf16[6,16,512]{2,1,0:T(8,128)(2,1)S(1)} %pack_states.1.refs_1_), channel_id=1, source_target_pairs={{0,4},{4,8},{8,12},{1,5},{5,9},{9,13},{2,6},{6,10},{10,14},{3,7},{... | collective-permute-start | bytes 294920 | tf_op jit(solution)/shard_map/ppermute | solution.py:52
  169.9 2.5 collective-permute-done.10.refs_1_.refs_3_
  172.4 5.8 %all-to-all-done.2.v_ref = bf16[8,512,128]{2,1,0:T(8,128)(2,1)S(1)} async-done(((bf16[8,512,128]{2,1,0:T(8,128)(2,1)}), bf16[8,512,128]{2,1,0:T(8,128)(2,1)S(1)}, u32[]{:S(2)}, u32[]{:S(2)}) %all-to-all-start.2) | async-done | bytes 1048608 | tf_op jit(solution)/shard_map/all_to_all | solution.py:35
  178.2 3.0 %gradient.1 = (bf16[16,4,16,512]{3,2,1,0:T(8,128)(2,1)S(1)}, f32[16,512]{1,0:T(8,128)S(1)}) custom-call(s32[5]{0:T(128)S(1)} %stack.23.refs_0_.place, bf16[1024,1024]{1,0:T(8,128)(2,1)S(1)} %bitcast.10, bf16[8,512,128]{2,1,0:T(8,128)(2,1)S(1)} %all-to-all-done.2.v_ref, bf16[6,16,512]{2,1,0:T(8,128)(2,1)S(1)} %collective-permute-done.9.refs_0_.refs_2_, ...), custom_call_target="tpu_custom_call" | custom-call | flops 1 | bytes 1024 | tf_op jit(solution)/shard_map/gradient/pallas_call | solution.py:235
  182.8 13.7 %all-to-all-start.3 = ((bf16[64,16,512]{2,1,0:T(8,128)(2,1)}), bf16[64,16,512]{2,1,0:T(8,128)(2,1)S(1)}, u32[]{:S(2)}, u32[]{:S(2)}) async-start(bf16[64,16,512]{2,1,0:T(8,128)(2,1)} %bitcast.11), calls=%async_computation.3 | async-start | bytes 2097152 | tf_op jit(solution)/shard_map/all_to_all | solution.py:35
  197.1 2.9 %collective-permute-start.14 = (bf16[3,6,16,512]{3,2,1,0:T(8,128)(2,1)S(1)}, bf16[3,6,16,512]{3,2,1,0:T(8,128)(2,1)S(1)}, u32[]{:S(2)}, u32[]{:S(2)}) collective-permute-start(bf16[3,6,16,512]{3,2,1,0:T(8,128)(2,1)S(1)} %join_planes.1.refs_2_), channel_id=1, source_target_pairs={{0,3},{1,0},{2,1},{3,2},{4,7},{5,4},{6,5},{7,6},{8,11},{9,8},{10,9... | collective-permute-start | bytes 884744 | tf_op jit(solution)/shard_map/ppermute | solution.py:40
  200.0 3.3 %collective-permute-start.13 = (bf16[3,6,16,512]{3,2,1,0:T(8,128)(2,1)S(1)}, bf16[3,6,16,512]{3,2,1,0:T(8,128)(2,1)S(1)}, u32[]{:S(2)}, u32[]{:S(2)}) collective-permute-start(bf16[3,6,16,512]{3,2,1,0:T(8,128)(2,1)S(1)} %join_planes.1.refs_2_), channel_id=1, source_target_pairs={{0,2},{1,3},{2,0},{3,1},{4,6},{5,7},{6,4},{7,5},{8,10},{9,11},{10,... | collective-permute-start | bytes 884744 | tf_op jit(solution)/shard_map/ppermute | solution.py:40
  203.3 1.9 collective-permute-start.12
  206.9 3.6 %collective-permute-done.13.refs_4_ = bf16[3,6,16,512]{3,2,1,0:T(8,128)(2,1)S(1)} collective-permute-done((bf16[3,6,16,512]{3,2,1,0:T(8,128)(2,1)S(1)}, bf16[3,6,16,512]{3,2,1,0:T(8,128)(2,1)S(1)}, u32[]{:S(2)}, u32[]{:S(2)}) %collective-permute-start.13) | collective-permute-done | bytes 294944 | tf_op jit(solution)/shard_map/ppermute | solution.py:40
  210.5 8.2 %collective-permute-done.12.refs_3_ = bf16[3,6,16,512]{3,2,1,0:T(8,128)(2,1)S(1)} collective-permute-done((bf16[3,6,16,512]{3,2,1,0:T(8,128)(2,1)S(1)}, bf16[3,6,16,512]{3,2,1,0:T(8,128)(2,1)S(1)}, u32[]{:S(2)}, u32[]{:S(2)}) %collective-permute-start.12) | collective-permute-done | bytes 294944 | tf_op jit(solution)/shard_map/ppermute | solution.py:40
  218.7 5.1 %all-to-all-done.3.refs_1_ = bf16[64,16,512]{2,1,0:T(8,128)(2,1)S(1)} async-done(((bf16[64,16,512]{2,1,0:T(8,128)(2,1)}), bf16[64,16,512]{2,1,0:T(8,128)(2,1)S(1)}, u32[]{:S(2)}, u32[]{:S(2)}) %all-to-all-start.3) | async-done | bytes 1048608 | tf_op jit(solution)/shard_map/all_to_all | solution.py:35
  225.3 9.5 %all-to-all-start.4 = ((f32[32,2,4,512]{3,2,1,0:T(4,128)}), f32[32,2,4,512]{3,2,1,0:T(4,128)S(1)}, u32[]{:S(2)}, u32[]{:S(2)}) async-start(f32[32,2,4,512]{3,2,1,0:T(4,128)} %sum_rows.1), calls=%async_computation.4 | async-start | bytes 1048576 | tf_op jit(solution)/shard_map/all_to_all | solution.py:35
  234.8 3.7 %order.1.refs_3_ = f32[64,3,4,512]{3,2,1,0:T(4,128)S(1)} custom-call(s32[5]{0:T(128)S(1)} %stack.23.refs_0_.place, s32[64]{0:T(128)S(1)} %copy-done.11, bf16[3,6,16,512]{3,2,1,0:T(8,128)(2,1)S(1)} %join_planes.1.refs_2_, bf16[3,6,16,512]{3,2,1,0:T(8,128)(2,1)S(1)} %collective-permute-done.12.refs_3_, ...), custom_call_target="tpu_custom_call" | custom-call | flops 1 | bytes 1024 | tf_op jit(solution)/shard_map/order/pallas_call | solution.py:61
  238.5 12.6 %all-to-all-done.4.refs_2_ = f32[32,2,4,512]{3,2,1,0:T(4,128)S(1)} async-done(((f32[32,2,4,512]{3,2,1,0:T(4,128)}), f32[32,2,4,512]{3,2,1,0:T(4,128)S(1)}, u32[]{:S(2)}, u32[]{:S(2)}) %all-to-all-start.4) | async-done | bytes 524320 | tf_op jit(solution)/shard_map/all_to_all | solution.py:35
  251.0 3.9 %update.1 = (f32[4,4,512]{2,1,0:T(4,128)}, f32[4,4,512]{2,1,0:T(4,128)}, f32[4,4,512]{2,1,0:T(4,128)}, bf16[4,64,512]{2,1,0:T(8,128)(2,1)}) custom-call(s32[5]{0:T(128)S(1)} %stack.23.refs_0_.place, s32[64]{0:T(128)S(1)} %copy-done.12, f32[32,2,4,512]{3,2,1,0:T(4,128)S(1)} %all-to-all-done.4.refs_2_, f32[64,3,4,512]{3,2,1,0:T(4,128)S(1)} %order.1.refs_3_), custom_call_target="tpu_custom_call" | custom-call | flops 1 | bytes 1024 | tf_op jit(solution)/shard_map/update/pallas_call | solution.py:61
  (47 shorter events, 19.3 us)
Async XLA Ops:
  65.3 5.1 %copy-start.5 = (bf16[128,512]{1,0:T(8,128)(2,1)S(1)}, bf16[128,512]{1,0:T(8,128)(2,1)}, u32[]{:S(2)}) copy-start(bf16[128,512]{1,0:T(8,128)(2,1)} %refs_1_.4) | copy-start | bytes 393220
  65.4 50.1 %all-to-all-start.1 = ((bf16[4,128,2048]{2,1,0:T(8,128)(2,1)}), bf16[4,128,2048]{2,1,0:T(8,128)(2,1)S(1)}, u32[]{:S(2)}, u32[]{:S(2)}) async-start(bf16[4,128,2048]{2,1,0:T(8,128)(2,1)} %pack_heads.1), calls=%async_computation.1 | async-start | bytes 4194304 | tf_op jit(solution)/shard_map/all_to_all | solution.py:35
  71.0 17.3 %collective-permute-start = (bf16[128,128]{1,0:T(8,128)(2,1)S(1)}, bf16[128,128]{1,0:T(8,128)(2,1)S(1)}, u32[]{:S(2)}, u32[]{:S(2)}) collective-permute-start(bf16[128,128]{1,0:T(8,128)(2,1)S(1)} %get-tuple-element.15), channel_id=1, source_target_pairs={{0,1},{1,2},{2,3},{3,0},{4,5},{5,6},{6,7},{7,4},{8,9},{9,10},{10,1... | collective-permute-start | bytes 98312 | tf_op jit(solution)/shard_map/ppermute | solution.py:40
  74.4 18.1 %collective-permute-start.1 = (bf16[128,128]{1,0:T(8,128)(2,1)S(1)}, bf16[128,128]{1,0:T(8,128)(2,1)S(1)}, u32[]{:S(2)}, u32[]{:S(2)}) collective-permute-start(bf16[128,128]{1,0:T(8,128)(2,1)S(1)} %get-tuple-element.16), channel_id=1, source_target_pairs={{0,2},{1,3},{2,0},{3,1},{4,6},{5,7},{6,4},{7,5},{8,10},{9,11},{10,... | collective-permute-start | bytes 98312 | tf_op jit(solution)/shard_map/ppermute | solution.py:40
  78.7 13.8 %collective-permute-start.2 = (bf16[128,128]{1,0:T(8,128)(2,1)S(1)}, bf16[128,128]{1,0:T(8,128)(2,1)S(1)}, u32[]{:S(2)}, u32[]{:S(2)}) collective-permute-start(bf16[128,128]{1,0:T(8,128)(2,1)S(1)} %get-tuple-element.17), channel_id=1, source_target_pairs={{0,3},{1,0},{2,1},{3,2},{4,7},{5,4},{6,5},{7,6},{8,11},{9,8},{10,9... | collective-permute-start | bytes 98312 | tf_op jit(solution)/shard_map/ppermute | solution.py:40
  93.1 15.9 %collective-permute-start.5 = (bf16[512,128]{1,0:T(8,128)(2,1)S(1)}, bf16[512,128]{1,0:T(8,128)(2,1)S(1)}, u32[]{:S(2)}, u32[]{:S(2)}) collective-permute-start(bf16[512,128]{1,0:T(8,128)(2,1)S(1)} %join_keys.1.refs_2_), channel_id=1, source_target_pairs={{0,12},{1,13},{2,14},{3,15},{16,28},{17,29},{18,30},{19,31},{32,44... | collective-permute-start | bytes 393224 | tf_op jit(solution)/shard_map/ppermute | solution.py:44
  105.4 3.8 %collective-permute-start.4 = (bf16[512,128]{1,0:T(8,128)(2,1)S(1)}, bf16[512,128]{1,0:T(8,128)(2,1)S(1)}, u32[]{:S(2)}, u32[]{:S(2)}) collective-permute-start(bf16[512,128]{1,0:T(8,128)(2,1)S(1)} %join_keys.1.refs_2_), channel_id=1, source_target_pairs={{0,8},{4,12},{1,9},{5,13},{2,10},{6,14},{3,11},{7,15},{16,24},{20,... | collective-permute-start | bytes 393224 | tf_op jit(solution)/shard_map/ppermute | solution.py:44
  106.7 5.5 %collective-permute-start.3 = (bf16[512,128]{1,0:T(8,128)(2,1)S(1)}, bf16[512,128]{1,0:T(8,128)(2,1)S(1)}, u32[]{:S(2)}, u32[]{:S(2)}) collective-permute-start(bf16[512,128]{1,0:T(8,128)(2,1)S(1)} %join_keys.1.refs_2_), channel_id=1, source_target_pairs={{0,4},{4,8},{8,12},{1,5},{5,9},{9,13},{2,6},{6,10},{10,14},{3,7},{... | collective-permute-start | bytes 393224 | tf_op jit(solution)/shard_map/ppermute | solution.py:44
  112.2 1.6 copy-start.3
  114.1 1.4 copy-start.2
  115.4 1.3 copy-start
  116.8 40.2 %all-to-all-start = ((bf16[8,128,1024]{2,1,0:T(8,128)(2,1)}), bf16[8,128,1024]{2,1,0:T(8,128)(2,1)S(1)}, u32[]{:S(2)}, u32[]{:S(2)}) async-start(bf16[8,128,1024]{2,1,0:T(8,128)(2,1)} %copy-done.2), calls=%async_computation | async-start | bytes 4194304 | tf_op jit(solution)/shard_map/all_to_all | solution.py:35
  122.8 1.6 copy-start.1
  129.1 13.4 %collective-permute-start.6 = (bf16[512,128]{1,0:T(8,128)(2,1)S(1)}, bf16[512,128]{1,0:T(8,128)(2,1)S(1)}, u32[]{:S(2)}, u32[]{:S(2)}) collective-permute-start(bf16[512,128]{1,0:T(8,128)(2,1)S(1)} %get-tuple-element.19), channel_id=1, source_target_pairs={{4,0},{8,4},{12,8},{5,1},{9,5},{13,9},{6,2},{10,6},{14,10},{7,3},{... | collective-permute-start | bytes 393224 | tf_op jit(solution)/shard_map/ppermute | solution.py:48
  130.4 26.6 %collective-permute-start.7 = (bf16[512,128]{1,0:T(8,128)(2,1)S(1)}, bf16[512,128]{1,0:T(8,128)(2,1)S(1)}, u32[]{:S(2)}, u32[]{:S(2)}) collective-permute-start(bf16[512,128]{1,0:T(8,128)(2,1)S(1)} %get-tuple-element.20), channel_id=1, source_target_pairs={{8,0},{12,4},{9,1},{13,5},{10,2},{14,6},{11,3},{15,7},{24,16},{28,... | collective-permute-start | bytes 393224 | tf_op jit(solution)/shard_map/ppermute | solution.py:48
  131.7 25.3 %collective-permute-start.8 = (bf16[512,128]{1,0:T(8,128)(2,1)S(1)}, bf16[512,128]{1,0:T(8,128)(2,1)S(1)}, u32[]{:S(2)}, u32[]{:S(2)}) collective-permute-start(bf16[512,128]{1,0:T(8,128)(2,1)S(1)} %get-tuple-element.21), channel_id=1, source_target_pairs={{12,0},{13,1},{14,2},{15,3},{28,16},{29,17},{30,18},{31,19},{44,32... | collective-permute-start | bytes 393224 | tf_op jit(solution)/shard_map/ppermute | solution.py:48
  157.0 6.2 %copy-start.6 = (f32[4,6,512]{2,0,1:T(4,128)S(1)}, f32[4,6,512]{2,0,1:T(4,128)}, u32[]{:S(2)}) copy-start(f32[4,6,512]{2,0,1:T(4,128)} %param.15) | copy-start | bytes 147460
  157.0 6.2 %copy-start.7 = (f32[4,6,512]{2,0,1:T(4,128)S(1)}, f32[4,6,512]{2,0,1:T(4,128)}, u32[]{:S(2)}) copy-start(f32[4,6,512]{2,0,1:T(4,128)} %param.16) | copy-start | bytes 147460
  157.0 6.2 %copy-start.8 = (f32[4,6,512]{2,0,1:T(4,128)S(1)}, f32[4,6,512]{2,0,1:T(4,128)}, u32[]{:S(2)}) copy-start(f32[4,6,512]{2,0,1:T(4,128)} %param.17) | copy-start | bytes 147460
  158.1 20.1 %all-to-all-start.2 = ((bf16[8,512,128]{2,1,0:T(8,128)(2,1)}), bf16[8,512,128]{2,1,0:T(8,128)(2,1)S(1)}, u32[]{:S(2)}, u32[]{:S(2)}) async-start(bf16[8,512,128]{2,1,0:T(8,128)(2,1)} %sum_values.1.refs_3_), calls=%async_computation.2 | async-start | bytes 2097152 | tf_op jit(solution)/shard_map/all_to_all | solution.py:35
  163.3 6.6 %collective-permute-start.11 = (bf16[6,16,512]{2,1,0:T(8,128)(2,1)S(1)}, bf16[6,16,512]{2,1,0:T(8,128)(2,1)S(1)}, u32[]{:S(2)}, u32[]{:S(2)}) collective-permute-start(bf16[6,16,512]{2,1,0:T(8,128)(2,1)S(1)} %pack_states.1.refs_1_), channel_id=1, source_target_pairs={{0,12},{4,0},{8,4},{1,13},{5,1},{9,5},{2,14},{6,2},{10,6},{3,15},{... | collective-permute-start | bytes 294920 | tf_op jit(solution)/shard_map/ppermute | solution.py:52
  165.2 7.2 %collective-permute-start.10 = (bf16[6,16,512]{2,1,0:T(8,128)(2,1)S(1)}, bf16[6,16,512]{2,1,0:T(8,128)(2,1)S(1)}, u32[]{:S(2)}, u32[]{:S(2)}) collective-permute-start(bf16[6,16,512]{2,1,0:T(8,128)(2,1)S(1)} %pack_states.1.refs_1_), channel_id=1, source_target_pairs={{0,8},{4,12},{8,0},{1,9},{5,13},{9,1},{2,10},{6,14},{10,2},{3,11},... | collective-permute-start | bytes 294920 | tf_op jit(solution)/shard_map/ppermute | solution.py:52
  167.1 5.3 %collective-permute-start.9 = (bf16[6,16,512]{2,1,0:T(8,128)(2,1)S(1)}, bf16[6,16,512]{2,1,0:T(8,128)(2,1)S(1)}, u32[]{:S(2)}, u32[]{:S(2)}) collective-permute-start(bf16[6,16,512]{2,1,0:T(8,128)(2,1)S(1)} %pack_states.1.refs_1_), channel_id=1, source_target_pairs={{0,4},{4,8},{8,12},{1,5},{5,9},{9,13},{2,6},{6,10},{10,14},{3,7},{... | collective-permute-start | bytes 294920 | tf_op jit(solution)/shard_map/ppermute | solution.py:52
  181.8 1.0 copy-start.4
  182.8 41.0 %copy-start.10 = (f32[16,512]{1,0:T(8,128)S(1)}, f32[16,512]{1,0:T(8,128)}, u32[]{:S(2)}) copy-start(f32[16,512]{1,0:T(8,128)} %copy-done.9) | copy-start | bytes 98308
  182.8 41.0 %all-to-all-start.3 = ((bf16[64,16,512]{2,1,0:T(8,128)(2,1)}), bf16[64,16,512]{2,1,0:T(8,128)(2,1)S(1)}, u32[]{:S(2)}, u32[]{:S(2)}) async-start(bf16[64,16,512]{2,1,0:T(8,128)(2,1)} %bitcast.11), calls=%async_computation.3 | async-start | bytes 2097152 | tf_op jit(solution)/shard_map/all_to_all | solution.py:35
  196.5 38.3 %copy-start.11 = (s32[64]{0:T(128)S(1)}, s32[64]{0:T(128)}, u32[]{:S(2)}) copy-start(s32[64]{0:T(128)} %refs_1_.6) | copy-start | bytes 772
  197.1 9.8 %collective-permute-start.14 = (bf16[3,6,16,512]{3,2,1,0:T(8,128)(2,1)S(1)}, bf16[3,6,16,512]{3,2,1,0:T(8,128)(2,1)S(1)}, u32[]{:S(2)}, u32[]{:S(2)}) collective-permute-start(bf16[3,6,16,512]{3,2,1,0:T(8,128)(2,1)S(1)} %join_planes.1.refs_2_), channel_id=1, source_target_pairs={{0,3},{1,0},{2,1},{3,2},{4,7},{5,4},{6,5},{7,6},{8,11},{9,8},{10,9... | collective-permute-start | bytes 884744 | tf_op jit(solution)/shard_map/ppermute | solution.py:40
  200.0 10.5 %collective-permute-start.13 = (bf16[3,6,16,512]{3,2,1,0:T(8,128)(2,1)S(1)}, bf16[3,6,16,512]{3,2,1,0:T(8,128)(2,1)S(1)}, u32[]{:S(2)}, u32[]{:S(2)}) collective-permute-start(bf16[3,6,16,512]{3,2,1,0:T(8,128)(2,1)S(1)} %join_planes.1.refs_2_), channel_id=1, source_target_pairs={{0,2},{1,3},{2,0},{3,1},{4,6},{5,7},{6,4},{7,5},{8,10},{9,11},{10,... | collective-permute-start | bytes 884744 | tf_op jit(solution)/shard_map/ppermute | solution.py:40
  203.3 15.4 %collective-permute-start.12 = (bf16[3,6,16,512]{3,2,1,0:T(8,128)(2,1)S(1)}, bf16[3,6,16,512]{3,2,1,0:T(8,128)(2,1)S(1)}, u32[]{:S(2)}, u32[]{:S(2)}) collective-permute-start(bf16[3,6,16,512]{3,2,1,0:T(8,128)(2,1)S(1)} %join_planes.1.refs_2_), channel_id=1, source_target_pairs={{0,1},{1,2},{2,3},{3,0},{4,5},{5,6},{6,7},{7,4},{8,9},{9,10},{10,1... | collective-permute-start | bytes 884744 | tf_op jit(solution)/shard_map/ppermute | solution.py:40
  225.3 25.7 %copy-start.12 = (s32[64]{0:T(128)S(1)}, s32[64]{0:T(128)}, u32[]{:S(2)}) copy-start(s32[64]{0:T(128)} %refs_1_.7) | copy-start | bytes 772
  225.3 25.7 %all-to-all-start.4 = ((f32[32,2,4,512]{3,2,1,0:T(4,128)}), f32[32,2,4,512]{3,2,1,0:T(4,128)S(1)}, u32[]{:S(2)}, u32[]{:S(2)}) async-start(f32[32,2,4,512]{3,2,1,0:T(4,128)} %sum_rows.1), calls=%async_computation.4 | async-start | bytes 1048576 | tf_op jit(solution)/shard_map/all_to_all | solution.py:35
  (1 other events, 0.6 us)

commit v6 on v5

--- a/solution.py
+++ b/solution.py
@@ -24,7 +24,6 @@
 CHUNK = 256
 ZH, Y, C, ZL, X = range(5)
 WHOLE = pl.BlockSpec(memory_space=pltpu.VMEM)
-IN_HBM = pl.BlockSpec(memory_space=pltpu.HBM)
 ELSEWHERE = pl.BlockSpec(memory_space=pl.ANY)
 SCALARS = pl.BlockSpec(memory_space=pltpu.SMEM)
 NT = (((1,), (1,)), ((), ()))
@@ -74,55 +73,21 @@
     return jax.ShapeDtypeStruct(dims, dtype)
 
 
-def copy_all(pairs, done):
-    copies = [pltpu.make_async_copy(a, b, done.at[i]) for i, (a, b) in enumerate(pairs)]
-    for copy in copies:
-        copy.start()
-    for copy in copies:
-        copy.wait()
-
-
-def pack_heads_kernel(q_ref, d_ref, out_ref, done):
+def pack_heads_kernel(q_ref, d_ref, out_ref):
     width = GRP * HD
-    pairs = []
     for g in range(KV):
-        at = pl.ds(g * width, width)
-        pairs.append((q_ref.at[:, at], out_ref.at[g, :, pl.ds(0, width)]))
-        pairs.append((d_ref.at[:, at], out_ref.at[g, :, pl.ds(width, width)]))
-    copy_all(pairs, done)
-
-
-def pack_inputs_kernel(in_ref, out_ref, done):
-    copy_all([(in_ref.at[:, pl.ds(k * 1024, 1024)], out_ref.at[k]) for k in range(8)], done)
-
-
-def packed_in_hbm(kernel, name, out, arrays, limit, behind=()):
-    given = len(arrays)
-
-    def body(*refs):
-        kernel(*refs[:given], *refs[given + len(behind) :])
-
-    return pl.pallas_call(
-        body,
-        out_shape=out,
-        in_specs=[IN_HBM] * given + [ELSEWHERE] * len(behind),
-        out_specs=IN_HBM,
-        scratch_shapes=[pltpu.SemaphoreType.DMA((8,))],
-        compiler_params=pltpu.CompilerParams(vmem_limit_bytes=limit * MIB),
-        cost_estimate=pl.CostEstimate(flops=1, bytes_accessed=1024, transcendentals=0),
-        name=name,
-    )(*arrays, *behind)
-
-
-def pack_keys_kernel(place, k_ref, *out):
-    for k, ref in enumerate(out):
-        ref[...] = k_ref[:, pl.ds(pl.multiple_of(((place[X] + k) % 4) * HD, HD), HD)]
-
-
-def join_keys_kernel(place, *refs):
-    *parts, out_ref = refs
-    for k, part in enumerate(parts):
-        out_ref[pl.ds(pl.multiple_of(((place[X] + 4 - k) % 4) * 128, 128), 128), :] = part[...]
+        out_ref[g, :, 0:width] = q_ref[:, g * width : (g + 1) * width]
+        out_ref[g, :, width:] = d_ref[:, g * width : (g + 1) * width]
+
+
+def pack_inputs_kernel(in_ref, out_ref):
+    for k in range(8):
+        out_ref[k] = in_ref[:, k * 1024 : (k + 1) * 1024]
+
+
+def pack_keys_kernel(k_ref, out_ref):
+    for g in range(KV):
+        out_ref[g] = k_ref[:, g * HD : (g + 1) * HD]
 
 
 def pack_states_kernel(p_ref, f_ref, s_ref, out_ref):
@@ -143,7 +108,7 @@
             out_ref[plane] = ref[...]
 
 
-def value_kernel(place, heads, k0, k1, k2, k3, own_ref, down1, down2, down3, s_a, s_b, total):
+def value_kernel(place, heads, k0, k1, k2, k3, own_ref, down1, down2, down3, s_a, s_b, total, tops):
     plane = place[ZL]
     factor = HD**-0.5 * LOG2E
     width = GRP * HD
@@ -152,45 +117,69 @@
         at = pl.ds(pl.multiple_of(start, HD), HD)
         return heads[:, :, at].reshape(PLANE, HD)
 
-    def scores(h, last, s_ref):
-        q = columns(h * HD)
-        top = jnp.full((8, PLANE), -jnp.inf, jnp.float32)
-        for at in range(0, (last + 1) * PLANE, CHUNK):
-            k_ref = (k0, k1, k2, k3)[last - at // PLANE]
-            k = k_ref[at % PLANE : at % PLANE + CHUNK, :]
-            s = lax.dot_general(k, q, NT, preferred_element_type=jnp.float32)
-            if at >= last * PLANE:
-                key = lax.broadcasted_iota(jnp.int32, s.shape, 0) + (at - last * PLANE)
-                s = jnp.where(key <= lax.broadcasted_iota(jnp.int32, s.shape, 1), s, -jnp.inf)
-            s_ref[at : at + CHUNK, :] = s
-            top = jnp.maximum(top, jnp.max(s.reshape(CHUNK // 8, 8, PLANE), axis=0))
+    def scores(q, at, last, s_ref, top):
+        k_ref = (k0, k1, k2, k3)[last - at // PLANE]
+        k = k_ref[at % PLANE : at % PLANE + CHUNK, :]
+        s = lax.dot_general(k, q, NT, preferred_element_type=jnp.float32)
+        if at >= last * PLANE:
+            key = lax.broadcasted_iota(jnp.int32, s.shape, 0) + (at - last * PLANE)
+            s = jnp.where(key <= lax.broadcasted_iota(jnp.int32, s.shape, 1), s, -jnp.inf)
+        s_ref[at : at + CHUNK, :] = s
+        return jnp.maximum(top, jnp.max(s.reshape(CHUNK // 8, 8, PLANE), axis=0))
+
+    def powers(at, s_ref, top, size):
+        w = jnp.exp2((s_ref[at : at + CHUNK, :] - top) * factor)
+        s_ref[at : at + CHUNK, :] = w
+        return size + jnp.sum(w.reshape(CHUNK // 8, 8, PLANE), axis=0)
+
+    def add_terms(d, at, s_ref, inverse):
+        p = (s_ref[at : at + CHUNK, :] * inverse).astype(jnp.bfloat16)
+        total[at : at + CHUNK, :] += jnp.dot(p, d, preferred_element_type=jnp.float32)
+
+    lowest = jnp.full((8, PLANE), -jnp.inf, jnp.float32)
+    nothing = jnp.zeros((8, PLANE), jnp.float32)
+
+    def largest(top):
         return jnp.max(top, axis=0, keepdims=True)
 
-    def add_terms(h, last, s_ref, top):
-        d = columns(h * HD + width)
-        size = jnp.zeros((8, PLANE), jnp.float32)
-        for at in range(0, (last + 1) * PLANE, CHUNK):
-            w = jnp.exp2((s_ref[at : at + CHUNK, :] - top) * factor)
-            s_ref[at : at + CHUNK, :] = w
-            size = size + jnp.sum(w.reshape(CHUNK // 8, 8, PLANE), axis=0)
-        inverse = 1.0 / jnp.sum(size, axis=0, keepdims=True)
-        for at in range(0, (last + 1) * PLANE, CHUNK):
-            p = (s_ref[at : at + CHUNK, :] * inverse).astype(jnp.bfloat16)
-            total[at : at + CHUNK, :] += jnp.dot(p, d, preferred_element_type=jnp.float32)
+    def inverse_of(size):
+        return 1.0 / jnp.sum(size, axis=0, keepdims=True)
 
     for last in range(4):
 
         @pl.when(plane == last)
         def _(last=last):
             used = (last + 1) * PLANE
+            chunks = range(0, used, CHUNK)
             total[0:used, :] = jnp.zeros((used, HD), jnp.float32)
+            top = lowest
+            q = columns(0)
+            for at in chunks:
+                top = scores(q, at, last, s_a, top)
+            tops[...] = largest(top)
 
             @pl.loop(0, GRP // 2)
             def _(pair):
-                top_a = scores(2 * pair, last, s_a)
-                top_b = scores(2 * pair + 1, last, s_b)
-                add_terms(2 * pair, last, s_a, top_a)
-                add_terms(2 * pair + 1, last, s_b, top_b)
+                top_a = tops[...]
+                q = columns((2 * pair + 1) * HD)
+                top, size_a = lowest, nothing
+                for at in chunks:
+                    top = scores(q, at, last, s_b, top)
+                    size_a = powers(at, s_a, top_a, size_a)
+                top_b, inverse = largest(top), inverse_of(size_a)
+                d = columns(2 * pair * HD + width)
+                size_b = nothing
+                for at in chunks:
+                    add_terms(d, at, s_a, inverse)
+                    size_b = powers(at, s_b, top_b, size_b)
+                inverse = inverse_of(size_b)
+                d = columns((2 * pair + 1) * HD + width)
+                q = columns(jnp.minimum(2 * pair + 2, GRP - 1) * HD)
+                top = lowest
+                for at in chunks:
+                    add_terms(d, at, s_b, inverse)
+                    top = scores(q, at, last, s_a, top)
+                tops[...] = largest(top)
 
             own_ref[...] = total[last * PLANE : used, :]
             for k, out in enumerate((down1, down2, down3)[:last], 1):
@@ -323,16 +312,15 @@
     columns = KV * HD
     place = jnp.stack([lax.axis_index(a) for a in ("zh", "y", "c", "zl", "x")]).astype(jnp.int32)
 
-    packed = packed_in_hbm(
-        pack_heads_kernel, "pack_heads", shape(KV, here, 2 * GRP * HD), [queries, grad_out], 60
+    packed = call(pack_keys_kernel, "pack_keys", shape(KV, here, HD), [], [keys], [])
+    plane_keys = swapped(packed, "x").reshape(PLANE, HD)
+    packed = call(
+        pack_heads_kernel, "pack_heads", shape(KV, here, 2 * GRP * HD), [], [queries, grad_out], []
     )
     heads = swapped(packed, "x")
-    own, *packed = call(pack_keys_kernel, "pack_keys", (shape(here, HD),) * 4, [place], [keys], [])
-    plane_keys = [own, *(shifted(packed[k - 1], "x", k) for k in (1, 2, 3))]
-    plane_keys = call(join_keys_kernel, "join_keys", shape(PLANE, HD), [place], plane_keys, [])
     all_keys = [plane_keys, *(sent_up(plane_keys, k) for k in (1, 2, 3))]
-    packed = packed_in_hbm(
-        pack_inputs_kernel, "pack_inputs", shape(8, here, 1024), [inputs], 1, all_keys[1:]
+    packed = call(
+        pack_inputs_kernel, "pack_inputs", shape(8, here, 1024), [], [inputs], [], all_keys[1:]
     )
     pieces = swapped(packed, ("c", "x"))
 
@@ -342,7 +330,7 @@
         (shape(PLANE, HD, dtype=f32), *(shape(PLANE, HD),) * 3),
         [place],
         [heads, *all_keys],
-        [pltpu.VMEM((4 * PLANE, PLANE), f32)] * 2 + [pltpu.VMEM((4 * PLANE, HD), f32)],
+        [pltpu.VMEM((4 * PLANE, PLANE), f32)] * 2 + [pltpu.VMEM((4 * PLANE, HD), f32), pltpu.VMEM((1, PLANE), f32)],
         limit=16,
     )
     parts = [sent_down(parts[k - 1], k) for k in (1, 2, 3)]

time: 256 us -> 182 us (0.71)
  Pallas kernels: 84.5 us -> 20 us
  waiting for transfers between devices: 77.4 us -> 70.2 us
  starting transfers between devices: 84.5 us -> 77.6 us
  local copies, waits for them, and re-layouts: 7.58 us -> 12.2 us
    pallas_call x2 -> x0, Pallas kernels: 64.9 us -> none  [packed_in_hbm(): pl.pallas_call(body, out_shape=out, in_specs=[IN_HBM] * given + [ELSEWHER...]
    ppermute x6 -> x3, starting transfers between devices: 18.9 us -> 8.09 us  [shifted(): return lax.ppermute(x, axis, [(i, (i + k) % n) for i in range(n)])]
    ppermute x6 -> x3, waiting for transfers between devices: 24.1 us -> 13.4 us  [shifted(): return lax.ppermute(x, axis, [(i, (i + k) % n) for i in range(n)])]
    all_to_all x5 -> x6, starting transfers between devices: 39.4 us -> 47.9 us  [swapped(): return lax.all_to_all(x, axes, split_axis=0, concat_axis=0, tiled=True)]
    ppermute x3, starting transfers between devices: 15.8 us -> 11.1 us  [sent_up(): return lax.ppermute(x, 'zl', [(i, i + k) for i in range(4 - k)])]
    unnamed x26 -> x32, local copies, waits for them, and re-layouts: 7.49 us -> 12.2 us
    all_to_all x5 -> x6, waiting for transfers between devices: 23.5 us -> 26.4 us  [swapped(): return lax.all_to_all(x, axes, split_axis=0, concat_axis=0, tiled=True)]
    pallas_call x9 -> x10, Pallas kernels: 16.6 us -> 17 us  [call(): pl.pallas_call(body, out_shape=out, in_specs=[SCALARS] * len(scalars) + [...]
  transfers between devices with their start and end apart: 20 -> 18, of which waited for: 13 -> 13; matrix products, arithmetic and copies ran while one was open for 0% -> 0% of each run, Pallas kernels for 4% -> 5%
where the time goes in v6:
time: 182 us; the launch traced here: 181 us
  starting transfers between devices  77.6 us (43%)
  waiting for transfers between devices  70.2 us (39%)
  Pallas kernels  20 us (11%)
  local copies, waits for them, and re-layouts  12.2 us (7%)
    all_to_all x6, starting transfers between devices, swapped(): return lax.all_to_all(x, axes, split_axis=0, concat_axis=0, tiled=True)  47.9 us
    all_to_all x6, waiting for transfers between devices, swapped(): return lax.all_to_all(x, axes, split_axis=0, concat_axis=0, tiled=True)  26.4 us
    ppermute x3, waiting for transfers between devices, sent_down(): return lax.ppermute(x, 'zl', [(i, i - k) for i in range(k, 4)])  24.5 us
    pallas_call x10, Pallas kernels, call(): pl.pallas_call(body, out_shape=out, in_specs=[SCALARS] * len(scalars) + [...  17 us
    ppermute x3, waiting for transfers between devices, shifted(): return lax.ppermute(x, axis, [(i, (i + k) % n) for i in range(n)])  13.4 us
    unnamed x32, local copies, waits for them, and re-layouts  12.2 us
    ppermute x3, starting transfers between devices, sent_up(): return lax.ppermute(x, 'zl', [(i, i + k) for i in range(4 - k)])  11.1 us
    ppermute x3, starting transfers between devices, shifted(): return lax.ppermute(x, axis, [(i, (i + k) % n) for i in range(n)])  8.09 us
  transfers between devices with their start and end apart: 18, of which 13 were waited for; matrix products, arithmetic and copies ran while one was open for 0% of the time, Pallas kernels for 5%

profile of v6, /device:TPU:1, one launch (start us, length us, event | category | flops | bytes accessed | tf_op | source)
XLA Modules:
  0.0 180.9 jit_solution(12743371736168039428)
XLA Ops:
  2.2 4.8 %all-to-all-start = ((bf16[4,128,128]{2,1,0:T(8,128)(2,1)}), bf16[4,128,128]{2,1,0:T(8,128)(2,1)S(1)}, u32[]{:S(2)}, u32[]{:S(2)}) async-start(bf16[4,128,128]{2,1,0:T(8,128)(2,1)} %pack_keys.1), calls=%async_computation | async-start | bytes 262144 | tf_op jit(solution)/shard_map/all_to_all | solution.py:34
  11.9 3.6 %all-to-all-start.2 = ((bf16[4,128,2048]{2,1,0:T(8,128)(2,1)}), bf16[4,128,2048]{2,1,0:T(8,128)(2,1)S(1)}, u32[]{:S(2)}, u32[]{:S(2)}) async-start(bf16[4,128,2048]{2,1,0:T(8,128)(2,1)} %copy-done.3), calls=%async_computation.2 | async-start | bytes 4194304 | tf_op jit(solution)/shard_map/all_to_all | solution.py:34
  15.5 7.6 %collective-permute-start.2 = (bf16[512,128]{1,0:T(8,128)(2,1)S(1)}, bf16[512,128]{1,0:T(8,128)(2,1)S(1)}, u32[]{:S(2)}, u32[]{:S(2)}) collective-permute-start(bf16[512,128]{1,0:T(8,128)(2,1)S(1)} %bitcast.13), channel_id=1, source_target_pairs={{0,12},{1,13},{2,14},{3,15},{16,28},{17,29},{18,30},{19,31},{32,44... | collective-permute-start | bytes 393224 | tf_op jit(solution)/shard_map/ppermute | solution.py:43
  24.4 2.2 %collective-permute-start = (bf16[512,128]{1,0:T(8,128)(2,1)S(1)}, bf16[512,128]{1,0:T(8,128)(2,1)S(1)}, u32[]{:S(2)}, u32[]{:S(2)}) collective-permute-start(bf16[512,128]{1,0:T(8,128)(2,1)S(1)} %bitcast.15), channel_id=1, source_target_pairs={{0,4},{4,8},{8,12},{1,5},{5,9},{9,13},{2,6},{6,10},{10,14},{3,7},{... | collective-permute-start | bytes 393224 | tf_op jit(solution)/shard_map/ppermute | solution.py:43
  26.7 3.2 %collective-permute-done.refs_1_.refs_3_ = bf16[512,128]{1,0:T(8,128)(2,1)S(1)} collective-permute-done((bf16[512,128]{1,0:T(8,128)(2,1)S(1)}, bf16[512,128]{1,0:T(8,128)(2,1)S(1)}, u32[]{:S(2)}, u32[]{:S(2)}) %collective-permute-start) | collective-permute-done | bytes 131104 | tf_op jit(solution)/shard_map/ppermute | solution.py:43
  29.9 1.6 copy-done.4
  33.0 2.1 %all-to-all-done.2.refs_1_ = bf16[4,128,2048]{2,1,0:T(8,128)(2,1)S(1)} async-done(((bf16[4,128,2048]{2,1,0:T(8,128)(2,1)}), bf16[4,128,2048]{2,1,0:T(8,128)(2,1)S(1)}, u32[]{:S(2)}, u32[]{:S(2)}) %all-to-all-start.2) | async-done | bytes 2097184 | tf_op jit(solution)/shard_map/all_to_all | solution.py:34
  36.4 11.2 %all-to-all-start.1 = ((bf16[8,128,1024]{2,1,0:T(8,128)(2,1)}), bf16[8,128,1024]{2,1,0:T(8,128)(2,1)S(1)}, u32[]{:S(2)}, u32[]{:S(2)}) async-start(bf16[8,128,1024]{2,1,0:T(8,128)(2,1)} %copy-done), calls=%async_computation.1 | async-start | bytes 4194304 | tf_op jit(solution)/shard_map/all_to_all | solution.py:34
  47.7 1.6 copy-done.2
  49.3 5.3 %values.1 = (f32[512,128]{1,0:T(8,128)S(1)}, bf16[512,128]{1,0:T(8,128)(2,1)S(1)}, bf16[512,128]{1,0:T(8,128)(2,1)S(1)}, bf16[512,128]{1,0:T(8,128)(2,1)S(1)}) custom-call(s32[5]{0:T(128)S(1)} %stack.23.refs_0_.place, bf16[4,128,2048]{2,1,0:T(8,128)(2,1)S(1)} %copy-done.2, bf16[512,128]{1,0:T(8,128)(2,1)S(1)} %bitcast.16, ...), custom_call_target="tpu_custom_call" | custom-call | flops 1 | bytes 1024 | tf_op jit(solution)/shard_map/values/pallas_call | solution.py:60
  58.5 8.0 %collective-permute-done.3.refs_1_ = bf16[512,128]{1,0:T(8,128)(2,1)S(1)} collective-permute-done((bf16[512,128]{1,0:T(8,128)(2,1)S(1)}, bf16[512,128]{1,0:T(8,128)(2,1)S(1)}, u32[]{:S(2)}, u32[]{:S(2)}) %collective-permute-start.3) | collective-permute-done | bytes 131104 | tf_op jit(solution)/shard_map/ppermute | solution.py:47
  66.6 8.6 %collective-permute-done.4.refs_2_ = bf16[512,128]{1,0:T(8,128)(2,1)S(1)} collective-permute-done((bf16[512,128]{1,0:T(8,128)(2,1)S(1)}, bf16[512,128]{1,0:T(8,128)(2,1)S(1)}, u32[]{:S(2)}, u32[]{:S(2)}) %collective-permute-start.4) | collective-permute-done | bytes 131104 | tf_op jit(solution)/shard_map/ppermute | solution.py:47
  75.1 7.9 %collective-permute-done.5.refs_3_ = bf16[512,128]{1,0:T(8,128)(2,1)S(1)} collective-permute-done((bf16[512,128]{1,0:T(8,128)(2,1)S(1)}, bf16[512,128]{1,0:T(8,128)(2,1)S(1)}, u32[]{:S(2)}, u32[]{:S(2)}) %collective-permute-start.5) | collective-permute-done | bytes 131104 | tf_op jit(solution)/shard_map/ppermute | solution.py:47
  84.1 5.1 %all-to-all-start.3 = ((bf16[8,512,128]{2,1,0:T(8,128)(2,1)}), bf16[8,512,128]{2,1,0:T(8,128)(2,1)S(1)}, u32[]{:S(2)}, u32[]{:S(2)}) async-start(bf16[8,512,128]{2,1,0:T(8,128)(2,1)} %sum_values.1.refs_3_), calls=%async_computation.3 | async-start | bytes 2097152 | tf_op jit(solution)/shard_map/all_to_all | solution.py:34
  89.3 1.9 %collective-permute-start.8 = (bf16[6,16,512]{2,1,0:T(8,128)(2,1)S(1)}, bf16[6,16,512]{2,1,0:T(8,128)(2,1)S(1)}, u32[]{:S(2)}, u32[]{:S(2)}) collective-permute-start(bf16[6,16,512]{2,1,0:T(8,128)(2,1)S(1)} %pack_states.1.refs_1_), channel_id=1, source_target_pairs={{0,12},{4,0},{8,4},{1,13},{5,1},{9,5},{2,14},{6,2},{10,6},{3,15},{... | collective-permute-start | bytes 294920 | tf_op jit(solution)/shard_map/ppermute | solution.py:51
  91.2 1.9 %collective-permute-start.7 = (bf16[6,16,512]{2,1,0:T(8,128)(2,1)S(1)}, bf16[6,16,512]{2,1,0:T(8,128)(2,1)S(1)}, u32[]{:S(2)}, u32[]{:S(2)}) collective-permute-start(bf16[6,16,512]{2,1,0:T(8,128)(2,1)S(1)} %pack_states.1.refs_1_), channel_id=1, source_target_pairs={{0,8},{4,12},{8,0},{1,9},{5,13},{9,1},{2,10},{6,14},{10,2},{3,11},... | collective-permute-start | bytes 294920 | tf_op jit(solution)/shard_map/ppermute | solution.py:51
  93.1 2.7 %collective-permute-start.6 = (bf16[6,16,512]{2,1,0:T(8,128)(2,1)S(1)}, bf16[6,16,512]{2,1,0:T(8,128)(2,1)S(1)}, u32[]{:S(2)}, u32[]{:S(2)}) collective-permute-start(bf16[6,16,512]{2,1,0:T(8,128)(2,1)S(1)} %pack_states.1.refs_1_), channel_id=1, source_target_pairs={{0,4},{4,8},{8,12},{1,5},{5,9},{9,13},{2,6},{6,10},{10,14},{3,7},{... | collective-permute-start | bytes 294920 | tf_op jit(solution)/shard_map/ppermute | solution.py:51
  95.9 2.5 %collective-permute-done.7.refs_1_.refs_3_ = bf16[6,16,512]{2,1,0:T(8,128)(2,1)S(1)} collective-permute-done((bf16[6,16,512]{2,1,0:T(8,128)(2,1)S(1)}, bf16[6,16,512]{2,1,0:T(8,128)(2,1)S(1)}, u32[]{:S(2)}, u32[]{:S(2)}) %collective-permute-start.7) | collective-permute-done | bytes 98336 | tf_op jit(solution)/shard_map/ppermute | solution.py:51
  98.4 5.8 %all-to-all-done.3.v_ref = bf16[8,512,128]{2,1,0:T(8,128)(2,1)S(1)} async-done(((bf16[8,512,128]{2,1,0:T(8,128)(2,1)}), bf16[8,512,128]{2,1,0:T(8,128)(2,1)S(1)}, u32[]{:S(2)}, u32[]{:S(2)}) %all-to-all-start.3) | async-done | bytes 1048608 | tf_op jit(solution)/shard_map/all_to_all | solution.py:34
  104.2 3.0 %gradient.1 = (bf16[16,4,16,512]{3,2,1,0:T(8,128)(2,1)S(1)}, f32[16,512]{1,0:T(8,128)S(1)}) custom-call(s32[5]{0:T(128)S(1)} %stack.23.refs_0_.place, bf16[1024,1024]{1,0:T(8,128)(2,1)S(1)} %bitcast.11, bf16[8,512,128]{2,1,0:T(8,128)(2,1)S(1)} %all-to-all-done.3.v_ref, bf16[6,16,512]{2,1,0:T(8,128)(2,1)S(1)} %collective-permute-done.6.refs_0_.refs_2_, ...), custom_call_target="tpu_custom_call" | custom-call | flops 1 | bytes 1024 | tf_op jit(solution)/shard_map/gradient/pallas_call | solution.py:224
  108.8 13.7 %all-to-all-start.4 = ((bf16[64,16,512]{2,1,0:T(8,128)(2,1)}), bf16[64,16,512]{2,1,0:T(8,128)(2,1)S(1)}, u32[]{:S(2)}, u32[]{:S(2)}) async-start(bf16[64,16,512]{2,1,0:T(8,128)(2,1)} %bitcast.12), calls=%async_computation.4 | async-start | bytes 2097152 | tf_op jit(solution)/shard_map/all_to_all | solution.py:34
  123.1 2.9 %collective-permute-start.11 = (bf16[3,6,16,512]{3,2,1,0:T(8,128)(2,1)S(1)}, bf16[3,6,16,512]{3,2,1,0:T(8,128)(2,1)S(1)}, u32[]{:S(2)}, u32[]{:S(2)}) collective-permute-start(bf16[3,6,16,512]{3,2,1,0:T(8,128)(2,1)S(1)} %join_planes.1.refs_2_), channel_id=1, source_target_pairs={{0,3},{1,0},{2,1},{3,2},{4,7},{5,4},{6,5},{7,6},{8,11},{9,8},{10,9... | collective-permute-start | bytes 884744 | tf_op jit(solution)/shard_map/ppermute | solution.py:39
  126.0 3.3 %collective-permute-start.10 = (bf16[3,6,16,512]{3,2,1,0:T(8,128)(2,1)S(1)}, bf16[3,6,16,512]{3,2,1,0:T(8,128)(2,1)S(1)}, u32[]{:S(2)}, u32[]{:S(2)}) collective-permute-start(bf16[3,6,16,512]{3,2,1,0:T(8,128)(2,1)S(1)} %join_planes.1.refs_2_), channel_id=1, source_target_pairs={{0,2},{1,3},{2,0},{3,1},{4,6},{5,7},{6,4},{7,5},{8,10},{9,11},{10,... | collective-permute-start | bytes 884744 | tf_op jit(solution)/shard_map/ppermute | solution.py:39
  129.3 1.9 %collective-permute-start.9 = (bf16[3,6,16,512]{3,2,1,0:T(8,128)(2,1)S(1)}, bf16[3,6,16,512]{3,2,1,0:T(8,128)(2,1)S(1)}, u32[]{:S(2)}, u32[]{:S(2)}) collective-permute-start(bf16[3,6,16,512]{3,2,1,0:T(8,128)(2,1)S(1)} %join_planes.1.refs_2_), channel_id=1, source_target_pairs={{0,1},{1,2},{2,3},{3,0},{4,5},{5,6},{6,7},{7,4},{8,9},{9,10},{10,1... | collective-permute-start | bytes 884744 | tf_op jit(solution)/shard_map/ppermute | solution.py:39
  131.2 1.7 collective-permute-done.11.refs_5_
  132.9 3.6 %collective-permute-done.10.refs_4_ = bf16[3,6,16,512]{3,2,1,0:T(8,128)(2,1)S(1)} collective-permute-done((bf16[3,6,16,512]{3,2,1,0:T(8,128)(2,1)S(1)}, bf16[3,6,16,512]{3,2,1,0:T(8,128)(2,1)S(1)}, u32[]{:S(2)}, u32[]{:S(2)}) %collective-permute-start.10) | collective-permute-done | bytes 294944 | tf_op jit(solution)/shard_map/ppermute | solution.py:39
  136.5 8.2 %collective-permute-done.9.refs_3_ = bf16[3,6,16,512]{3,2,1,0:T(8,128)(2,1)S(1)} collective-permute-done((bf16[3,6,16,512]{3,2,1,0:T(8,128)(2,1)S(1)}, bf16[3,6,16,512]{3,2,1,0:T(8,128)(2,1)S(1)}, u32[]{:S(2)}, u32[]{:S(2)}) %collective-permute-start.9) | collective-permute-done | bytes 294944 | tf_op jit(solution)/shard_map/ppermute | solution.py:39
  144.7 5.1 %all-to-all-done.4.refs_1_ = bf16[64,16,512]{2,1,0:T(8,128)(2,1)S(1)} async-done(((bf16[64,16,512]{2,1,0:T(8,128)(2,1)}), bf16[64,16,512]{2,1,0:T(8,128)(2,1)S(1)}, u32[]{:S(2)}, u32[]{:S(2)}) %all-to-all-start.4) | async-done | bytes 1048608 | tf_op jit(solution)/shard_map/all_to_all | solution.py:34
  151.3 9.4 %all-to-all-start.5 = ((f32[32,2,4,512]{3,2,1,0:T(4,128)}), f32[32,2,4,512]{3,2,1,0:T(4,128)S(1)}, u32[]{:S(2)}, u32[]{:S(2)}) async-start(f32[32,2,4,512]{3,2,1,0:T(4,128)} %sum_rows.1), calls=%async_computation.5 | async-start | bytes 1048576 | tf_op jit(solution)/shard_map/all_to_all | solution.py:34
  160.8 3.7 %order.1.refs_3_ = f32[64,3,4,512]{3,2,1,0:T(4,128)S(1)} custom-call(s32[5]{0:T(128)S(1)} %stack.23.refs_0_.place, s32[64]{0:T(128)S(1)} %copy-done.14, bf16[3,6,16,512]{3,2,1,0:T(8,128)(2,1)S(1)} %join_planes.1.refs_2_, bf16[3,6,16,512]{3,2,1,0:T(8,128)(2,1)S(1)} %collective-permute-done.9.refs_3_, ...), custom_call_target="tpu_custom_call" | custom-call | flops 1 | bytes 1024 | tf_op jit(solution)/shard_map/order/pallas_call | solution.py:60
  164.4 12.6 %all-to-all-done.5.refs_2_ = f32[32,2,4,512]{3,2,1,0:T(4,128)S(1)} async-done(((f32[32,2,4,512]{3,2,1,0:T(4,128)}), f32[32,2,4,512]{3,2,1,0:T(4,128)S(1)}, u32[]{:S(2)}, u32[]{:S(2)}) %all-to-all-start.5) | async-done | bytes 524320 | tf_op jit(solution)/shard_map/all_to_all | solution.py:34
  177.0 3.9 %update.1 = (f32[4,4,512]{2,1,0:T(4,128)}, f32[4,4,512]{2,1,0:T(4,128)}, f32[4,4,512]{2,1,0:T(4,128)}, bf16[4,64,512]{2,1,0:T(8,128)(2,1)}) custom-call(s32[5]{0:T(128)S(1)} %stack.23.refs_0_.place, s32[64]{0:T(128)S(1)} %copy-done.15, f32[32,2,4,512]{3,2,1,0:T(4,128)S(1)} %all-to-all-done.5.refs_2_, f32[64,3,4,512]{3,2,1,0:T(4,128)S(1)} %order.1.refs_3_), custom_call_target="tpu_custom_call" | custom-call | flops 1 | bytes 1024 | tf_op jit(solution)/shard_map/update/pallas_call | solution.py:60
  (48 shorter events, 19.4 us)
Async XLA Ops:
  2.2 9.7 %all-to-all-start = ((bf16[4,128,128]{2,1,0:T(8,128)(2,1)}), bf16[4,128,128]{2,1,0:T(8,128)(2,1)S(1)}, u32[]{:S(2)}, u32[]{:S(2)}) async-start(bf16[4,128,128]{2,1,0:T(8,128)(2,1)} %pack_keys.1), calls=%async_computation | async-start | bytes 262144 | tf_op jit(solution)/shard_map/all_to_all | solution.py:34
  7.1 1.2 copy-start.6
  8.3 1.2 copy-start.7
  9.6 1.3 copy-start.3
  11.9 23.2 %all-to-all-start.2 = ((bf16[4,128,2048]{2,1,0:T(8,128)(2,1)}), bf16[4,128,2048]{2,1,0:T(8,128)(2,1)S(1)}, u32[]{:S(2)}, u32[]{:S(2)}) async-start(bf16[4,128,2048]{2,1,0:T(8,128)(2,1)} %copy-done.3), calls=%async_computation.2 | async-start | bytes 4194304 | tf_op jit(solution)/shard_map/all_to_all | solution.py:34
  15.5 11.1 %collective-permute-start.2 = (bf16[512,128]{1,0:T(8,128)(2,1)S(1)}, bf16[512,128]{1,0:T(8,128)(2,1)S(1)}, u32[]{:S(2)}, u32[]{:S(2)}) collective-permute-start(bf16[512,128]{1,0:T(8,128)(2,1)S(1)} %bitcast.13), channel_id=1, source_target_pairs={{0,12},{1,13},{2,14},{3,15},{16,28},{17,29},{18,30},{19,31},{32,44... | collective-permute-start | bytes 393224 | tf_op jit(solution)/shard_map/ppermute | solution.py:43
  23.1 3.6 %collective-permute-start.1 = (bf16[512,128]{1,0:T(8,128)(2,1)S(1)}, bf16[512,128]{1,0:T(8,128)(2,1)S(1)}, u32[]{:S(2)}, u32[]{:S(2)}) collective-permute-start(bf16[512,128]{1,0:T(8,128)(2,1)S(1)} %bitcast.14), channel_id=1, source_target_pairs={{0,8},{4,12},{1,9},{5,13},{2,10},{6,14},{3,11},{7,15},{16,24},{20,... | collective-permute-start | bytes 393224 | tf_op jit(solution)/shard_map/ppermute | solution.py:43
  24.4 5.5 %collective-permute-start = (bf16[512,128]{1,0:T(8,128)(2,1)S(1)}, bf16[512,128]{1,0:T(8,128)(2,1)S(1)}, u32[]{:S(2)}, u32[]{:S(2)}) collective-permute-start(bf16[512,128]{1,0:T(8,128)(2,1)S(1)} %bitcast.15), channel_id=1, source_target_pairs={{0,4},{4,8},{8,12},{1,5},{5,9},{9,13},{2,6},{6,10},{10,14},{3,7},{... | collective-permute-start | bytes 393224 | tf_op jit(solution)/shard_map/ppermute | solution.py:43
  29.9 1.6 copy-start.4
  31.6 1.4 copy-start
  35.0 1.3 copy-start.1
  36.4 46.6 %all-to-all-start.1 = ((bf16[8,128,1024]{2,1,0:T(8,128)(2,1)}), bf16[8,128,1024]{2,1,0:T(8,128)(2,1)S(1)}, u32[]{:S(2)}, u32[]{:S(2)}) async-start(bf16[8,128,1024]{2,1,0:T(8,128)(2,1)} %copy-done), calls=%async_computation.1 | async-start | bytes 4194304 | tf_op jit(solution)/shard_map/all_to_all | solution.py:34
  47.7 1.6 copy-start.2
  54.6 11.9 %collective-permute-start.3 = (bf16[512,128]{1,0:T(8,128)(2,1)S(1)}, bf16[512,128]{1,0:T(8,128)(2,1)S(1)}, u32[]{:S(2)}, u32[]{:S(2)}) collective-permute-start(bf16[512,128]{1,0:T(8,128)(2,1)S(1)} %get-tuple-element.11), channel_id=1, source_target_pairs={{4,0},{8,4},{12,8},{5,1},{9,5},{13,9},{6,2},{10,6},{14,10},{7,3},{... | collective-permute-start | bytes 393224 | tf_op jit(solution)/shard_map/ppermute | solution.py:47
  55.9 19.2 %collective-permute-start.4 = (bf16[512,128]{1,0:T(8,128)(2,1)S(1)}, bf16[512,128]{1,0:T(8,128)(2,1)S(1)}, u32[]{:S(2)}, u32[]{:S(2)}) collective-permute-start(bf16[512,128]{1,0:T(8,128)(2,1)S(1)} %get-tuple-element.12), channel_id=1, source_target_pairs={{8,0},{12,4},{9,1},{13,5},{10,2},{14,6},{11,3},{15,7},{24,16},{28,... | collective-permute-start | bytes 393224 | tf_op jit(solution)/shard_map/ppermute | solution.py:47
  57.2 25.8 %collective-permute-start.5 = (bf16[512,128]{1,0:T(8,128)(2,1)S(1)}, bf16[512,128]{1,0:T(8,128)(2,1)S(1)}, u32[]{:S(2)}, u32[]{:S(2)}) collective-permute-start(bf16[512,128]{1,0:T(8,128)(2,1)S(1)} %get-tuple-element.13), channel_id=1, source_target_pairs={{12,0},{13,1},{14,2},{15,3},{28,16},{29,17},{30,18},{31,19},{44,32... | collective-permute-start | bytes 393224 | tf_op jit(solution)/shard_map/ppermute | solution.py:47
  83.0 6.2 %copy-start.9 = (f32[4,6,512]{2,0,1:T(4,128)S(1)}, f32[4,6,512]{2,0,1:T(4,128)}, u32[]{:S(2)}) copy-start(f32[4,6,512]{2,0,1:T(4,128)} %param.15) | copy-start | bytes 147460
  83.0 6.2 %copy-start.10 = (f32[4,6,512]{2,0,1:T(4,128)S(1)}, f32[4,6,512]{2,0,1:T(4,128)}, u32[]{:S(2)}) copy-start(f32[4,6,512]{2,0,1:T(4,128)} %param.16) | copy-start | bytes 147460
  83.0 6.2 %copy-start.11 = (f32[4,6,512]{2,0,1:T(4,128)S(1)}, f32[4,6,512]{2,0,1:T(4,128)}, u32[]{:S(2)}) copy-start(f32[4,6,512]{2,0,1:T(4,128)} %param.17) | copy-start | bytes 147460
  84.1 20.1 %all-to-all-start.3 = ((bf16[8,512,128]{2,1,0:T(8,128)(2,1)}), bf16[8,512,128]{2,1,0:T(8,128)(2,1)S(1)}, u32[]{:S(2)}, u32[]{:S(2)}) async-start(bf16[8,512,128]{2,1,0:T(8,128)(2,1)} %sum_values.1.refs_3_), calls=%async_computation.3 | async-start | bytes 2097152 | tf_op jit(solution)/shard_map/all_to_all | solution.py:34
  89.3 6.6 %collective-permute-start.8 = (bf16[6,16,512]{2,1,0:T(8,128)(2,1)S(1)}, bf16[6,16,512]{2,1,0:T(8,128)(2,1)S(1)}, u32[]{:S(2)}, u32[]{:S(2)}) collective-permute-start(bf16[6,16,512]{2,1,0:T(8,128)(2,1)S(1)} %pack_states.1.refs_1_), channel_id=1, source_target_pairs={{0,12},{4,0},{8,4},{1,13},{5,1},{9,5},{2,14},{6,2},{10,6},{3,15},{... | collective-permute-start | bytes 294920 | tf_op jit(solution)/shard_map/ppermute | solution.py:51
  91.2 7.2 %collective-permute-start.7 = (bf16[6,16,512]{2,1,0:T(8,128)(2,1)S(1)}, bf16[6,16,512]{2,1,0:T(8,128)(2,1)S(1)}, u32[]{:S(2)}, u32[]{:S(2)}) collective-permute-start(bf16[6,16,512]{2,1,0:T(8,128)(2,1)S(1)} %pack_states.1.refs_1_), channel_id=1, source_target_pairs={{0,8},{4,12},{8,0},{1,9},{5,13},{9,1},{2,10},{6,14},{10,2},{3,11},... | collective-permute-start | bytes 294920 | tf_op jit(solution)/shard_map/ppermute | solution.py:51
  93.1 5.3 %collective-permute-start.6 = (bf16[6,16,512]{2,1,0:T(8,128)(2,1)S(1)}, bf16[6,16,512]{2,1,0:T(8,128)(2,1)S(1)}, u32[]{:S(2)}, u32[]{:S(2)}) collective-permute-start(bf16[6,16,512]{2,1,0:T(8,128)(2,1)S(1)} %pack_states.1.refs_1_), channel_id=1, source_target_pairs={{0,4},{4,8},{8,12},{1,5},{5,9},{9,13},{2,6},{6,10},{10,14},{3,7},{... | collective-permute-start | bytes 294920 | tf_op jit(solution)/shard_map/ppermute | solution.py:51
  107.8 1.0 copy-start.5
  108.8 41.0 %copy-start.13 = (f32[16,512]{1,0:T(8,128)S(1)}, f32[16,512]{1,0:T(8,128)}, u32[]{:S(2)}) copy-start(f32[16,512]{1,0:T(8,128)} %copy-done.12) | copy-start | bytes 98308
  108.8 41.0 %all-to-all-start.4 = ((bf16[64,16,512]{2,1,0:T(8,128)(2,1)}), bf16[64,16,512]{2,1,0:T(8,128)(2,1)S(1)}, u32[]{:S(2)}, u32[]{:S(2)}) async-start(bf16[64,16,512]{2,1,0:T(8,128)(2,1)} %bitcast.12), calls=%async_computation.4 | async-start | bytes 2097152 | tf_op jit(solution)/shard_map/all_to_all | solution.py:34
  122.5 38.3 %copy-start.14 = (s32[64]{0:T(128)S(1)}, s32[64]{0:T(128)}, u32[]{:S(2)}) copy-start(s32[64]{0:T(128)} %refs_1_.4) | copy-start | bytes 772
  123.1 9.8 %collective-permute-start.11 = (bf16[3,6,16,512]{3,2,1,0:T(8,128)(2,1)S(1)}, bf16[3,6,16,512]{3,2,1,0:T(8,128)(2,1)S(1)}, u32[]{:S(2)}, u32[]{:S(2)}) collective-permute-start(bf16[3,6,16,512]{3,2,1,0:T(8,128)(2,1)S(1)} %join_planes.1.refs_2_), channel_id=1, source_target_pairs={{0,3},{1,0},{2,1},{3,2},{4,7},{5,4},{6,5},{7,6},{8,11},{9,8},{10,9... | collective-permute-start | bytes 884744 | tf_op jit(solution)/shard_map/ppermute | solution.py:39
  126.0 10.5 %collective-permute-start.10 = (bf16[3,6,16,512]{3,2,1,0:T(8,128)(2,1)S(1)}, bf16[3,6,16,512]{3,2,1,0:T(8,128)(2,1)S(1)}, u32[]{:S(2)}, u32[]{:S(2)}) collective-permute-start(bf16[3,6,16,512]{3,2,1,0:T(8,128)(2,1)S(1)} %join_planes.1.refs_2_), channel_id=1, source_target_pairs={{0,2},{1,3},{2,0},{3,1},{4,6},{5,7},{6,4},{7,5},{8,10},{9,11},{10,... | collective-permute-start | bytes 884744 | tf_op jit(solution)/shard_map/ppermute | solution.py:39
  129.3 15.4 %collective-permute-start.9 = (bf16[3,6,16,512]{3,2,1,0:T(8,128)(2,1)S(1)}, bf16[3,6,16,512]{3,2,1,0:T(8,128)(2,1)S(1)}, u32[]{:S(2)}, u32[]{:S(2)}) collective-permute-start(bf16[3,6,16,512]{3,2,1,0:T(8,128)(2,1)S(1)} %join_planes.1.refs_2_), channel_id=1, source_target_pairs={{0,1},{1,2},{2,3},{3,0},{4,5},{5,6},{6,7},{7,4},{8,9},{9,10},{10,1... | collective-permute-start | bytes 884744 | tf_op jit(solution)/shard_map/ppermute | solution.py:39
  151.3 25.7 %copy-start.15 = (s32[64]{0:T(128)S(1)}, s32[64]{0:T(128)}, u32[]{:S(2)}) copy-start(s32[64]{0:T(128)} %refs_1_.5) | copy-start | bytes 772
  151.3 25.7 %all-to-all-start.5 = ((f32[32,2,4,512]{3,2,1,0:T(4,128)}), f32[32,2,4,512]{3,2,1,0:T(4,128)S(1)}, u32[]{:S(2)}, u32[]{:S(2)}) async-start(f32[32,2,4,512]{3,2,1,0:T(4,128)} %sum_rows.1), calls=%async_computation.5 | async-start | bytes 1048576 | tf_op jit(solution)/shard_map/all_to_all | solution.py:34
  (2 other events, 1.5 us)

commit v7 on v5

--- a/solution.py
+++ b/solution.py
@@ -21,10 +21,9 @@
 epsilon = 1e-08
 
 PLANE = 512
-CHUNK = 256
+CHUNK = 512
 ZH, Y, C, ZL, X = range(5)
 WHOLE = pl.BlockSpec(memory_space=pltpu.VMEM)
-IN_HBM = pl.BlockSpec(memory_space=pltpu.HBM)
 ELSEWHERE = pl.BlockSpec(memory_space=pl.ANY)
 SCALARS = pl.BlockSpec(memory_space=pltpu.SMEM)
 NT = (((1,), (1,)), ((), ()))
@@ -74,55 +73,21 @@
     return jax.ShapeDtypeStruct(dims, dtype)
 
 
-def copy_all(pairs, done):
-    copies = [pltpu.make_async_copy(a, b, done.at[i]) for i, (a, b) in enumerate(pairs)]
-    for copy in copies:
-        copy.start()
-    for copy in copies:
-        copy.wait()
-
-
-def pack_heads_kernel(q_ref, d_ref, out_ref, done):
+def pack_heads_kernel(q_ref, d_ref, out_ref):
     width = GRP * HD
-    pairs = []
     for g in range(KV):
-        at = pl.ds(g * width, width)
-        pairs.append((q_ref.at[:, at], out_ref.at[g, :, pl.ds(0, width)]))
-        pairs.append((d_ref.at[:, at], out_ref.at[g, :, pl.ds(width, width)]))
-    copy_all(pairs, done)
-
-
-def pack_inputs_kernel(in_ref, out_ref, done):
-    copy_all([(in_ref.at[:, pl.ds(k * 1024, 1024)], out_ref.at[k]) for k in range(8)], done)
-
-
-def packed_in_hbm(kernel, name, out, arrays, limit, behind=()):
-    given = len(arrays)
-
-    def body(*refs):
-        kernel(*refs[:given], *refs[given + len(behind) :])
-
-    return pl.pallas_call(
-        body,
-        out_shape=out,
-        in_specs=[IN_HBM] * given + [ELSEWHERE] * len(behind),
-        out_specs=IN_HBM,
-        scratch_shapes=[pltpu.SemaphoreType.DMA((8,))],
-        compiler_params=pltpu.CompilerParams(vmem_limit_bytes=limit * MIB),
-        cost_estimate=pl.CostEstimate(flops=1, bytes_accessed=1024, transcendentals=0),
-        name=name,
-    )(*arrays, *behind)
-
-
-def pack_keys_kernel(place, k_ref, *out):
-    for k, ref in enumerate(out):
-        ref[...] = k_ref[:, pl.ds(pl.multiple_of(((place[X] + k) % 4) * HD, HD), HD)]
-
-
-def join_keys_kernel(place, *refs):
-    *parts, out_ref = refs
-    for k, part in enumerate(parts):
-        out_ref[pl.ds(pl.multiple_of(((place[X] + 4 - k) % 4) * 128, 128), 128), :] = part[...]
+        out_ref[g, :, 0:width] = q_ref[:, g * width : (g + 1) * width]
+        out_ref[g, :, width:] = d_ref[:, g * width : (g + 1) * width]
+
+
+def pack_inputs_kernel(in_ref, out_ref):
+    for k in range(8):
+        out_ref[k] = in_ref[:, k * 1024 : (k + 1) * 1024]
+
+
+def pack_keys_kernel(k_ref, out_ref):
+    for g in range(KV):
+        out_ref[g] = k_ref[:, g * HD : (g + 1) * HD]
 
 
 def pack_states_kernel(p_ref, f_ref, s_ref, out_ref):
@@ -323,16 +288,15 @@
     columns = KV * HD
     place = jnp.stack([lax.axis_index(a) for a in ("zh", "y", "c", "zl", "x")]).astype(jnp.int32)
 
-    packed = packed_in_hbm(
-        pack_heads_kernel, "pack_heads", shape(KV, here, 2 * GRP * HD), [queries, grad_out], 60
+    packed = call(pack_keys_kernel, "pack_keys", shape(KV, here, HD), [], [keys], [])
+    plane_keys = swapped(packed, "x").reshape(PLANE, HD)
+    packed = call(
+        pack_heads_kernel, "pack_heads", shape(KV, here, 2 * GRP * HD), [], [queries, grad_out], []
     )
     heads = swapped(packed, "x")
-    own, *packed = call(pack_keys_kernel, "pack_keys", (shape(here, HD),) * 4, [place], [keys], [])
-    plane_keys = [own, *(shifted(packed[k - 1], "x", k) for k in (1, 2, 3))]
-    plane_keys = call(join_keys_kernel, "join_keys", shape(PLANE, HD), [place], plane_keys, [])
     all_keys = [plane_keys, *(sent_up(plane_keys, k) for k in (1, 2, 3))]
-    packed = packed_in_hbm(
-        pack_inputs_kernel, "pack_inputs", shape(8, here, 1024), [inputs], 1, all_keys[1:]
+    packed = call(
+        pack_inputs_kernel, "pack_inputs", shape(8, here, 1024), [], [inputs], [], all_keys[1:]
     )
     pieces = swapped(packed, ("c", "x"))
 
@@ -343,7 +307,7 @@
         [place],
         [heads, *all_keys],
         [pltpu.VMEM((4 * PLANE, PLANE), f32)] * 2 + [pltpu.VMEM((4 * PLANE, HD), f32)],
-        limit=16,
+        limit=24,
     )
     parts = [sent_down(parts[k - 1], k) for k in (1, 2, 3)]
     values = call(sum_values_kernel, "sum_values", shape(8, PLANE, HD), [], [own, *parts], [], [pieces])
@@ -356,7 +320,6 @@
     state = call(join_planes_kernel, "join_planes", shape(3, 6, 16, columns), [place], planes, [])
     state = [state, *(shifted(state, "x", k) for k in (1, 2, 3))]
     arrived = swapped(parts, ("zh", "y", "zl"))
-    rows = call(sum_rows_kernel, "sum_rows", shape(32, 2, 4, columns, dtype=f32), [place], [arrived, own], [], state[1:])
     state = call(
         order_kernel,
         "order",
@@ -365,6 +328,7 @@
         state,
         [pltpu.SMEM((16,), jnp.int32)],
     )
+    rows = call(sum_rows_kernel, "sum_rows", shape(32, 2, 4, columns, dtype=f32), [place], [arrived, own], [], [state])
     gradient = swapped(rows, ("c", "zl", "x"))
     block = shape(4, 4, columns, dtype=f32)
     return call(

time: 256 us -> 180 us (0.70)
  Pallas kernels: 84.5 us -> 19.1 us
  blocking collectives: 0 us -> 25.4 us
  waiting for transfers between devices: 77.4 us -> 53.6 us
  starting transfers between devices: 84.5 us -> 67.5 us
  local copies, waits for them, and re-layouts: 7.58 us -> 12.2 us
    pallas_call x2 -> x0, Pallas kernels: 64.9 us -> none  [packed_in_hbm(): pl.pallas_call(body, out_shape=out, in_specs=[IN_HBM] * given + [ELSEWHER...]
    all_to_all x0 -> x1, blocking collectives: none -> 25.4 us  [swapped(): return lax.all_to_all(x, axes, split_axis=0, concat_axis=0, tiled=True)]
    ppermute x6 -> x3, waiting for transfers between devices: 24.1 us -> 9.4 us  [shifted(): return lax.ppermute(x, axis, [(i, (i + k) % n) for i in range(n)])]
    all_to_all x5, waiting for transfers between devices: 23.5 us -> 13.2 us  [swapped(): return lax.all_to_all(x, axes, split_axis=0, concat_axis=0, tiled=True)]
    ppermute x6 -> x3, starting transfers between devices: 18.9 us -> 8.71 us  [shifted(): return lax.ppermute(x, axis, [(i, (i + k) % n) for i in range(n)])]
    ppermute x3, starting transfers between devices: 15.8 us -> 11.1 us  [sent_up(): return lax.ppermute(x, 'zl', [(i, i + k) for i in range(4 - k)])]
    unnamed x26 -> x32, local copies, waits for them, and re-layouts: 7.49 us -> 12.1 us
    ppermute x3, waiting for transfers between devices: 2.53 us -> 5.46 us  [old_planes(): return lax.ppermute(x, 'zl', [(i, (i + k) % 4) for i in range(3)])]
  transfers between devices with their start and end apart: 20 -> 17, of which waited for: 13 -> 14; matrix products, arithmetic and copies ran while one was open for 0% -> 0% of each run, Pallas kernels for 4% -> 5%
where the time goes in v7:
time: 180 us; the launch traced here: 179 us
  starting transfers between devices  67.5 us (38%)
  waiting for transfers between devices  53.6 us (30%)
  blocking collectives  25.4 us (14%)
  Pallas kernels  19.1 us (11%)
  local copies, waits for them, and re-layouts  12.2 us (7%)
    all_to_all x5, starting transfers between devices, swapped(): return lax.all_to_all(x, axes, split_axis=0, concat_axis=0, tiled=True)  38.5 us
    all_to_all x1, blocking collectives, swapped(): return lax.all_to_all(x, axes, split_axis=0, concat_axis=0, tiled=True)  25.4 us
    ppermute x3, waiting for transfers between devices, sent_down(): return lax.ppermute(x, 'zl', [(i, i - k) for i in range(k, 4)])  23.5 us
    pallas_call x10, Pallas kernels, call(): pl.pallas_call(body, out_shape=out, in_specs=[SCALARS] * len(scalars) + [...  16.1 us
    all_to_all x5, waiting for transfers between devices, swapped(): return lax.all_to_all(x, axes, split_axis=0, concat_axis=0, tiled=True)  13.2 us
    unnamed x32, local copies, waits for them, and re-layouts  12.1 us
    ppermute x3, starting transfers between devices, sent_up(): return lax.ppermute(x, 'zl', [(i, i + k) for i in range(4 - k)])  11.1 us
    ppermute x3, waiting for transfers between devices, shifted(): return lax.ppermute(x, axis, [(i, (i + k) % n) for i in range(n)])  9.4 us
  transfers between devices with their start and end apart: 17, of which 14 were waited for; matrix products, arithmetic and copies ran while one was open for 0% of the time, Pallas kernels for 5%

profile of v7, /device:TPU:1, one launch (start us, length us, event | category | flops | bytes accessed | tf_op | source)
XLA Modules:
  0.0 178.6 jit_solution(751965363387858708)
XLA Ops:
  2.2 4.8 %all-to-all-start = ((bf16[4,128,128]{2,1,0:T(8,128)(2,1)}), bf16[4,128,128]{2,1,0:T(8,128)(2,1)S(1)}, u32[]{:S(2)}, u32[]{:S(2)}) async-start(bf16[4,128,128]{2,1,0:T(8,128)(2,1)} %pack_keys.1), calls=%async_computation | async-start | bytes 262144 | tf_op jit(solution)/shard_map/all_to_all | solution.py:34
  11.9 3.6 %all-to-all-start.2 = ((bf16[4,128,2048]{2,1,0:T(8,128)(2,1)}), bf16[4,128,2048]{2,1,0:T(8,128)(2,1)S(1)}, u32[]{:S(2)}, u32[]{:S(2)}) async-start(bf16[4,128,2048]{2,1,0:T(8,128)(2,1)} %copy-done.3), calls=%async_computation.2 | async-start | bytes 4194304 | tf_op jit(solution)/shard_map/all_to_all | solution.py:34
  15.5 4.0 %collective-permute-start = (bf16[512,128]{1,0:T(8,128)(2,1)S(1)}, bf16[512,128]{1,0:T(8,128)(2,1)S(1)}, u32[]{:S(2)}, u32[]{:S(2)}) collective-permute-start(bf16[512,128]{1,0:T(8,128)(2,1)S(1)} %bitcast.13), channel_id=1, source_target_pairs={{0,4},{4,8},{8,12},{1,5},{5,9},{9,13},{2,6},{6,10},{10,14},{3,7},{... | collective-permute-start | bytes 393224 | tf_op jit(solution)/shard_map/ppermute | solution.py:43
  19.5 5.8 %collective-permute-start.1 = (bf16[512,128]{1,0:T(8,128)(2,1)S(1)}, bf16[512,128]{1,0:T(8,128)(2,1)S(1)}, u32[]{:S(2)}, u32[]{:S(2)}) collective-permute-start(bf16[512,128]{1,0:T(8,128)(2,1)S(1)} %bitcast.14), channel_id=1, source_target_pairs={{0,8},{4,12},{1,9},{5,13},{2,10},{6,14},{3,11},{7,15},{16,24},{20,... | collective-permute-start | bytes 393224 | tf_op jit(solution)/shard_map/ppermute | solution.py:43
  27.3 1.4 collective-permute-done.2.refs_3_.refs_5_
  28.7 1.6 copy-done.4
  30.4 1.4 copy-done
  31.8 3.3 %all-to-all-done.2.refs_1_ = bf16[4,128,2048]{2,1,0:T(8,128)(2,1)S(1)} async-done(((bf16[4,128,2048]{2,1,0:T(8,128)(2,1)}), bf16[4,128,2048]{2,1,0:T(8,128)(2,1)S(1)}, u32[]{:S(2)}, u32[]{:S(2)}) %all-to-all-start.2) | async-done | bytes 2097184 | tf_op jit(solution)/shard_map/all_to_all | solution.py:34
  36.4 11.2 %all-to-all-start.1 = ((bf16[8,128,1024]{2,1,0:T(8,128)(2,1)}), bf16[8,128,1024]{2,1,0:T(8,128)(2,1)S(1)}, u32[]{:S(2)}, u32[]{:S(2)}) async-start(bf16[8,128,1024]{2,1,0:T(8,128)(2,1)} %copy-done), calls=%async_computation.1 | async-start | bytes 4194304 | tf_op jit(solution)/shard_map/all_to_all | solution.py:34
  47.7 1.6 copy-done.2
  49.3 5.2 %values.1 = (f32[512,128]{1,0:T(8,128)S(1)}, bf16[512,128]{1,0:T(8,128)(2,1)S(1)}, bf16[512,128]{1,0:T(8,128)(2,1)S(1)}, bf16[512,128]{1,0:T(8,128)(2,1)S(1)}) custom-call(s32[5]{0:T(128)S(1)} %stack.23.refs_0_.place, bf16[4,128,2048]{2,1,0:T(8,128)(2,1)S(1)} %copy-done.2, bf16[512,128]{1,0:T(8,128)(2,1)S(1)} %bitcast.16, ...), custom_call_target="tpu_custom_call" | custom-call | flops 1 | bytes 1024 | tf_op jit(solution)/shard_map/values/pallas_call | solution.py:60
  58.4 6.9 %collective-permute-done.3.refs_1_ = bf16[512,128]{1,0:T(8,128)(2,1)S(1)} collective-permute-done((bf16[512,128]{1,0:T(8,128)(2,1)S(1)}, bf16[512,128]{1,0:T(8,128)(2,1)S(1)}, u32[]{:S(2)}, u32[]{:S(2)}) %collective-permute-start.3) | collective-permute-done | bytes 131104 | tf_op jit(solution)/shard_map/ppermute | solution.py:47
  65.3 8.5 %collective-permute-done.4.refs_2_ = bf16[512,128]{1,0:T(8,128)(2,1)S(1)} collective-permute-done((bf16[512,128]{1,0:T(8,128)(2,1)S(1)}, bf16[512,128]{1,0:T(8,128)(2,1)S(1)}, u32[]{:S(2)}, u32[]{:S(2)}) %collective-permute-start.4) | collective-permute-done | bytes 131104 | tf_op jit(solution)/shard_map/ppermute | solution.py:47
  73.9 8.0 %collective-permute-done.5.refs_3_ = bf16[512,128]{1,0:T(8,128)(2,1)S(1)} collective-permute-done((bf16[512,128]{1,0:T(8,128)(2,1)S(1)}, bf16[512,128]{1,0:T(8,128)(2,1)S(1)}, u32[]{:S(2)}, u32[]{:S(2)}) %collective-permute-start.5) | collective-permute-done | bytes 131104 | tf_op jit(solution)/shard_map/ppermute | solution.py:47
  82.9 5.1 %all-to-all-start.3 = ((bf16[8,512,128]{2,1,0:T(8,128)(2,1)}), bf16[8,512,128]{2,1,0:T(8,128)(2,1)S(1)}, u32[]{:S(2)}, u32[]{:S(2)}) async-start(bf16[8,512,128]{2,1,0:T(8,128)(2,1)} %sum_values.1.refs_3_), calls=%async_computation.3 | async-start | bytes 2097152 | tf_op jit(solution)/shard_map/all_to_all | solution.py:34
  89.4 2.1 %collective-permute-start.7 = (bf16[6,16,512]{2,1,0:T(8,128)(2,1)S(1)}, bf16[6,16,512]{2,1,0:T(8,128)(2,1)S(1)}, u32[]{:S(2)}, u32[]{:S(2)}) collective-permute-start(bf16[6,16,512]{2,1,0:T(8,128)(2,1)S(1)} %pack_states.1.refs_1_), channel_id=1, source_target_pairs={{0,8},{4,12},{8,0},{1,9},{5,13},{9,1},{2,10},{6,14},{10,2},{3,11},... | collective-permute-start | bytes 294920 | tf_op jit(solution)/shard_map/ppermute | solution.py:51
  91.5 1.9 %collective-permute-start.8 = (bf16[6,16,512]{2,1,0:T(8,128)(2,1)S(1)}, bf16[6,16,512]{2,1,0:T(8,128)(2,1)S(1)}, u32[]{:S(2)}, u32[]{:S(2)}) collective-permute-start(bf16[6,16,512]{2,1,0:T(8,128)(2,1)S(1)} %pack_states.1.refs_1_), channel_id=1, source_target_pairs={{0,12},{4,0},{8,4},{1,13},{5,1},{9,5},{2,14},{6,2},{10,6},{3,15},{... | collective-permute-start | bytes 294920 | tf_op jit(solution)/shard_map/ppermute | solution.py:51
  93.4 3.2 %collective-permute-done.7.refs_1_.refs_3_ = bf16[6,16,512]{2,1,0:T(8,128)(2,1)S(1)} collective-permute-done((bf16[6,16,512]{2,1,0:T(8,128)(2,1)S(1)}, bf16[6,16,512]{2,1,0:T(8,128)(2,1)S(1)}, u32[]{:S(2)}, u32[]{:S(2)}) %collective-permute-start.7) | collective-permute-done | bytes 98336 | tf_op jit(solution)/shard_map/ppermute | solution.py:51
  96.6 2.3 %collective-permute-done.8.refs_2_.refs_4_ = bf16[6,16,512]{2,1,0:T(8,128)(2,1)S(1)} collective-permute-done((bf16[6,16,512]{2,1,0:T(8,128)(2,1)S(1)}, bf16[6,16,512]{2,1,0:T(8,128)(2,1)S(1)}, u32[]{:S(2)}, u32[]{:S(2)}) %collective-permute-start.8) | collective-permute-done | bytes 98336 | tf_op jit(solution)/shard_map/ppermute | solution.py:51
  98.9 4.2 %all-to-all-done.3.v_ref = bf16[8,512,128]{2,1,0:T(8,128)(2,1)S(1)} async-done(((bf16[8,512,128]{2,1,0:T(8,128)(2,1)}), bf16[8,512,128]{2,1,0:T(8,128)(2,1)S(1)}, u32[]{:S(2)}, u32[]{:S(2)}) %all-to-all-start.3) | async-done | bytes 1048608 | tf_op jit(solution)/shard_map/all_to_all | solution.py:34
  103.0 3.0 %gradient.1 = (bf16[16,4,16,512]{3,2,1,0:T(8,128)(2,1)S(1)}, f32[16,512]{1,0:T(8,128)S(1)}) custom-call(s32[5]{0:T(128)S(1)} %stack.23.refs_0_.place, bf16[1024,1024]{1,0:T(8,128)(2,1)S(1)} %bitcast.11, bf16[8,512,128]{2,1,0:T(8,128)(2,1)S(1)} %all-to-all-done.3.v_ref, bf16[6,16,512]{2,1,0:T(8,128)(2,1)S(1)} %collective-permute-done.6.refs_0_.refs_2_, ...), custom_call_target="tpu_custom_call" | custom-call | flops 1 | bytes 1024 | tf_op jit(solution)/shard_map/gradient/pallas_call | solution.py:200
  107.6 13.7 %all-to-all-start.4 = ((bf16[64,16,512]{2,1,0:T(8,128)(2,1)}), bf16[64,16,512]{2,1,0:T(8,128)(2,1)S(1)}, u32[]{:S(2)}, u32[]{:S(2)}) async-start(bf16[64,16,512]{2,1,0:T(8,128)(2,1)} %bitcast.12), calls=%async_computation.4 | async-start | bytes 2097152 | tf_op jit(solution)/shard_map/all_to_all | solution.py:34
  122.0 2.5 %collective-permute-start.10 = (bf16[3,6,16,512]{3,2,1,0:T(8,128)(2,1)S(1)}, bf16[3,6,16,512]{3,2,1,0:T(8,128)(2,1)S(1)}, u32[]{:S(2)}, u32[]{:S(2)}) collective-permute-start(bf16[3,6,16,512]{3,2,1,0:T(8,128)(2,1)S(1)} %join_planes.1.refs_2_), channel_id=1, source_target_pairs={{0,2},{1,3},{2,0},{3,1},{4,6},{5,7},{6,4},{7,5},{8,10},{9,11},{10,... | collective-permute-start | bytes 884744 | tf_op jit(solution)/shard_map/ppermute | solution.py:39
  124.5 4.3 %collective-permute-start.11 = (bf16[3,6,16,512]{3,2,1,0:T(8,128)(2,1)S(1)}, bf16[3,6,16,512]{3,2,1,0:T(8,128)(2,1)S(1)}, u32[]{:S(2)}, u32[]{:S(2)}) collective-permute-start(bf16[3,6,16,512]{3,2,1,0:T(8,128)(2,1)S(1)} %join_planes.1.refs_2_), channel_id=1, source_target_pairs={{0,3},{1,0},{2,1},{3,2},{4,7},{5,4},{6,5},{7,6},{8,11},{9,8},{10,9... | collective-permute-start | bytes 884744 | tf_op jit(solution)/shard_map/ppermute | solution.py:39
  128.8 1.9 %collective-permute-start.9 = (bf16[3,6,16,512]{3,2,1,0:T(8,128)(2,1)S(1)}, bf16[3,6,16,512]{3,2,1,0:T(8,128)(2,1)S(1)}, u32[]{:S(2)}, u32[]{:S(2)}) collective-permute-start(bf16[3,6,16,512]{3,2,1,0:T(8,128)(2,1)S(1)} %join_planes.1.refs_2_), channel_id=1, source_target_pairs={{0,1},{1,2},{2,3},{3,0},{4,5},{5,6},{6,7},{7,4},{8,9},{9,10},{10,1... | collective-permute-start | bytes 884744 | tf_op jit(solution)/shard_map/ppermute | solution.py:39
  130.7 2.6 %collective-permute-done.10.refs_4_ = bf16[3,6,16,512]{3,2,1,0:T(8,128)(2,1)S(1)} collective-permute-done((bf16[3,6,16,512]{3,2,1,0:T(8,128)(2,1)S(1)}, bf16[3,6,16,512]{3,2,1,0:T(8,128)(2,1)S(1)}, u32[]{:S(2)}, u32[]{:S(2)}) %collective-permute-start.10) | collective-permute-done | bytes 294944 | tf_op jit(solution)/shard_map/ppermute | solution.py:39
  133.3 4.9 %collective-permute-done.11.refs_5_ = bf16[3,6,16,512]{3,2,1,0:T(8,128)(2,1)S(1)} collective-permute-done((bf16[3,6,16,512]{3,2,1,0:T(8,128)(2,1)S(1)}, bf16[3,6,16,512]{3,2,1,0:T(8,128)(2,1)S(1)}, u32[]{:S(2)}, u32[]{:S(2)}) %collective-permute-start.11) | collective-permute-done | bytes 294944 | tf_op jit(solution)/shard_map/ppermute | solution.py:39
  138.2 1.9 %collective-permute-done.9.refs_3_ = bf16[3,6,16,512]{3,2,1,0:T(8,128)(2,1)S(1)} collective-permute-done((bf16[3,6,16,512]{3,2,1,0:T(8,128)(2,1)S(1)}, bf16[3,6,16,512]{3,2,1,0:T(8,128)(2,1)S(1)}, u32[]{:S(2)}, u32[]{:S(2)}) %collective-permute-start.9) | collective-permute-done | bytes 294944 | tf_op jit(solution)/shard_map/ppermute | solution.py:39
  140.1 3.7 %order.1.refs_3_ = f32[64,3,4,512]{3,2,1,0:T(4,128)S(1)} custom-call(s32[5]{0:T(128)S(1)} %stack.23.refs_0_.place, s32[64]{0:T(128)S(1)} %copy-done.14, bf16[3,6,16,512]{3,2,1,0:T(8,128)(2,1)S(1)} %join_planes.1.refs_2_, bf16[3,6,16,512]{3,2,1,0:T(8,128)(2,1)S(1)} %collective-permute-done.9.refs_3_, ...), custom_call_target="tpu_custom_call" | custom-call | flops 1 | bytes 1024 | tf_op jit(solution)/shard_map/order/pallas_call | solution.py:60
  143.8 4.9 %all-to-all-done.4.refs_1_ = bf16[64,16,512]{2,1,0:T(8,128)(2,1)S(1)} async-done(((bf16[64,16,512]{2,1,0:T(8,128)(2,1)}), bf16[64,16,512]{2,1,0:T(8,128)(2,1)S(1)}, u32[]{:S(2)}, u32[]{:S(2)}) %all-to-all-start.4) | async-done | bytes 1048608 | tf_op jit(solution)/shard_map/all_to_all | solution.py:34
  149.4 25.4 %all_to_all.30.refs_2_ = f32[32,2,4,512]{3,2,1,0:T(4,128)S(1)} all-to-all(f32[32,2,4,512]{3,2,1,0:T(4,128)S(1)} %sum_rows.1), channel_id=1, replica_groups=mesh['zh'=2,'y'=8,'c'=2,'zl'=4,'x'=4] {'c','zl','x'}, dimensions={0} | all-to-all | bytes 1048576 | tf_op jit(solution)/shard_map/all_to_all | solution.py:34
  174.7 3.9 %update.1 = (f32[4,4,512]{2,1,0:T(4,128)}, f32[4,4,512]{2,1,0:T(4,128)}, f32[4,4,512]{2,1,0:T(4,128)}, bf16[4,64,512]{2,1,0:T(8,128)(2,1)}) custom-call(s32[5]{0:T(128)S(1)} %stack.23.refs_0_.place, s32[64]{0:T(128)S(1)} %copy-done.15, f32[32,2,4,512]{3,2,1,0:T(4,128)S(1)} %all_to_all.30.refs_2_, f32[64,3,4,512]{3,2,1,0:T(4,128)S(1)} %order.1.refs_3_), custom_call_target="tpu_custom_call" | custom-call | flops 1 | bytes 1024 | tf_op jit(solution)/shard_map/update/pallas_call | solution.py:60
  (47 shorter events, 19.1 us)
Async XLA Ops:
  0.6 0.9 copy-start.8
  2.2 9.7 %all-to-all-start = ((bf16[4,128,128]{2,1,0:T(8,128)(2,1)}), bf16[4,128,128]{2,1,0:T(8,128)(2,1)S(1)}, u32[]{:S(2)}, u32[]{:S(2)}) async-start(bf16[4,128,128]{2,1,0:T(8,128)(2,1)} %pack_keys.1), calls=%async_computation | async-start | bytes 262144 | tf_op jit(solution)/shard_map/all_to_all | solution.py:34
  7.1 1.2 copy-start.6
  8.3 1.2 copy-start.7
  9.6 1.3 copy-start.3
  11.9 23.2 %all-to-all-start.2 = ((bf16[4,128,2048]{2,1,0:T(8,128)(2,1)}), bf16[4,128,2048]{2,1,0:T(8,128)(2,1)S(1)}, u32[]{:S(2)}, u32[]{:S(2)}) async-start(bf16[4,128,2048]{2,1,0:T(8,128)(2,1)} %copy-done.3), calls=%async_computation.2 | async-start | bytes 4194304 | tf_op jit(solution)/shard_map/all_to_all | solution.py:34
  15.5 11.1 %collective-permute-start = (bf16[512,128]{1,0:T(8,128)(2,1)S(1)}, bf16[512,128]{1,0:T(8,128)(2,1)S(1)}, u32[]{:S(2)}, u32[]{:S(2)}) collective-permute-start(bf16[512,128]{1,0:T(8,128)(2,1)S(1)} %bitcast.13), channel_id=1, source_target_pairs={{0,4},{4,8},{8,12},{1,5},{5,9},{9,13},{2,6},{6,10},{10,14},{3,7},{... | collective-permute-start | bytes 393224 | tf_op jit(solution)/shard_map/ppermute | solution.py:43
  19.5 7.8 %collective-permute-start.1 = (bf16[512,128]{1,0:T(8,128)(2,1)S(1)}, bf16[512,128]{1,0:T(8,128)(2,1)S(1)}, u32[]{:S(2)}, u32[]{:S(2)}) collective-permute-start(bf16[512,128]{1,0:T(8,128)(2,1)S(1)} %bitcast.14), channel_id=1, source_target_pairs={{0,8},{4,12},{1,9},{5,13},{2,10},{6,14},{3,11},{7,15},{16,24},{20,... | collective-permute-start | bytes 393224 | tf_op jit(solution)/shard_map/ppermute | solution.py:43
  25.3 3.3 %collective-permute-start.2 = (bf16[512,128]{1,0:T(8,128)(2,1)S(1)}, bf16[512,128]{1,0:T(8,128)(2,1)S(1)}, u32[]{:S(2)}, u32[]{:S(2)}) collective-permute-start(bf16[512,128]{1,0:T(8,128)(2,1)S(1)} %bitcast.15), channel_id=1, source_target_pairs={{0,12},{1,13},{2,14},{3,15},{16,28},{17,29},{18,30},{19,31},{32,44... | collective-permute-start | bytes 393224 | tf_op jit(solution)/shard_map/ppermute | solution.py:43
  28.7 1.6 copy-start.4
  30.4 1.4 copy-start
  35.0 1.3 copy-start.1
  36.4 45.5 %all-to-all-start.1 = ((bf16[8,128,1024]{2,1,0:T(8,128)(2,1)}), bf16[8,128,1024]{2,1,0:T(8,128)(2,1)S(1)}, u32[]{:S(2)}, u32[]{:S(2)}) async-start(bf16[8,128,1024]{2,1,0:T(8,128)(2,1)} %copy-done), calls=%async_computation.1 | async-start | bytes 4194304 | tf_op jit(solution)/shard_map/all_to_all | solution.py:34
  47.7 1.6 copy-start.2
  54.5 10.8 %collective-permute-start.3 = (bf16[512,128]{1,0:T(8,128)(2,1)S(1)}, bf16[512,128]{1,0:T(8,128)(2,1)S(1)}, u32[]{:S(2)}, u32[]{:S(2)}) collective-permute-start(bf16[512,128]{1,0:T(8,128)(2,1)S(1)} %get-tuple-element.11), channel_id=1, source_target_pairs={{4,0},{8,4},{12,8},{5,1},{9,5},{13,9},{6,2},{10,6},{14,10},{7,3},{... | collective-permute-start | bytes 393224 | tf_op jit(solution)/shard_map/ppermute | solution.py:47
  55.8 18.1 %collective-permute-start.4 = (bf16[512,128]{1,0:T(8,128)(2,1)S(1)}, bf16[512,128]{1,0:T(8,128)(2,1)S(1)}, u32[]{:S(2)}, u32[]{:S(2)}) collective-permute-start(bf16[512,128]{1,0:T(8,128)(2,1)S(1)} %get-tuple-element.12), channel_id=1, source_target_pairs={{8,0},{12,4},{9,1},{13,5},{10,2},{14,6},{11,3},{15,7},{24,16},{28,... | collective-permute-start | bytes 393224 | tf_op jit(solution)/shard_map/ppermute | solution.py:47
  57.1 24.8 %collective-permute-start.5 = (bf16[512,128]{1,0:T(8,128)(2,1)S(1)}, bf16[512,128]{1,0:T(8,128)(2,1)S(1)}, u32[]{:S(2)}, u32[]{:S(2)}) collective-permute-start(bf16[512,128]{1,0:T(8,128)(2,1)S(1)} %get-tuple-element.13), channel_id=1, source_target_pairs={{12,0},{13,1},{14,2},{15,3},{28,16},{29,17},{30,18},{31,19},{44,32... | collective-permute-start | bytes 393224 | tf_op jit(solution)/shard_map/ppermute | solution.py:47
  81.9 6.2 %copy-start.9 = (f32[4,6,512]{2,0,1:T(4,128)S(1)}, f32[4,6,512]{2,0,1:T(4,128)}, u32[]{:S(2)}) copy-start(f32[4,6,512]{2,0,1:T(4,128)} %param.15) | copy-start | bytes 147460
  81.9 6.2 %copy-start.10 = (f32[4,6,512]{2,0,1:T(4,128)S(1)}, f32[4,6,512]{2,0,1:T(4,128)}, u32[]{:S(2)}) copy-start(f32[4,6,512]{2,0,1:T(4,128)} %param.16) | copy-start | bytes 147460
  81.9 6.2 %copy-start.11 = (f32[4,6,512]{2,0,1:T(4,128)S(1)}, f32[4,6,512]{2,0,1:T(4,128)}, u32[]{:S(2)}) copy-start(f32[4,6,512]{2,0,1:T(4,128)} %param.17) | copy-start | bytes 147460
  82.9 20.1 %all-to-all-start.3 = ((bf16[8,512,128]{2,1,0:T(8,128)(2,1)}), bf16[8,512,128]{2,1,0:T(8,128)(2,1)S(1)}, u32[]{:S(2)}, u32[]{:S(2)}) async-start(bf16[8,512,128]{2,1,0:T(8,128)(2,1)} %sum_values.1.refs_3_), calls=%async_computation.3 | async-start | bytes 2097152 | tf_op jit(solution)/shard_map/all_to_all | solution.py:34
  88.1 5.3 %collective-permute-start.6 = (bf16[6,16,512]{2,1,0:T(8,128)(2,1)S(1)}, bf16[6,16,512]{2,1,0:T(8,128)(2,1)S(1)}, u32[]{:S(2)}, u32[]{:S(2)}) collective-permute-start(bf16[6,16,512]{2,1,0:T(8,128)(2,1)S(1)} %pack_states.1.refs_1_), channel_id=1, source_target_pairs={{0,4},{4,8},{8,12},{1,5},{5,9},{9,13},{2,6},{6,10},{10,14},{3,7},{... | collective-permute-start | bytes 294920 | tf_op jit(solution)/shard_map/ppermute | solution.py:51
  89.4 7.2 %collective-permute-start.7 = (bf16[6,16,512]{2,1,0:T(8,128)(2,1)S(1)}, bf16[6,16,512]{2,1,0:T(8,128)(2,1)S(1)}, u32[]{:S(2)}, u32[]{:S(2)}) collective-permute-start(bf16[6,16,512]{2,1,0:T(8,128)(2,1)S(1)} %pack_states.1.refs_1_), channel_id=1, source_target_pairs={{0,8},{4,12},{8,0},{1,9},{5,13},{9,1},{2,10},{6,14},{10,2},{3,11},... | collective-permute-start | bytes 294920 | tf_op jit(solution)/shard_map/ppermute | solution.py:51
  91.5 7.4 %collective-permute-start.8 = (bf16[6,16,512]{2,1,0:T(8,128)(2,1)S(1)}, bf16[6,16,512]{2,1,0:T(8,128)(2,1)S(1)}, u32[]{:S(2)}, u32[]{:S(2)}) collective-permute-start(bf16[6,16,512]{2,1,0:T(8,128)(2,1)S(1)} %pack_states.1.refs_1_), channel_id=1, source_target_pairs={{0,12},{4,0},{8,4},{1,13},{5,1},{9,5},{2,14},{6,2},{10,6},{3,15},{... | collective-permute-start | bytes 294920 | tf_op jit(solution)/shard_map/ppermute | solution.py:51
  106.0 1.0 copy-start.5
  107.6 32.5 %copy-start.14 = (s32[64]{0:T(128)S(1)}, s32[64]{0:T(128)}, u32[]{:S(2)}) copy-start(s32[64]{0:T(128)} %refs_1_.4) | copy-start | bytes 772
  107.6 41.0 %all-to-all-start.4 = ((bf16[64,16,512]{2,1,0:T(8,128)(2,1)}), bf16[64,16,512]{2,1,0:T(8,128)(2,1)S(1)}, u32[]{:S(2)}, u32[]{:S(2)}) async-start(bf16[64,16,512]{2,1,0:T(8,128)(2,1)} %bitcast.12), calls=%async_computation.4 | async-start | bytes 2097152 | tf_op jit(solution)/shard_map/all_to_all | solution.py:34
  121.3 27.3 %copy-start.13 = (f32[16,512]{1,0:T(8,128)S(1)}, f32[16,512]{1,0:T(8,128)}, u32[]{:S(2)}) copy-start(f32[16,512]{1,0:T(8,128)} %copy-done.12) | copy-start | bytes 98308
  122.0 11.3 %collective-permute-start.10 = (bf16[3,6,16,512]{3,2,1,0:T(8,128)(2,1)S(1)}, bf16[3,6,16,512]{3,2,1,0:T(8,128)(2,1)S(1)}, u32[]{:S(2)}, u32[]{:S(2)}) collective-permute-start(bf16[3,6,16,512]{3,2,1,0:T(8,128)(2,1)S(1)} %join_planes.1.refs_2_), channel_id=1, source_target_pairs={{0,2},{1,3},{2,0},{3,1},{4,6},{5,7},{6,4},{7,5},{8,10},{9,11},{10,... | collective-permute-start | bytes 884744 | tf_op jit(solution)/shard_map/ppermute | solution.py:39
  124.5 13.7 %collective-permute-start.11 = (bf16[3,6,16,512]{3,2,1,0:T(8,128)(2,1)S(1)}, bf16[3,6,16,512]{3,2,1,0:T(8,128)(2,1)S(1)}, u32[]{:S(2)}, u32[]{:S(2)}) collective-permute-start(bf16[3,6,16,512]{3,2,1,0:T(8,128)(2,1)S(1)} %join_planes.1.refs_2_), channel_id=1, source_target_pairs={{0,3},{1,0},{2,1},{3,2},{4,7},{5,4},{6,5},{7,6},{8,11},{9,8},{10,9... | collective-permute-start | bytes 884744 | tf_op jit(solution)/shard_map/ppermute | solution.py:39
  128.8 11.3 %collective-permute-start.9 = (bf16[3,6,16,512]{3,2,1,0:T(8,128)(2,1)S(1)}, bf16[3,6,16,512]{3,2,1,0:T(8,128)(2,1)S(1)}, u32[]{:S(2)}, u32[]{:S(2)}) collective-permute-start(bf16[3,6,16,512]{3,2,1,0:T(8,128)(2,1)S(1)} %join_planes.1.refs_2_), channel_id=1, source_target_pairs={{0,1},{1,2},{2,3},{3,0},{4,5},{5,6},{6,7},{7,4},{8,9},{9,10},{10,1... | collective-permute-start | bytes 884744 | tf_op jit(solution)/shard_map/ppermute | solution.py:39
  148.6 26.1 %copy-start.15 = (s32[64]{0:T(128)S(1)}, s32[64]{0:T(128)}, u32[]{:S(2)}) copy-start(s32[64]{0:T(128)} %refs_1_.5) | copy-start | bytes 772
  (1 other events, 0.6 us)

commit v8 on v7

--- a/solution.py
+++ b/solution.py
@@ -51,8 +51,8 @@
     return lax.ppermute(x, "zl", [(i, (i + k) % 4) for i in range(3)])
 
 
-def call(kernel, name, out, scalars, arrays, scratch, behind=(), limit=8):
-    given = len(scalars) + len(arrays)
+def call(kernel, name, out, scalars, arrays, scratch, behind=(), limit=8, elsewhere=()):
+    given = len(scalars) + len(arrays) + len(elsewhere)
 
     def body(*refs):
         kernel(*refs[:given], *refs[given + len(behind) :])
@@ -60,13 +60,13 @@
     return pl.pallas_call(
         body,
         out_shape=out,
-        in_specs=[SCALARS] * len(scalars) + [WHOLE] * len(arrays) + [ELSEWHERE] * len(behind),
+        in_specs=[SCALARS] * len(scalars) + [WHOLE] * len(arrays) + [ELSEWHERE] * len((*elsewhere, *behind)),
         out_specs=jax.tree.map(lambda _: WHOLE, out),
         scratch_shapes=scratch,
         compiler_params=pltpu.CompilerParams(vmem_limit_bytes=limit * MIB),
         cost_estimate=pl.CostEstimate(flops=1, bytes_accessed=1024, transcendentals=0),
         name=name,
-    )(*scalars, *arrays, *behind)
+    )(*scalars, *arrays, *elsewhere, *behind)
 
 
 def shape(*dims, dtype=jnp.bfloat16):
@@ -108,10 +108,14 @@
             out_ref[plane] = ref[...]
 
 
-def value_kernel(place, heads, k0, k1, k2, k3, own_ref, down1, down2, down3, s_a, s_b, total):
+def value_kernel(place, k0, k1, k2, k3, given, own_ref, down1, down2, down3, s_a, s_b, total, heads, done):
     plane = place[ZL]
     factor = HD**-0.5 * LOG2E
     width = GRP * HD
+
+    copy = pltpu.make_async_copy(given, heads, done.at[0])
+    copy.start()
+    copy.wait()
 
     def columns(start):
         at = pl.ds(pl.multiple_of(start, HD), HD)
@@ -251,7 +255,7 @@
 
 
 def update_kernel(place, new_owner, g_ref, st_ref, p_out, f_out, s_out, w_out, w_rows, changed, count):
-    @pl.loop(0, 64, unroll=4)
+    @pl.loop(0, 64, unroll=8)
     def _(b):
         owner = (b // 32) * 16 + ((b // 2) % 4) * 4 + (b // 8) % 4
         gradient = g_ref[owner, b % 2]
@@ -305,9 +309,15 @@
         "values",
         (shape(PLANE, HD, dtype=f32), *(shape(PLANE, HD),) * 3),
         [place],
-        [heads, *all_keys],
-        [pltpu.VMEM((4 * PLANE, PLANE), f32)] * 2 + [pltpu.VMEM((4 * PLANE, HD), f32)],
-        limit=24,
+        all_keys,
+        [
+            *[pltpu.VMEM((4 * PLANE, PLANE), f32)] * 2,
+            pltpu.VMEM((4 * PLANE, HD), f32),
+            pltpu.VMEM((KV, here, 2 * GRP * HD), jnp.bfloat16),
+            pltpu.SemaphoreType.DMA((1,)),
+        ],
+        elsewhere=[heads],
+        limit=56,
     )
     parts = [sent_down(parts[k - 1], k) for k in (1, 2, 3)]
     values = call(sum_values_kernel, "sum_values", shape(8, PLANE, HD), [], [own, *parts], [], [pieces])

time: 180 us -> 182 us (1.011)
  Pallas kernels: 19.1 us -> 23.3 us
  local copies, waits for them, and re-layouts: 12.2 us -> 8.39 us
    unnamed x32 -> x38, local copies, waits for them, and re-layouts: 12.1 us -> 7.8 us
    pallas_call x10, Pallas kernels: 16.1 us -> 20.3 us  [call(): pl.pallas_call(body, out_shape=out, in_specs=[SCALARS] * len(scalars) + [...]
  transfers between devices with their start and end apart: 17 -> 17, of which waited for: 14 -> 14; matrix products, arithmetic and copies ran while one was open for 0% -> 0% of each run, Pallas kernels for 5% -> 8%
where the time goes in v8:
time: 182 us; the launch traced here: 181 us
  starting transfers between devices  68.5 us (38%)
  waiting for transfers between devices  54.7 us (30%)
  blocking collectives  25.4 us (14%)
  Pallas kernels  23.3 us (13%)
  local copies, waits for them, and re-layouts  8.39 us (5%)
    all_to_all x5, starting transfers between devices, swapped(): return lax.all_to_all(x, axes, split_axis=0, concat_axis=0, tiled=True)  39.5 us
    all_to_all x1, blocking collectives, swapped(): return lax.all_to_all(x, axes, split_axis=0, concat_axis=0, tiled=True)  25.4 us
    ppermute x3, waiting for transfers between devices, sent_down(): return lax.ppermute(x, 'zl', [(i, i - k) for i in range(k, 4)])  23.6 us
    pallas_call x10, Pallas kernels, call(): pl.pallas_call(body, out_shape=out, in_specs=[SCALARS] * len(scalars) + [...  20.3 us
    all_to_all x5, waiting for transfers between devices, swapped(): return lax.all_to_all(x, axes, split_axis=0, concat_axis=0, tiled=True)  14.4 us
    ppermute x3, starting transfers between devices, sent_up(): return lax.ppermute(x, 'zl', [(i, i + k) for i in range(4 - k)])  11.1 us
    ppermute x3, waiting for transfers between devices, shifted(): return lax.ppermute(x, axis, [(i, (i + k) % n) for i in range(n)])  9.39 us
    ppermute x3, starting transfers between devices, shifted(): return lax.ppermute(x, axis, [(i, (i + k) % n) for i in range(n)])  8.7 us
  transfers between devices with their start and end apart: 17, of which 14 were waited for; matrix products, arithmetic and copies ran while one was open for 0% of the time, Pallas kernels for 8%

profile of v8, /device:TPU:1, one launch (start us, length us, event | category | flops | bytes accessed | tf_op | source)
XLA Modules:
  0.0 181.2 jit_solution(5665357650267522547)
XLA Ops:
  2.2 4.8 %all-to-all-start = ((bf16[4,128,128]{2,1,0:T(8,128)(2,1)}), bf16[4,128,128]{2,1,0:T(8,128)(2,1)S(1)}, u32[]{:S(2)}, u32[]{:S(2)}) async-start(bf16[4,128,128]{2,1,0:T(8,128)(2,1)} %pack_keys.1), calls=%async_computation | async-start | bytes 262144 | tf_op jit(solution)/shard_map/all_to_all | solution.py:34
  9.5 1.5 pack_heads.1
  11.9 4.5 %all-to-all-start.2 = ((bf16[4,128,2048]{2,1,0:T(8,128)(2,1)}), bf16[4,128,2048]{2,1,0:T(8,128)(2,1)}, u32[]{:S(2)}, u32[]{:S(2)}) async-start(bf16[4,128,2048]{2,1,0:T(8,128)(2,1)} %pack_heads.1), calls=%async_computation.2 | async-start | bytes 4194304 | tf_op jit(solution)/shard_map/all_to_all | solution.py:34
  16.3 4.0 %collective-permute-start = (bf16[512,128]{1,0:T(8,128)(2,1)S(1)}, bf16[512,128]{1,0:T(8,128)(2,1)S(1)}, u32[]{:S(2)}, u32[]{:S(2)}) collective-permute-start(bf16[512,128]{1,0:T(8,128)(2,1)S(1)} %bitcast.16), channel_id=1, source_target_pairs={{0,4},{4,8},{8,12},{1,5},{5,9},{9,13},{2,6},{6,10},{10,14},{3,7},{... | collective-permute-start | bytes 393224 | tf_op jit(solution)/shard_map/ppermute | solution.py:43
  20.4 5.8 %collective-permute-start.1 = (bf16[512,128]{1,0:T(8,128)(2,1)S(1)}, bf16[512,128]{1,0:T(8,128)(2,1)S(1)}, u32[]{:S(2)}, u32[]{:S(2)}) collective-permute-start(bf16[512,128]{1,0:T(8,128)(2,1)S(1)} %bitcast.17), channel_id=1, source_target_pairs={{0,8},{4,12},{1,9},{5,13},{2,10},{6,14},{3,11},{7,15},{16,24},{20,... | collective-permute-start | bytes 393224 | tf_op jit(solution)/shard_map/ppermute | solution.py:43
  26.2 1.3 collective-permute-start.2
  28.1 1.4 collective-permute-done.2.refs_3_.refs_4_
  30.2 1.4 copy-done
  31.5 4.5 %all-to-all-done.2.refs_5_ = bf16[4,128,2048]{2,1,0:T(8,128)(2,1)} async-done(((bf16[4,128,2048]{2,1,0:T(8,128)(2,1)}), bf16[4,128,2048]{2,1,0:T(8,128)(2,1)}, u32[]{:S(2)}, u32[]{:S(2)}) %all-to-all-start.2) | async-done | bytes 2097184 | tf_op jit(solution)/shard_map/all_to_all | solution.py:34
  36.0 11.2 %all-to-all-start.1 = ((bf16[8,128,1024]{2,1,0:T(8,128)(2,1)}), bf16[8,128,1024]{2,1,0:T(8,128)(2,1)S(1)}, u32[]{:S(2)}, u32[]{:S(2)}) async-start(bf16[8,128,1024]{2,1,0:T(8,128)(2,1)} %copy-done), calls=%async_computation.1 | async-start | bytes 4194304 | tf_op jit(solution)/shard_map/all_to_all | solution.py:34
  47.8 8.2 %values.1 = (f32[512,128]{1,0:T(8,128)}, bf16[512,128]{1,0:T(8,128)(2,1)}, bf16[512,128]{1,0:T(8,128)(2,1)}, bf16[512,128]{1,0:T(8,128)(2,1)}) custom-call(s32[5]{0:T(128)} %stack.23.refs_0_.place, bf16[512,128]{1,0:T(8,128)(2,1)} %bitcast.19, bf16[512,128]{1,0:T(8,128)(2,1)} %copy-done.5, bf16[512,128]{1,0:T(8,128)(2,1)} %copy-done.6, ...), custom_call_target="tpu_custom_call" | custom-call | flops 1 | bytes 1024 | tf_op jit(solution)/shard_map/values/pallas_call | solution.py:60
  59.9 7.1 %collective-permute-done.3.refs_1_ = bf16[512,128]{1,0:T(8,128)(2,1)S(1)} collective-permute-done((bf16[512,128]{1,0:T(8,128)(2,1)}, bf16[512,128]{1,0:T(8,128)(2,1)S(1)}, u32[]{:S(2)}, u32[]{:S(2)}) %collective-permute-start.3) | collective-permute-done | bytes 131104 | tf_op jit(solution)/shard_map/ppermute | solution.py:47
  67.0 8.6 %collective-permute-done.4.refs_2_ = bf16[512,128]{1,0:T(8,128)(2,1)S(1)} collective-permute-done((bf16[512,128]{1,0:T(8,128)(2,1)}, bf16[512,128]{1,0:T(8,128)(2,1)S(1)}, u32[]{:S(2)}, u32[]{:S(2)}) %collective-permute-start.4) | collective-permute-done | bytes 131104 | tf_op jit(solution)/shard_map/ppermute | solution.py:47
  75.6 7.9 %collective-permute-done.5.refs_3_ = bf16[512,128]{1,0:T(8,128)(2,1)S(1)} collective-permute-done((bf16[512,128]{1,0:T(8,128)(2,1)}, bf16[512,128]{1,0:T(8,128)(2,1)S(1)}, u32[]{:S(2)}, u32[]{:S(2)}) %collective-permute-start.5) | collective-permute-done | bytes 131104 | tf_op jit(solution)/shard_map/ppermute | solution.py:47
  85.5 5.2 %all-to-all-start.3 = ((bf16[8,512,128]{2,1,0:T(8,128)(2,1)}), bf16[8,512,128]{2,1,0:T(8,128)(2,1)S(1)}, u32[]{:S(2)}, u32[]{:S(2)}) async-start(bf16[8,512,128]{2,1,0:T(8,128)(2,1)} %sum_values.1.refs_3_), calls=%async_computation.3 | async-start | bytes 2097152 | tf_op jit(solution)/shard_map/all_to_all | solution.py:34
  92.1 2.2 %collective-permute-start.7 = (bf16[6,16,512]{2,1,0:T(8,128)(2,1)S(1)}, bf16[6,16,512]{2,1,0:T(8,128)(2,1)S(1)}, u32[]{:S(2)}, u32[]{:S(2)}) collective-permute-start(bf16[6,16,512]{2,1,0:T(8,128)(2,1)S(1)} %pack_states.1.refs_1_), channel_id=1, source_target_pairs={{0,8},{4,12},{8,0},{1,9},{5,13},{9,1},{2,10},{6,14},{10,2},{3,11},... | collective-permute-start | bytes 294920 | tf_op jit(solution)/shard_map/ppermute | solution.py:51
  94.3 1.9 %collective-permute-start.8 = (bf16[6,16,512]{2,1,0:T(8,128)(2,1)S(1)}, bf16[6,16,512]{2,1,0:T(8,128)(2,1)S(1)}, u32[]{:S(2)}, u32[]{:S(2)}) collective-permute-start(bf16[6,16,512]{2,1,0:T(8,128)(2,1)S(1)} %pack_states.1.refs_1_), channel_id=1, source_target_pairs={{0,12},{4,0},{8,4},{1,13},{5,1},{9,5},{2,14},{6,2},{10,6},{3,15},{... | collective-permute-start | bytes 294920 | tf_op jit(solution)/shard_map/ppermute | solution.py:51
  96.2 3.1 %collective-permute-done.7.refs_1_.refs_3_ = bf16[6,16,512]{2,1,0:T(8,128)(2,1)S(1)} collective-permute-done((bf16[6,16,512]{2,1,0:T(8,128)(2,1)S(1)}, bf16[6,16,512]{2,1,0:T(8,128)(2,1)S(1)}, u32[]{:S(2)}, u32[]{:S(2)}) %collective-permute-start.7) | collective-permute-done | bytes 98336 | tf_op jit(solution)/shard_map/ppermute | solution.py:51
  99.3 2.2 %collective-permute-done.8.refs_2_.refs_4_ = bf16[6,16,512]{2,1,0:T(8,128)(2,1)S(1)} collective-permute-done((bf16[6,16,512]{2,1,0:T(8,128)(2,1)S(1)}, bf16[6,16,512]{2,1,0:T(8,128)(2,1)S(1)}, u32[]{:S(2)}, u32[]{:S(2)}) %collective-permute-start.8) | collective-permute-done | bytes 98336 | tf_op jit(solution)/shard_map/ppermute | solution.py:51
  101.5 4.2 %all-to-all-done.3.v_ref = bf16[8,512,128]{2,1,0:T(8,128)(2,1)S(1)} async-done(((bf16[8,512,128]{2,1,0:T(8,128)(2,1)}), bf16[8,512,128]{2,1,0:T(8,128)(2,1)S(1)}, u32[]{:S(2)}, u32[]{:S(2)}) %all-to-all-start.3) | async-done | bytes 1048608 | tf_op jit(solution)/shard_map/all_to_all | solution.py:34
  105.8 3.0 %gradient.1 = (bf16[16,4,16,512]{3,2,1,0:T(8,128)(2,1)S(1)}, f32[16,512]{1,0:T(8,128)S(1)}) custom-call(s32[5]{0:T(128)S(1)} %copy-done.15, bf16[1024,1024]{1,0:T(8,128)(2,1)S(1)} %bitcast.11, bf16[8,512,128]{2,1,0:T(8,128)(2,1)S(1)} %all-to-all-done.3.v_ref, bf16[6,16,512]{2,1,0:T(8,128)(2,1)S(1)} %collective-permute-done.6.refs_0_.refs_2_, ...), custom_call_target="tpu_custom_call" | custom-call | flops 1 | bytes 1024 | tf_op jit(solution)/shard_map/gradient/pallas_call | solution.py:204
  110.3 13.7 %all-to-all-start.4 = ((bf16[64,16,512]{2,1,0:T(8,128)(2,1)}), bf16[64,16,512]{2,1,0:T(8,128)(2,1)S(1)}, u32[]{:S(2)}, u32[]{:S(2)}) async-start(bf16[64,16,512]{2,1,0:T(8,128)(2,1)} %bitcast.12), calls=%async_computation.4 | async-start | bytes 2097152 | tf_op jit(solution)/shard_map/all_to_all | solution.py:34
  124.7 2.5 %collective-permute-start.10 = (bf16[3,6,16,512]{3,2,1,0:T(8,128)(2,1)S(1)}, bf16[3,6,16,512]{3,2,1,0:T(8,128)(2,1)S(1)}, u32[]{:S(2)}, u32[]{:S(2)}) collective-permute-start(bf16[3,6,16,512]{3,2,1,0:T(8,128)(2,1)S(1)} %join_planes.1.refs_2_), channel_id=1, source_target_pairs={{0,2},{1,3},{2,0},{3,1},{4,6},{5,7},{6,4},{7,5},{8,10},{9,11},{10,... | collective-permute-start | bytes 884744 | tf_op jit(solution)/shard_map/ppermute | solution.py:39
  127.2 4.3 %collective-permute-start.11 = (bf16[3,6,16,512]{3,2,1,0:T(8,128)(2,1)S(1)}, bf16[3,6,16,512]{3,2,1,0:T(8,128)(2,1)S(1)}, u32[]{:S(2)}, u32[]{:S(2)}) collective-permute-start(bf16[3,6,16,512]{3,2,1,0:T(8,128)(2,1)S(1)} %join_planes.1.refs_2_), channel_id=1, source_target_pairs={{0,3},{1,0},{2,1},{3,2},{4,7},{5,4},{6,5},{7,6},{8,11},{9,8},{10,9... | collective-permute-start | bytes 884744 | tf_op jit(solution)/shard_map/ppermute | solution.py:39
  131.5 1.9 %collective-permute-start.9 = (bf16[3,6,16,512]{3,2,1,0:T(8,128)(2,1)S(1)}, bf16[3,6,16,512]{3,2,1,0:T(8,128)(2,1)S(1)}, u32[]{:S(2)}, u32[]{:S(2)}) collective-permute-start(bf16[3,6,16,512]{3,2,1,0:T(8,128)(2,1)S(1)} %join_planes.1.refs_2_), channel_id=1, source_target_pairs={{0,1},{1,2},{2,3},{3,0},{4,5},{5,6},{6,7},{7,4},{8,9},{9,10},{10,1... | collective-permute-start | bytes 884744 | tf_op jit(solution)/shard_map/ppermute | solution.py:39
  133.4 2.6 %collective-permute-done.10.refs_4_ = bf16[3,6,16,512]{3,2,1,0:T(8,128)(2,1)S(1)} collective-permute-done((bf16[3,6,16,512]{3,2,1,0:T(8,128)(2,1)S(1)}, bf16[3,6,16,512]{3,2,1,0:T(8,128)(2,1)S(1)}, u32[]{:S(2)}, u32[]{:S(2)}) %collective-permute-start.10) | collective-permute-done | bytes 294944 | tf_op jit(solution)/shard_map/ppermute | solution.py:39
  136.0 4.9 %collective-permute-done.11.refs_5_ = bf16[3,6,16,512]{3,2,1,0:T(8,128)(2,1)S(1)} collective-permute-done((bf16[3,6,16,512]{3,2,1,0:T(8,128)(2,1)S(1)}, bf16[3,6,16,512]{3,2,1,0:T(8,128)(2,1)S(1)}, u32[]{:S(2)}, u32[]{:S(2)}) %collective-permute-start.11) | collective-permute-done | bytes 294944 | tf_op jit(solution)/shard_map/ppermute | solution.py:39
  140.9 1.9 %collective-permute-done.9.refs_3_ = bf16[3,6,16,512]{3,2,1,0:T(8,128)(2,1)S(1)} collective-permute-done((bf16[3,6,16,512]{3,2,1,0:T(8,128)(2,1)S(1)}, bf16[3,6,16,512]{3,2,1,0:T(8,128)(2,1)S(1)}, u32[]{:S(2)}, u32[]{:S(2)}) %collective-permute-start.9) | collective-permute-done | bytes 294944 | tf_op jit(solution)/shard_map/ppermute | solution.py:39
  142.8 3.7 %order.1.refs_3_ = f32[64,3,4,512]{3,2,1,0:T(4,128)S(1)} custom-call(s32[5]{0:T(128)S(1)} %copy-done.15, s32[64]{0:T(128)S(1)} %copy-done.16, bf16[3,6,16,512]{3,2,1,0:T(8,128)(2,1)S(1)} %join_planes.1.refs_2_, bf16[3,6,16,512]{3,2,1,0:T(8,128)(2,1)S(1)} %collective-permute-done.9.refs_3_, bf16[3,6,16,512]{3,2,1,0:T(8,128)(2,1)S(1)} %collective-permute-done.10.refs_4_, ...), custom_call_target="tpu_custom_call" | custom-call | flops 1 | bytes 1024 | tf_op jit(solution)/shard_map/order/pallas_call | solution.py:60
  146.5 4.9 %all-to-all-done.4.refs_1_ = bf16[64,16,512]{2,1,0:T(8,128)(2,1)S(1)} async-done(((bf16[64,16,512]{2,1,0:T(8,128)(2,1)}), bf16[64,16,512]{2,1,0:T(8,128)(2,1)S(1)}, u32[]{:S(2)}, u32[]{:S(2)}) %all-to-all-start.4) | async-done | bytes 1048608 | tf_op jit(solution)/shard_map/all_to_all | solution.py:34
  152.1 25.4 %all_to_all.30.refs_2_ = f32[32,2,4,512]{3,2,1,0:T(4,128)S(1)} all-to-all(f32[32,2,4,512]{3,2,1,0:T(4,128)S(1)} %sum_rows.1), channel_id=1, replica_groups=mesh['zh'=2,'y'=8,'c'=2,'zl'=4,'x'=4] {'c','zl','x'}, dimensions={0} | all-to-all | bytes 1048576 | tf_op jit(solution)/shard_map/all_to_all | solution.py:34
  177.5 3.8 %update.1 = (f32[4,4,512]{2,1,0:T(4,128)}, f32[4,4,512]{2,1,0:T(4,128)}, f32[4,4,512]{2,1,0:T(4,128)}, bf16[4,64,512]{2,1,0:T(8,128)(2,1)}) custom-call(s32[5]{0:T(128)S(1)} %copy-done.15, s32[64]{0:T(128)S(1)} %copy-done.17, f32[32,2,4,512]{3,2,1,0:T(4,128)S(1)} %all_to_all.30.refs_2_, f32[64,3,4,512]{3,2,1,0:T(4,128)S(1)} %order.1.refs_3_), custom_call_target="tpu_custom_call" | custom-call | flops 1 | bytes 1024 | tf_op jit(solution)/shard_map/update/pallas_call | solution.py:60
  (53 shorter events, 16.9 us)
Async XLA Ops:
  2.2 9.7 %all-to-all-start = ((bf16[4,128,128]{2,1,0:T(8,128)(2,1)}), bf16[4,128,128]{2,1,0:T(8,128)(2,1)S(1)}, u32[]{:S(2)}, u32[]{:S(2)}) async-start(bf16[4,128,128]{2,1,0:T(8,128)(2,1)} %pack_keys.1), calls=%async_computation | async-start | bytes 262144 | tf_op jit(solution)/shard_map/all_to_all | solution.py:34
  7.1 1.2 copy-start.3
  8.3 1.2 copy-start.4
  11.0 18.5 %copy-start.1 = (bf16[128,8192]{1,0:T(8,128)(2,1)S(1)}, bf16[128,8192]{1,0:T(8,128)(2,1)}, u32[]{:S(2)}) copy-start(bf16[128,8192]{1,0:T(8,128)(2,1)} %refs_0_.4) | copy-start | bytes 6291460
  11.9 14.3 %copy-start.18 = (bf16[4,128,128]{2,1,0:T(8,128)(2,1)}, bf16[4,128,128]{2,1,0:T(8,128)(2,1)S(1)}, u32[]{:S(2)}) copy-start(bf16[4,128,128]{2,1,0:T(8,128)(2,1)S(1)} %all-to-all-done) | copy-start | bytes 393220
  11.9 24.1 %all-to-all-start.2 = ((bf16[4,128,2048]{2,1,0:T(8,128)(2,1)}), bf16[4,128,2048]{2,1,0:T(8,128)(2,1)}, u32[]{:S(2)}, u32[]{:S(2)}) async-start(bf16[4,128,2048]{2,1,0:T(8,128)(2,1)} %pack_heads.1), calls=%async_computation.2 | async-start | bytes 4194304 | tf_op jit(solution)/shard_map/all_to_all | solution.py:34
  16.3 11.1 %collective-permute-start = (bf16[512,128]{1,0:T(8,128)(2,1)S(1)}, bf16[512,128]{1,0:T(8,128)(2,1)S(1)}, u32[]{:S(2)}, u32[]{:S(2)}) collective-permute-start(bf16[512,128]{1,0:T(8,128)(2,1)S(1)} %bitcast.16), channel_id=1, source_target_pairs={{0,4},{4,8},{8,12},{1,5},{5,9},{9,13},{2,6},{6,10},{10,14},{3,7},{... | collective-permute-start | bytes 393224 | tf_op jit(solution)/shard_map/ppermute | solution.py:43
  20.4 7.8 %collective-permute-start.1 = (bf16[512,128]{1,0:T(8,128)(2,1)S(1)}, bf16[512,128]{1,0:T(8,128)(2,1)S(1)}, u32[]{:S(2)}, u32[]{:S(2)}) collective-permute-start(bf16[512,128]{1,0:T(8,128)(2,1)S(1)} %bitcast.17), channel_id=1, source_target_pairs={{0,8},{4,12},{1,9},{5,13},{2,10},{6,14},{3,11},{7,15},{16,24},{20,... | collective-permute-start | bytes 393224 | tf_op jit(solution)/shard_map/ppermute | solution.py:43
  26.2 3.3 %collective-permute-start.2 = (bf16[512,128]{1,0:T(8,128)(2,1)S(1)}, bf16[512,128]{1,0:T(8,128)(2,1)S(1)}, u32[]{:S(2)}, u32[]{:S(2)}) collective-permute-start(bf16[512,128]{1,0:T(8,128)(2,1)S(1)} %bitcast.18), channel_id=1, source_target_pairs={{0,12},{1,13},{2,14},{3,15},{16,28},{17,29},{18,30},{19,31},{32,44... | collective-permute-start | bytes 393224 | tf_op jit(solution)/shard_map/ppermute | solution.py:43
  27.5 2.2 %copy-start.5 = (bf16[512,128]{1,0:T(8,128)(2,1)}, bf16[512,128]{1,0:T(8,128)(2,1)S(1)}, u32[]{:S(2)}) copy-start(bf16[512,128]{1,0:T(8,128)(2,1)S(1)} %collective-permute-done.refs_1_.refs_2_) | copy-start | bytes 393220
  28.1 1.6 copy-start.6
  30.2 1.4 copy-start
  36.0 47.5 %all-to-all-start.1 = ((bf16[8,128,1024]{2,1,0:T(8,128)(2,1)}), bf16[8,128,1024]{2,1,0:T(8,128)(2,1)S(1)}, u32[]{:S(2)}, u32[]{:S(2)}) async-start(bf16[8,128,1024]{2,1,0:T(8,128)(2,1)} %copy-done), calls=%async_computation.1 | async-start | bytes 4194304 | tf_op jit(solution)/shard_map/all_to_all | solution.py:34
  56.0 11.0 %collective-permute-start.3 = (bf16[512,128]{1,0:T(8,128)(2,1)}, bf16[512,128]{1,0:T(8,128)(2,1)S(1)}, u32[]{:S(2)}, u32[]{:S(2)}) collective-permute-start(bf16[512,128]{1,0:T(8,128)(2,1)} %get-tuple-element.11), channel_id=1, source_target_pairs={{4,0},{8,4},{12,8},{5,1},{9,5},{13,9},{6,2},{10,6},{14,10},{7,3},{... | collective-permute-start | bytes 393224 | tf_op jit(solution)/shard_map/ppermute | solution.py:47
  57.3 18.3 %collective-permute-start.4 = (bf16[512,128]{1,0:T(8,128)(2,1)}, bf16[512,128]{1,0:T(8,128)(2,1)S(1)}, u32[]{:S(2)}, u32[]{:S(2)}) collective-permute-start(bf16[512,128]{1,0:T(8,128)(2,1)} %get-tuple-element.12), channel_id=1, source_target_pairs={{8,0},{12,4},{9,1},{13,5},{10,2},{14,6},{11,3},{15,7},{24,16},{28,... | collective-permute-start | bytes 393224 | tf_op jit(solution)/shard_map/ppermute | solution.py:47
  58.6 24.9 %collective-permute-start.5 = (bf16[512,128]{1,0:T(8,128)(2,1)}, bf16[512,128]{1,0:T(8,128)(2,1)S(1)}, u32[]{:S(2)}, u32[]{:S(2)}) collective-permute-start(bf16[512,128]{1,0:T(8,128)(2,1)} %get-tuple-element.13), channel_id=1, source_target_pairs={{12,0},{13,1},{14,2},{15,3},{28,16},{29,17},{30,18},{31,19},{44,32... | collective-permute-start | bytes 393224 | tf_op jit(solution)/shard_map/ppermute | solution.py:47
  84.5 6.3 %copy-start.10 = (f32[4,6,512]{2,0,1:T(4,128)S(1)}, f32[4,6,512]{2,0,1:T(4,128)}, u32[]{:S(2)}) copy-start(f32[4,6,512]{2,0,1:T(4,128)} %param.15) | copy-start | bytes 147460
  84.5 6.3 %copy-start.11 = (f32[4,6,512]{2,0,1:T(4,128)S(1)}, f32[4,6,512]{2,0,1:T(4,128)}, u32[]{:S(2)}) copy-start(f32[4,6,512]{2,0,1:T(4,128)} %param.16) | copy-start | bytes 147460
  84.5 6.3 %copy-start.12 = (f32[4,6,512]{2,0,1:T(4,128)S(1)}, f32[4,6,512]{2,0,1:T(4,128)}, u32[]{:S(2)}) copy-start(f32[4,6,512]{2,0,1:T(4,128)} %param.17) | copy-start | bytes 147460
  85.5 20.2 %copy-start.15 = (s32[5]{0:T(128)S(1)}, s32[5]{0:T(128)}, u32[]{:S(2)}) copy-start(s32[5]{0:T(128)} %stack.23.refs_0_.place) | copy-start | bytes 64
  85.5 20.2 %all-to-all-start.3 = ((bf16[8,512,128]{2,1,0:T(8,128)(2,1)}), bf16[8,512,128]{2,1,0:T(8,128)(2,1)S(1)}, u32[]{:S(2)}, u32[]{:S(2)}) async-start(bf16[8,512,128]{2,1,0:T(8,128)(2,1)} %sum_values.1.refs_3_), calls=%async_computation.3 | async-start | bytes 2097152 | tf_op jit(solution)/shard_map/all_to_all | solution.py:34
  90.8 5.4 %collective-permute-start.6 = (bf16[6,16,512]{2,1,0:T(8,128)(2,1)S(1)}, bf16[6,16,512]{2,1,0:T(8,128)(2,1)S(1)}, u32[]{:S(2)}, u32[]{:S(2)}) collective-permute-start(bf16[6,16,512]{2,1,0:T(8,128)(2,1)S(1)} %pack_states.1.refs_1_), channel_id=1, source_target_pairs={{0,4},{4,8},{8,12},{1,5},{5,9},{9,13},{2,6},{6,10},{10,14},{3,7},{... | collective-permute-start | bytes 294920 | tf_op jit(solution)/shard_map/ppermute | solution.py:51
  92.1 7.2 %collective-permute-start.7 = (bf16[6,16,512]{2,1,0:T(8,128)(2,1)S(1)}, bf16[6,16,512]{2,1,0:T(8,128)(2,1)S(1)}, u32[]{:S(2)}, u32[]{:S(2)}) collective-permute-start(bf16[6,16,512]{2,1,0:T(8,128)(2,1)S(1)} %pack_states.1.refs_1_), channel_id=1, source_target_pairs={{0,8},{4,12},{8,0},{1,9},{5,13},{9,1},{2,10},{6,14},{10,2},{3,11},... | collective-permute-start | bytes 294920 | tf_op jit(solution)/shard_map/ppermute | solution.py:51
  94.3 7.2 %collective-permute-start.8 = (bf16[6,16,512]{2,1,0:T(8,128)(2,1)S(1)}, bf16[6,16,512]{2,1,0:T(8,128)(2,1)S(1)}, u32[]{:S(2)}, u32[]{:S(2)}) collective-permute-start(bf16[6,16,512]{2,1,0:T(8,128)(2,1)S(1)} %pack_states.1.refs_1_), channel_id=1, source_target_pairs={{0,12},{4,0},{8,4},{1,13},{5,1},{9,5},{2,14},{6,2},{10,6},{3,15},{... | collective-permute-start | bytes 294920 | tf_op jit(solution)/shard_map/ppermute | solution.py:51
  108.7 1.0 copy-start.2
  110.3 32.5 %copy-start.16 = (s32[64]{0:T(128)S(1)}, s32[64]{0:T(128)}, u32[]{:S(2)}) copy-start(s32[64]{0:T(128)} %refs_1_.4) | copy-start | bytes 772
  110.3 41.0 %all-to-all-start.4 = ((bf16[64,16,512]{2,1,0:T(8,128)(2,1)}), bf16[64,16,512]{2,1,0:T(8,128)(2,1)S(1)}, u32[]{:S(2)}, u32[]{:S(2)}) async-start(bf16[64,16,512]{2,1,0:T(8,128)(2,1)} %bitcast.12), calls=%async_computation.4 | async-start | bytes 2097152 | tf_op jit(solution)/shard_map/all_to_all | solution.py:34
  124.1 27.3 %copy-start.14 = (f32[16,512]{1,0:T(8,128)S(1)}, f32[16,512]{1,0:T(8,128)}, u32[]{:S(2)}) copy-start(f32[16,512]{1,0:T(8,128)} %copy-done.13) | copy-start | bytes 98308
  124.7 11.3 %collective-permute-start.10 = (bf16[3,6,16,512]{3,2,1,0:T(8,128)(2,1)S(1)}, bf16[3,6,16,512]{3,2,1,0:T(8,128)(2,1)S(1)}, u32[]{:S(2)}, u32[]{:S(2)}) collective-permute-start(bf16[3,6,16,512]{3,2,1,0:T(8,128)(2,1)S(1)} %join_planes.1.refs_2_), channel_id=1, source_target_pairs={{0,2},{1,3},{2,0},{3,1},{4,6},{5,7},{6,4},{7,5},{8,10},{9,11},{10,... | collective-permute-start | bytes 884744 | tf_op jit(solution)/shard_map/ppermute | solution.py:39
  127.2 13.7 %collective-permute-start.11 = (bf16[3,6,16,512]{3,2,1,0:T(8,128)(2,1)S(1)}, bf16[3,6,16,512]{3,2,1,0:T(8,128)(2,1)S(1)}, u32[]{:S(2)}, u32[]{:S(2)}) collective-permute-start(bf16[3,6,16,512]{3,2,1,0:T(8,128)(2,1)S(1)} %join_planes.1.refs_2_), channel_id=1, source_target_pairs={{0,3},{1,0},{2,1},{3,2},{4,7},{5,4},{6,5},{7,6},{8,11},{9,8},{10,9... | collective-permute-start | bytes 884744 | tf_op jit(solution)/shard_map/ppermute | solution.py:39
  131.5 11.3 %collective-permute-start.9 = (bf16[3,6,16,512]{3,2,1,0:T(8,128)(2,1)S(1)}, bf16[3,6,16,512]{3,2,1,0:T(8,128)(2,1)S(1)}, u32[]{:S(2)}, u32[]{:S(2)}) collective-permute-start(bf16[3,6,16,512]{3,2,1,0:T(8,128)(2,1)S(1)} %join_planes.1.refs_2_), channel_id=1, source_target_pairs={{0,1},{1,2},{2,3},{3,0},{4,5},{5,6},{6,7},{7,4},{8,9},{9,10},{10,1... | collective-permute-start | bytes 884744 | tf_op jit(solution)/shard_map/ppermute | solution.py:39
  151.3 26.1 %copy-start.17 = (s32[64]{0:T(128)S(1)}, s32[64]{0:T(128)}, u32[]{:S(2)}) copy-start(s32[64]{0:T(128)} %refs_1_.5) | copy-start | bytes 772
  (4 other events, 3.1 us)
